TPU v7x, 512 devices: a whole 4x8x8 slice. The times are simulated.
512 devices in a mesh: grp: 16 (over y_hi, z), seq: 32 (over x, y_lo, core).
Axes of the slice: x: 4, y: 8 (y_hi: 2, y_lo: 4; y = y_hi * 4 + y_lo), z: 8, core: 2. Of those that a mesh axis runs over, the one named last changes fastest.
Arguments:
- text_heads: bfloat16 [16, 512, 3, 2048], P('grp', 'seq'), may hold values from -6 to 6
- image_heads: bfloat16 [16, 2048, 3, 2048], P('grp', 'seq'), may hold values from -6 to 6
- text_cotangent: bfloat16 [16, 512, 2048], P('grp', 'seq'), may hold values from -3 to 3
- image_cotangent: bfloat16 [16, 2048, 2048], P('grp', 'seq'), may hold values from -3 to 3
- control_residual: bfloat16 [16, 32, 64, 2048], P(None, 'seq', 'grp'), may hold values from -1.5 to 1.5
- control_gain: float32 [2048], replicated, may hold values from 0.1 to 1.9
- text_lengths: int32 [16], P('grp'), may hold values from 64 to 512, as said below
Outputs:
- text_attention: bfloat16 [16, 512, 2048], P('grp', 'seq')
- image_output: bfloat16 [16, 2048, 2048], P('grp', 'seq')
- text_grads: bfloat16 [16, 512, 3, 2048], P('grp', 'seq')
- image_grads: bfloat16 [16, 2048, 3, 2048], P('grp', 'seq')
- control_grads: bfloat16 [16, 32, 64, 2048], P(None, 'seq', 'grp')
Inputs may be any that keep to these rules, and one draw needn't show every extreme that they name: `text_lengths`: padding text tokens follow the valid ones.
All inputs are finite; a program needn't handle non-finite values.
Results may differ from a plain program's by a relative error of at most 0.033.
Values may be sent and summed in bfloat16 or wider, within the bound.
No kernel may reach another device: no remote copies, remote signals or barrier semaphores. Data moves between devices by JAX's collectives and lax.ppermute only.
A program may use at most 64 MiB of HBM per device.

v0:
```python
from functools import partial
import math

import jax
import jax.numpy as jnp
from jax import lax
from jax.sharding import PartitionSpec as P

HEAD_DIM = 128


NEG_FLOOR = -1e30


def unit_halves(values, half_rows):
    row_total, head_count, head_size = values.shape
    reshaped = values.reshape(2, half_rows, head_count, head_size)
    return jnp.transpose(reshaped, (1, 2, 0, 3)).reshape(half_rows, 2 * head_count, head_size)


def units_to_rows(values, half_rows):
    head_count = values.shape[1] // 2
    head_size = values.shape[2]
    reshaped = values.reshape(half_rows, head_count, 2, head_size)
    return jnp.transpose(reshaped, (2, 0, 1, 3)).reshape(2 * half_rows, head_count * head_size)


def unit_attention(queries, upstream, keys_all, values_all, valid, block_rows, scale_factor):
    key_total = keys_all.shape[0]
    block_count = key_total // block_rows
    head_size = keys_all.shape[1]
    query_total = queries.shape[0]
    key_blocks = keys_all.reshape(block_count, block_rows, head_size)
    value_blocks = values_all.reshape(block_count, block_rows, head_size)
    valid_blocks = valid.reshape(block_count, block_rows)

    def scores_for(key_block, valid_block):
        scores = (
            jnp.einsum("qd,kd->qk", queries, key_block, preferred_element_type=jnp.float32)
            * scale_factor
        )
        return jnp.where(valid_block[None, :], scores, -jnp.inf)

    def stats_step(carry, inputs):
        running_max, running_sum = carry
        key_block, valid_block = inputs
        scores = scores_for(key_block, valid_block)
        new_max = jnp.maximum(running_max, jnp.max(scores, axis=1))
        new_sum = running_sum * jnp.exp(running_max - new_max) + jnp.sum(
            jnp.exp(scores - new_max[:, None]), axis=1
        )
        return ((new_max, new_sum), None)

    start_stats = (
        jnp.full((query_total,), NEG_FLOOR, jnp.float32),
        jnp.zeros((query_total,), jnp.float32),
    )
    (row_max, row_sum), unused = lax.scan(stats_step, start_stats, (key_blocks, valid_blocks))

    def probs_for(key_block, valid_block):
        return jnp.exp(scores_for(key_block, valid_block) - row_max[:, None]) / row_sum[:, None]

    def forward_step(running, inputs):
        key_block, value_block, valid_block = inputs
        weights = probs_for(key_block, valid_block).astype(jnp.bfloat16)
        return (running + jnp.dot(weights, value_block, preferred_element_type=jnp.float32), None)

    start_out = jnp.zeros((query_total, head_size), jnp.float32)
    summed, unused = lax.scan(forward_step, start_out, (key_blocks, value_blocks, valid_blocks))
    attention = summed.astype(jnp.bfloat16)
    delta = jnp.sum(upstream.astype(jnp.float32) * attention.astype(jnp.float32), axis=1)

    def backward_step(running, inputs):
        key_block, value_block, valid_block = inputs
        probs = probs_for(key_block, valid_block)
        weights = probs.astype(jnp.bfloat16)
        value_grad = jnp.einsum("qk,qd->kd", weights, upstream, preferred_element_type=jnp.float32)
        prob_grad = jnp.einsum(
            "qd,kd->qk", upstream, value_block, preferred_element_type=jnp.float32
        )
        score_grad = (probs * (prob_grad - delta[:, None])).astype(jnp.bfloat16)
        running = running + jnp.dot(score_grad, key_block, preferred_element_type=jnp.float32)
        key_grad = (
            jnp.einsum("qk,qd->kd", score_grad, queries, preferred_element_type=jnp.float32)
            * scale_factor
        )
        return (running, (key_grad, value_grad))

    query_sum, (key_grads, value_grads) = lax.scan(
        backward_step, start_out, (key_blocks, value_blocks, valid_blocks)
    )
    query_grad = (query_sum * scale_factor).astype(jnp.bfloat16)
    return (
        attention,
        query_grad,
        key_grads.reshape(key_total, head_size),
        value_grads.reshape(key_total, head_size),
    )


def body(
    text_heads,
    image_heads,
    text_cotangent,
    image_cotangent,
    control_residual,
    control_gain,
    text_lengths,
):
    seq_count = lax.axis_size("seq")
    text_rows = text_heads.shape[1]
    image_rows = image_heads.shape[1]
    width = text_heads.shape[3]
    head_size = HEAD_DIM
    head_count = width // head_size
    row_count = text_rows + image_rows
    half_rows = row_count // 2
    per_device = 2 * head_count // seq_count
    scale_factor = 1.0 / math.sqrt(head_size)
    joint = jnp.concatenate([text_heads[0], image_heads[0]], axis=0).reshape(
        row_count, 3, head_count, head_size
    )
    upstream = jnp.concatenate([text_cotangent[0], image_cotangent[0]], axis=0).reshape(
        row_count, head_count, head_size
    )
    query_units = unit_halves(joint[:, 0], half_rows)
    grad_units = unit_halves(upstream, half_rows)
    unit_parity = (lax.axis_index("seq") * per_device + jnp.arange(per_device, dtype=jnp.int32)) % 2
    key_total = seq_count * row_count
    key_ids = jnp.arange(key_total, dtype=jnp.int32)[:, None]
    outgoing = (control_gain[None, :] * image_cotangent[0].astype(jnp.float32)).astype(jnp.bfloat16)
    outgoing = outgoing.reshape(control_residual.shape)
    key_units = jnp.repeat(joint[:, 1], 2, axis=1)
    value_units = jnp.repeat(joint[:, 2], 2, axis=1)
    queries, grads_in, keys_all, values_all = (
        lax.all_to_all(query_units, "seq", split_axis=1, concat_axis=0, tiled=True),
        lax.all_to_all(grad_units, "seq", split_axis=1, concat_axis=0, tiled=True),
        lax.all_to_all(key_units, "seq", split_axis=1, concat_axis=0, tiled=True),
        lax.all_to_all(value_units, "seq", split_axis=1, concat_axis=0, tiled=True),
    )
    source_ids = key_ids // row_count
    local_ids = key_ids % row_count
    valid = (local_ids >= text_rows) | (source_ids * text_rows + local_ids < text_lengths[0])
    group_size = 1
    while group_size * row_count < 512 and group_size < seq_count:
        group_size = group_size * 2
    attend = jax.vmap(
        partial(unit_attention, block_rows=group_size * row_count, scale_factor=scale_factor),
        in_axes=(1, 1, 1, 1, 1),
        out_axes=1,
    )
    attention, query_grad, key_grad, value_grad = attend(
        queries, grads_in, keys_all, values_all, valid
    )
    attention_rows = units_to_rows(
        lax.all_to_all(attention, "seq", split_axis=0, concat_axis=1, tiled=True), half_rows
    )
    arrived = lax.all_to_all(control_residual, "grp", split_axis=0, concat_axis=0, tiled=True)
    residual = arrived.reshape(image_rows, width).astype(jnp.float32)
    image_output = (
        attention_rows[text_rows:].astype(jnp.float32) + control_gain[None, :] * residual
    ).astype(jnp.bfloat16)
    query_rows = units_to_rows(
        lax.all_to_all(query_grad, "seq", split_axis=0, concat_axis=1, tiled=True), half_rows
    )
    key_back, value_back = (
        lax.all_to_all(key_grad, "seq", split_axis=0, concat_axis=1, tiled=True),
        lax.all_to_all(value_grad, "seq", split_axis=0, concat_axis=1, tiled=True),
    )
    key_rows = (
        jnp.sum(key_back.reshape(row_count, head_count, 2, head_size), axis=2)
        .astype(jnp.bfloat16)
        .reshape(row_count, width)
    )
    value_rows = (
        jnp.sum(value_back.reshape(row_count, head_count, 2, head_size), axis=2)
        .astype(jnp.bfloat16)
        .reshape(row_count, width)
    )
    control_grads = lax.all_to_all(outgoing, "grp", split_axis=0, concat_axis=0, tiled=True)
    grads_all = jnp.stack([query_rows, key_rows, value_rows], axis=1)
    text_attention = attention_rows[:text_rows][None]
    return (
        text_attention,
        image_output[None],
        grads_all[:text_rows][None],
        grads_all[text_rows:][None],
        control_grads,
    )


def solution(mesh):
    in_specs = (
        P("grp", "seq", None, None),
        P("grp", "seq", None, None),
        P("grp", "seq", None),
        P("grp", "seq", None),
        P(None, "seq", "grp", None),
        P(),
        P("grp"),
    )
    out_specs = (
        P("grp", "seq", None),
        P("grp", "seq", None),
        P("grp", "seq", None, None),
        P("grp", "seq", None, None),
        P(None, "seq", "grp", None),
    )
    return jax.shard_map(body, mesh=mesh, in_specs=in_specs, out_specs=out_specs, check_vma=False)
```

profile of v0, /device:TPU:1, one launch (start us, length us, event | category | flops | bytes accessed | tf_op | source)
XLA Modules:
  0.0 266.3 jit_solution(17582707160712290556)
XLA Ops:
  0.7 16.4 %all-to-all-start.4 = ((bf16[16,1,4,2048]{3,2,1,0:T(4,128)(2,1)}), bf16[16,1,4,2048]{3,2,1,0:T(4,128)(2,1)S(1)}, u32[]{:S(2)}, u32[]{:S(2)}) async-start(bf16[16,1,4,2048]{3,2,1,0:T(4,128)(2,1)} %param.17), calls=%async_computation.4 | async-start | bytes 524288 | tf_op jit(solution)/shard_map/all_to_all | solution.py:158
  17.0 1.0 maximum_bitcast_fusion
  18.9 10.0 %all-to-all-done.4 = bf16[16,1,4,2048]{3,2,1,0:T(4,128)(2,1)S(1)} async-done(((bf16[16,1,4,2048]{3,2,1,0:T(4,128)(2,1)}), bf16[16,1,4,2048]{3,2,1,0:T(4,128)(2,1)S(1)}, u32[]{:S(2)}, u32[]{:S(2)}) %all-to-all-start.4) | async-done | bytes 262176 | tf_op jit(solution)/shard_map/all_to_all | solution.py:158
  28.9 9.0 %all-to-all-start.5 = ((bf16[40,32,128]{2,0,1:T(8,128)(2,1)}), bf16[40,32,128]{2,0,1:T(8,128)(2,1)S(1)}, u32[]{:S(2)}, u32[]{:S(2)}) async-start(bf16[40,32,128]{2,0,1:T(8,128)(2,1)} %bitcast.32), calls=%async_computation.5 | async-start | bytes 655360 | tf_op jit(solution)/shard_map/all_to_all | solution.py:137
  39.3 11.2 %all-to-all-done.5 = bf16[40,32,128]{2,0,1:T(8,128)(2,1)S(1)} async-done(((bf16[40,32,128]{2,0,1:T(8,128)(2,1)}), bf16[40,32,128]{2,0,1:T(8,128)(2,1)S(1)}, u32[]{:S(2)}, u32[]{:S(2)}) %all-to-all-start.5) | async-done | bytes 327712 | tf_op jit(solution)/shard_map/all_to_all | solution.py:137
  50.5 3.7 %all-to-all-start.1 = ((bf16[40,32,128]{2,0,1:T(8,128)(2,1)}), bf16[40,32,128]{2,0,1:T(8,128)(2,1)S(1)}, u32[]{:S(2)}, u32[]{:S(2)}) async-start(bf16[40,32,128]{2,0,1:T(8,128)(2,1)} %bitcast.8), calls=%async_computation.1 | async-start | bytes 655360 | tf_op jit(solution)/shard_map/all_to_all | solution.py:136
  54.3 12.6 %all-to-all-done.1 = bf16[40,32,128]{2,0,1:T(8,128)(2,1)S(1)} async-done(((bf16[40,32,128]{2,0,1:T(8,128)(2,1)}), bf16[40,32,128]{2,0,1:T(8,128)(2,1)S(1)}, u32[]{:S(2)}, u32[]{:S(2)}) %all-to-all-start.1) | async-done | bytes 327712 | tf_op jit(solution)/shard_map/all_to_all | solution.py:136
  66.9 0.9 broadcast_in_dim.77
  67.8 3.7 %all-to-all-start = ((bf16[80,32,128]{2,0,1:T(8,128)(2,1)}), bf16[80,32,128]{2,0,1:T(8,128)(2,1)S(1)}, u32[]{:S(2)}, u32[]{:S(2)}) async-start(bf16[80,32,128]{2,0,1:T(8,128)(2,1)} %bitcast.2), calls=%async_computation | async-start | bytes 1310720 | tf_op jit(solution)/shard_map/all_to_all | solution.py:138
  73.4 17.8 %all-to-all-done = bf16[80,32,128]{2,0,1:T(8,128)(2,1)S(1)} async-done(((bf16[80,32,128]{2,0,1:T(8,128)(2,1)}), bf16[80,32,128]{2,0,1:T(8,128)(2,1)S(1)}, u32[]{:S(2)}, u32[]{:S(2)}) %all-to-all-start) | async-done | bytes 655392 | tf_op jit(solution)/shard_map/all_to_all | solution.py:138
  91.2 0.9 broadcast_in_dim.80
  92.1 3.7 %all-to-all-start.2 = ((bf16[80,32,128]{2,0,1:T(8,128)(2,1)}), bf16[80,32,128]{2,0,1:T(8,128)(2,1)S(1)}, u32[]{:S(2)}, u32[]{:S(2)}) async-start(bf16[80,32,128]{2,0,1:T(8,128)(2,1)} %bitcast.17), calls=%async_computation.2 | async-start | bytes 1310720 | tf_op jit(solution)/shard_map/all_to_all | solution.py:139
  95.8 4.9 %while.39 = (s32[]{:T(128)}, f32[1,1280]{1,0:T(1,128)S(1)}, f32[1,1280]{1,0:T(1,128)S(1)}, pred[4,1,640]{2,1,0:T(4,128)(4,1)S(1)}, bf16[4,1,640,128]{3,2,1,0:T(8...) while((s32[]{:T(128)}, f32[1,1280]{1,0:T(1,128)S(1)}, ...), condition=%wide.region_3.4_spmd.clone, body=%wide.region_0.3_spmd.clone.sunk | while | flops 213817600 | bytes 7119216 | solution.py:58
  100.7 14.8 %all-to-all-done.2 = bf16[80,32,128]{2,0,1:T(8,128)(2,1)S(1)} async-done(((bf16[80,32,128]{2,0,1:T(8,128)(2,1)}), bf16[80,32,128]{2,0,1:T(8,128)(2,1)S(1)}, u32[]{:S(2)}, u32[]{:S(2)}) %all-to-all-start.2) | async-done | bytes 655392 | tf_op jit(solution)/shard_map/all_to_all | solution.py:139
  115.5 4.2 %all-to-all-start.9 = ((bf16[16,1,4,2048]{3,2,1,0:T(4,128)(2,1)}), bf16[16,1,4,2048]{3,2,1,0:T(4,128)(2,1)}, u32[]{:S(2)}, u32[]{:S(2)}) async-start(bf16[16,1,4,2048]{3,2,1,0:T(4,128)(2,1)} %multiply_convert_fusion.1), calls=%async_computation.9 | async-start | bytes 524288 | tf_op jit(solution)/shard_map/all_to_all | solution.py:180
  119.7 12.7 %while.40 = (s32[]{:T(128)}, f32[1,1280,128]{2,1,0:T(8,128)}, pred[4,1,640]{2,1,0:T(4,128)(4,1)S(1)}, bf16[4,1,640,128]{3,2,1,0:T(8,128)(2,1)S(1)}, bf16[1,1280,...) while((s32[]{:T(128)}, f32[1,1280,128]{2,1,0:T(8,128)}, ...), condition=%wide.region_5.6_spmd.clone, body=%wide.region_4.5_spmd.clone.sunk | while | flops 423854080 | bytes 2006922 | solution.py:69
  119.8 2.3 fusion.87
  122.2 3.4 %fusion.87 = f32[1,1280,128]{2,1,0:T(8,128)} fusion(f32[1280]{0:T(1024)S(1)} %reduce.34, f32[1280]{0:T(1024)S(1)} %reduce.35, pred[640]{0:T(1024)(128)(4,1)S(1)} %dynamic-slice_reduce_fusion.7, f32[1,1280,128]{2,1,0:T(8,128)} %get-tuple-element.501, bf16[1,1280,128]{2,1,0:T(8,128)(2,1)S(1)} %get-tuple-element.515, pred[]{:T(512)S(6)} %compare.10, ...), kind=kOutput, calls=%fused_computation.19.clone.1 | convolution fusion | flops 423854080 | bytes 1985024 | tf_op jit(solution)/shard_map/vmap()/while/body/eval_jaxpr/dot_general | solution.py:66
  125.6 3.4 %fusion.87 = f32[1,1280,128]{2,1,0:T(8,128)} fusion(f32[1280]{0:T(1024)S(1)} %reduce.34, f32[1280]{0:T(1024)S(1)} %reduce.35, pred[640]{0:T(1024)(128)(4,1)S(1)} %dynamic-slice_reduce_fusion.7, f32[1,1280,128]{2,1,0:T(8,128)} %get-tuple-element.501, bf16[1,1280,128]{2,1,0:T(8,128)(2,1)S(1)} %get-tuple-element.515, pred[]{:T(512)S(6)} %compare.10, ...), kind=kOutput, calls=%fused_computation.19.clone.1 | convolution fusion | flops 423854080 | bytes 1985024 | tf_op jit(solution)/shard_map/vmap()/while/body/eval_jaxpr/dot_general | solution.py:66
  129.1 3.4 %fusion.87 = f32[1,1280,128]{2,1,0:T(8,128)} fusion(f32[1280]{0:T(1024)S(1)} %reduce.34, f32[1280]{0:T(1024)S(1)} %reduce.35, pred[640]{0:T(1024)(128)(4,1)S(1)} %dynamic-slice_reduce_fusion.7, f32[1,1280,128]{2,1,0:T(8,128)} %get-tuple-element.501, bf16[1,1280,128]{2,1,0:T(8,128)(2,1)S(1)} %get-tuple-element.515, pred[]{:T(512)S(6)} %compare.10, ...), kind=kOutput, calls=%fused_computation.19.clone.1 | convolution fusion | flops 423854080 | bytes 1985024 | tf_op jit(solution)/shard_map/vmap()/while/body/eval_jaxpr/dot_general | solution.py:66
  133.0 1.3 multiply_reduce_fusion
  135.5 0.9 reduce.20
  137.2 3.7 %all-to-all-start.3 = ((bf16[32,2,2560]{2,1,0:T(2,128)(2,1)}), bf16[32,2,2560]{2,1,0:T(2,128)(2,1)S(1)}, u32[]{:S(2)}, u32[]{:S(2)}) async-start(bf16[32,2,2560]{2,1,0:T(2,128)(2,1)} %reshape.332), calls=%async_computation.3 | async-start | bytes 655360 | tf_op jit(solution)/shard_map/all_to_all | solution.py:156
  140.9 25.8 %while.41 = (s32[]{:T(128)}, f32[1,1280,128]{2,1,0:T(8,128)S(1)}, f32[4,1,640,128]{3,2,1,0:T(8,128)}, f32[4,1,640,128]{3,2,1,0:T(8,128)}, pred[4,1,640]{2,1,0:T(...) while((s32[]{:T(128)}, f32[1,1280,128]{2,1,0:T(8,128)S(1)}, ...), condition=%wide.region_8.9_spmd.clone, body=%wide.region_7.8_spmd.clone.sunk | while | flops 1055539200 | bytes 18571716 | solution.py:89
  142.4 0.9 fusion.98
  143.3 1.4 fusion.102
  146.1 1.3 fusion.101
  148.8 0.9 fusion.98
  149.7 1.3 fusion.102
  152.5 1.3 fusion.101
  155.3 0.9 fusion.98
  156.2 1.3 fusion.102
  158.9 1.3 fusion.101
  161.7 0.9 fusion.98
  162.6 1.3 fusion.102
  165.4 1.3 fusion.101
  166.8 1.0 reduce.21
  167.8 20.4 %all_to_all.130 = bf16[32,2,2560]{2,1,0:T(2,128)(2,1)} all-to-all(bf16[32,2,2560]{2,1,0:T(2,128)(2,1)S(1)} %reshape.334), channel_id=1, replica_groups=mesh['grp'=16,'seq'=32] {'seq'}, dimensions={0} | all-to-all | bytes 655360 | tf_op jit(solution)/shard_map/all_to_all | solution.py:164
  188.2 37.1 %all_to_all.131 = f32[2560,1,128]{2,1,0:T(1,128)S(1)} all-to-all(f32[2560,1,128]{2,1,0:T(1,128)S(1)} %bitcast.203), channel_id=1, replica_groups=mesh['grp'=16,'seq'=32] {'seq'}, dimensions={0} | all-to-all | bytes 2621440 | tf_op jit(solution)/shard_map/all_to_all | solution.py:168
  225.3 3.7 %all-to-all-start.7 = ((f32[2560,1,128]{2,1,0:T(1,128)}), f32[2560,1,128]{2,1,0:T(1,128)S(1)}, u32[]{:S(2)}, u32[]{:S(2)}) async-start(f32[2560,1,128]{2,1,0:T(1,128)} %bitcast.204), calls=%async_computation.7 | async-start | bytes 2621440 | tf_op jit(solution)/shard_map/all_to_all | solution.py:167
  229.1 0.8 reshape.312
  229.9 2.5 reshape.333
  233.4 2.5 reshape.335
  236.9 1.5 slice_bitcast_fusion.4
  238.4 1.9 fusion.54
  240.6 21.9 %all-to-all-done.7 = f32[2560,1,128]{2,1,0:T(1,128)S(1)} async-done(((f32[2560,1,128]{2,1,0:T(1,128)}), f32[2560,1,128]{2,1,0:T(1,128)S(1)}, u32[]{:S(2)}, u32[]{:S(2)}) %all-to-all-start.7) | async-done | bytes 1310752 | tf_op jit(solution)/shard_map/all_to_all | solution.py:167
  263.6 0.9 slice_bitcast_fusion
  264.5 1.8 copy.86
  (121 shorter events, 25.9 us)
Async XLA Ops:
  0.6 37.2 %copy-start.6 = (bf16[1,16,3,2048]{3,1,2,0:T(8,128)(2,1)S(1)}, bf16[1,16,3,2048]{3,1,2,0:T(8,128)(2,1)}, u32[]{:S(2)}) copy-start(bf16[1,16,3,2048]{3,1,2,0:T(8,128)(2,1)} %param.13) | copy-start | bytes 589828
  0.6 37.3 %copy-start.4 = (bf16[1,64,3,2048]{3,1,2,0:T(8,128)(2,1)S(1)}, bf16[1,64,3,2048]{3,1,2,0:T(8,128)(2,1)}, u32[]{:S(2)}) copy-start(bf16[1,64,3,2048]{3,1,2,0:T(8,128)(2,1)} %param.14) | copy-start | bytes 2359300
  0.7 28.2 %all-to-all-start.4 = ((bf16[16,1,4,2048]{3,2,1,0:T(4,128)(2,1)}), bf16[16,1,4,2048]{3,2,1,0:T(4,128)(2,1)S(1)}, u32[]{:S(2)}, u32[]{:S(2)}) async-start(bf16[16,1,4,2048]{3,2,1,0:T(4,128)(2,1)} %param.17), calls=%async_computation.4 | async-start | bytes 524288 | tf_op jit(solution)/shard_map/all_to_all | solution.py:158
  28.9 21.6 %all-to-all-start.5 = ((bf16[40,32,128]{2,0,1:T(8,128)(2,1)}), bf16[40,32,128]{2,0,1:T(8,128)(2,1)S(1)}, u32[]{:S(2)}, u32[]{:S(2)}) async-start(bf16[40,32,128]{2,0,1:T(8,128)(2,1)} %bitcast.32), calls=%async_computation.5 | async-start | bytes 655360 | tf_op jit(solution)/shard_map/all_to_all | solution.py:137
  38.3 33.3 %copy-start.3 = (bf16[1,64,2048]{2,1,0:T(8,128)(2,1)S(1)}, bf16[1,64,2048]{2,1,0:T(8,128)(2,1)}, u32[]{:S(2)}) copy-start(bf16[1,64,2048]{2,1,0:T(8,128)(2,1)} %param.16) | copy-start | bytes 786436
  38.5 34.1 %copy-start.7 = (f32[2048]{0:T(1024)S(1)}, f32[2048]{0:T(1024)}, u32[]{:S(2)}) copy-start(f32[2048]{0:T(1024)} %param.18) | copy-start | bytes 24580
  50.5 16.4 %all-to-all-start.1 = ((bf16[40,32,128]{2,0,1:T(8,128)(2,1)}), bf16[40,32,128]{2,0,1:T(8,128)(2,1)S(1)}, u32[]{:S(2)}, u32[]{:S(2)}) async-start(bf16[40,32,128]{2,0,1:T(8,128)(2,1)} %bitcast.8), calls=%async_computation.1 | async-start | bytes 655360 | tf_op jit(solution)/shard_map/all_to_all | solution.py:136
  67.8 23.3 %all-to-all-start = ((bf16[80,32,128]{2,0,1:T(8,128)(2,1)}), bf16[80,32,128]{2,0,1:T(8,128)(2,1)S(1)}, u32[]{:S(2)}, u32[]{:S(2)}) async-start(bf16[80,32,128]{2,0,1:T(8,128)(2,1)} %bitcast.2), calls=%async_computation | async-start | bytes 1310720 | tf_op jit(solution)/shard_map/all_to_all | solution.py:138
  92.1 23.4 %all-to-all-start.2 = ((bf16[80,32,128]{2,0,1:T(8,128)(2,1)}), bf16[80,32,128]{2,0,1:T(8,128)(2,1)S(1)}, u32[]{:S(2)}, u32[]{:S(2)}) async-start(bf16[80,32,128]{2,0,1:T(8,128)(2,1)} %bitcast.17), calls=%async_computation.2 | async-start | bytes 1310720 | tf_op jit(solution)/shard_map/all_to_all | solution.py:139
  115.5 21.6 %all-to-all-start.9 = ((bf16[16,1,4,2048]{3,2,1,0:T(4,128)(2,1)}), bf16[16,1,4,2048]{3,2,1,0:T(4,128)(2,1)}, u32[]{:S(2)}, u32[]{:S(2)}) async-start(bf16[16,1,4,2048]{3,2,1,0:T(4,128)(2,1)} %multiply_convert_fusion.1), calls=%async_computation.9 | async-start | bytes 524288 | tf_op jit(solution)/shard_map/all_to_all | solution.py:180
  132.4 0.6 copy-start.5
  137.2 30.6 %all-to-all-start.3 = ((bf16[32,2,2560]{2,1,0:T(2,128)(2,1)}), bf16[32,2,2560]{2,1,0:T(2,128)(2,1)S(1)}, u32[]{:S(2)}, u32[]{:S(2)}) async-start(bf16[32,2,2560]{2,1,0:T(2,128)(2,1)} %reshape.332), calls=%async_computation.3 | async-start | bytes 655360 | tf_op jit(solution)/shard_map/all_to_all | solution.py:156
  166.7 21.5 %copy-start.1 = (f32[4,1,640,128]{3,2,1,0:T(8,128)S(1)}, f32[4,1,640,128]{3,2,1,0:T(8,128)}, u32[]{:S(2)}) copy-start(f32[4,1,640,128]{3,2,1,0:T(8,128)} %get-tuple-element.149) | copy-start | bytes 3932164
  167.8 61.2 %copy-start.2 = (bf16[32,2,2560]{2,1,0:T(2,128)(2,1)}, bf16[32,2,2560]{2,1,0:T(2,128)(2,1)S(1)}, u32[]{:S(2)}) copy-start(bf16[32,2,2560]{2,1,0:T(2,128)(2,1)S(1)} %all-to-all-done.3) | copy-start | bytes 983044
  225.3 37.2 %all-to-all-start.7 = ((f32[2560,1,128]{2,1,0:T(1,128)}), f32[2560,1,128]{2,1,0:T(1,128)S(1)}, u32[]{:S(2)}, u32[]{:S(2)}) async-start(f32[2560,1,128]{2,1,0:T(1,128)} %bitcast.204), calls=%async_computation.7 | async-start | bytes 2621440 | tf_op jit(solution)/shard_map/all_to_all | solution.py:167
  232.4 6.0 %copy-start.8 = (f32[2048]{0:T(1024)S(1)}, f32[2048]{0:T(1024)}, u32[]{:S(2)}) copy-start(f32[2048]{0:T(1024)} %param.18) | copy-start | bytes 24580
  240.3 22.5 %copy-start = (bf16[80,3,2048]{2,0,1:T(8,128)(2,1)S(1)}, bf16[80,3,2048]{2,0,1:T(8,128)(2,1)}, u32[]{:S(2)}) copy-start(bf16[80,3,2048]{2,0,1:T(8,128)(2,1)} %constant_dynamic-update-slice_fusion.4) | copy-start | bytes 2949124
where the time goes:
time: 268 us; the launch traced here: 266 us
  waiting for transfers between devices  88.3 us (33%)
  blocking collectives  57.5 us (21%)
  starting transfers between devices  48.1 us (18%)
  matrix products  34.6 us (13%)
  local copies, waits for them, and re-layouts  23.2 us (9%)
  other arithmetic  12.4 us (5%)
    all_to_all x1, blocking collectives, body(): lax.all_to_all(value_grad, 'seq', split_axis=0, concat_axis=1, tiled=True)  37.1 us
    all_to_all x1, waiting for transfers between devices, body(): lax.all_to_all(key_grad, 'seq', split_axis=0, concat_axis=1, tiled=True)  21.9 us
    all_to_all x1, blocking collectives, body(): lax.all_to_all(query_grad, 'seq', split_axis=0, concat_axis=1, tiled=True)  20.4 us
    all_to_all x1, waiting for transfers between devices, body(): lax.all_to_all(key_units, 'seq', split_axis=1, concat_axis=0, tiled=True)  17.8 us
    all_to_all x1, starting transfers between devices, body(): lax.all_to_all(control_residual, 'grp', split_axis=0, concat_axis=0, tile...  16.4 us
    all_to_all x1, waiting for transfers between devices, body(): lax.all_to_all(value_units, 'seq', split_axis=1, concat_axis=0, tiled=True)  14.8 us
    all_to_all x1, waiting for transfers between devices, body(): lax.all_to_all(query_units, 'seq', split_axis=1, concat_axis=0, tiled=True)  12.6 us
    dot_general x4, matrix products, forward_step(): jnp.dot(weights, value_block, preferred_element_type=jnp.float32)  12.4 us
  transfers between devices with their start and end apart: 8, of which 6 were waited for; matrix products, arithmetic and copies ran while one was open for 24% of the time, Pallas kernels for 0%

commit v1 on v0

v1 whole, which is shorter than its diff:
```python
import functools
import math

import jax
import jax.numpy as jnp
from jax import lax
from jax.experimental import pallas as pl
from jax.experimental.pallas import tpu as pltpu
from jax.sharding import Mesh, PartitionSpec as P

HEAD = 128
HEADS = 16
TXT = 16
IMG = 64
ROWS = TXT + IMG
CHIPS = 16
SCALE = 1.0 / math.sqrt(HEAD)
SCALE2 = SCALE * math.log2(math.e)
BQ = 256
BK = 512
NQ = CHIPS * ROWS
NK = 2 * NQ
TXT_KEYS = 2 * CHIPS * TXT

VM = pl.BlockSpec(memory_space=pltpu.VMEM)
SM = pl.BlockSpec(memory_space=pltpu.SMEM)


def dot(a, b):
    return lax.dot_general(a, b, (((1,), (0,)), ((), ())), preferred_element_type=jnp.float32)


def dot_t(a, b):
    return lax.dot_general(a, b, (((1,), (1,)), ((), ())), preferred_element_type=jnp.float32)


def pack_kernel(th, ih, tc, ic, out):
    for h in range(HEADS):
        cols = slice(h * HEAD, (h + 1) * HEAD)
        for t in range(3):
            out[h, t, :TXT, :] = th[t, :, cols]
            out[h, t, TXT:, :] = ih[t, :, cols]
        out[h, 3, :TXT, :] = tc[:, cols]
        out[h, 3, TXT:, :] = ic[:, cols]


def attention_kernel(
    info, own, oth, aq, part_own, part_oth, q_s, g_s, k_s, v_s, s_s, e_s, dk_s, dv_s, mask_s
):
    length = info[0]
    core = info[1]
    half_txt = CHIPS * TXT
    half_img = CHIPS * IMG
    for s in range(CHIPS):
        q_s[s * ROWS : (s + 1) * ROWS, :] = own[s, 0]
        g_s[s * ROWS : (s + 1) * ROWS, :] = own[s, 3]
        for h, src in ((0, own), (1, oth)):
            for t, dst in ((1, k_s), (2, v_s)):
                at = h * half_txt + s * TXT
                dst[at : at + TXT, :] = src[s, t, :TXT, :]
                at = TXT_KEYS + h * half_img + s * IMG
                dst[at : at + IMG, :] = src[s, t, TXT:, :]
    pos = lax.broadcasted_iota(jnp.int32, (8, TXT_KEYS), 1)
    half = jnp.where(pos < half_txt, core, 1 - core)
    token = ((pos % half_txt) // TXT) * (2 * TXT) + half * TXT + pos % TXT
    mask_s[...] = jnp.where(token < length, 0.0, -jnp.inf)
    dk_s[...] = jnp.zeros_like(dk_s)
    dv_s[...] = jnp.zeros_like(dv_s)
    chunks = NK // BK

    def block(i):
        rows = slice(i * BQ, (i + 1) * BQ)
        q = q_s[rows, :]
        g = g_s[rows, :]
        top = jnp.full((BQ, 128), -jnp.inf, jnp.float32)
        for c in range(chunks):
            cols = slice(c * BK, (c + 1) * BK)
            s = dot_t(q, k_s[cols, :])
            if c == 0:
                s = s + mask_s[0:1, :]
            s_s[:, cols] = s
            for t in range(BK // 128):
                top = jnp.maximum(top, s[:, t * 128 : (t + 1) * 128])
        row_max = jnp.max(top, axis=1, keepdims=True)
        total = jnp.zeros((BQ, 128), jnp.float32)
        a = jnp.zeros((BQ, HEAD), jnp.float32)
        for c in range(chunks):
            cols = slice(c * BK, (c + 1) * BK)
            e = jnp.exp2((s_s[:, cols] - row_max) * SCALE2)
            for t in range(BK // 128):
                total = total + e[:, t * 128 : (t + 1) * 128]
            eb = e.astype(jnp.bfloat16)
            e_s[:, cols] = eb
            a = a + dot(eb, v_s[cols, :])
        inv = 1.0 / jnp.sum(total, axis=1, keepdims=True)
        ab = (a * inv).astype(jnp.bfloat16)
        gs = (g.astype(jnp.float32) * inv).astype(jnp.bfloat16)
        delta = jnp.sum(gs.astype(jnp.float32) * ab.astype(jnp.float32), axis=1, keepdims=True)
        gt = gs.T
        qt = q.T
        dq = jnp.zeros((BQ, HEAD), jnp.float32)
        for c in range(chunks):
            cols = slice(c * BK, (c + 1) * BK)
            eb = e_s[:, cols]
            dp = dot_t(gs, v_s[cols, :])
            ds = eb * (dp - delta).astype(jnp.bfloat16)
            dv_s[:, cols] += dot(gt, eb)
            dk_s[:, cols] += dot(qt, ds)
            dq = dq + dot(ds, k_s[cols, :])
        aq[0, rows, :] = ab
        aq[1, rows, :] = (dq * SCALE).astype(jnp.bfloat16)

    for i in range(NQ // BQ):
        block(i)
    for t, src, factor in ((0, dk_s, SCALE), (1, dv_s, 1.0)):
        for h, dst in ((0, part_own), (1, part_oth)):
            xt = src[:, h * half_txt : (h + 1) * half_txt].T * factor
            at = TXT_KEYS + h * half_img
            xi = src[:, at : at + half_img].T * factor
            for s in range(CHIPS):
                dst[s, t, :TXT, :] = xt[s * TXT : (s + 1) * TXT]
                dst[s, t, TXT:, :] = xi[s * IMG : (s + 1) * IMG]


def combine_kernel(aq, mine, theirs, out):
    for s in range(CHIPS):
        for t in range(2):
            out[s, t] = aq[t, s * ROWS : (s + 1) * ROWS, :]
            out[s, 2 + t] = (mine[s, t] + theirs[s, t]).astype(jnp.bfloat16)


def unpack_kernel(back, residual, gain, ta, io, tg, ig):
    for h in range(HEADS):
        cols = slice(h * HEAD, (h + 1) * HEAD)
        ta[:, cols] = back[h, 0, :TXT, :]
        io[:, cols] = (
            back[h, 0, TXT:, :].astype(jnp.float32)
            + gain[0:1, cols] * residual[:, cols].astype(jnp.float32)
        ).astype(jnp.bfloat16)
        for t in range(3):
            tg[t, :, cols] = back[h, 1 + t, :TXT, :]
            ig[t, :, cols] = back[h, 1 + t, TXT:, :]


def call(kernel, ins, outs, scratch=(), **kw):
    return pl.pallas_call(
        kernel,
        in_specs=ins,
        out_specs=[VM] * len(outs) if len(outs) > 1 else VM,
        out_shape=[jax.ShapeDtypeStruct(s, d) for s, d in outs]
        if len(outs) > 1
        else jax.ShapeDtypeStruct(*outs[0]),
        scratch_shapes=scratch,
        compiler_params=pltpu.CompilerParams(vmem_limit_bytes=48 << 20),
        **kw,
    )


def body(th, ih, tc, ic, residual, gain, lengths):
    bf16, f32 = jnp.bfloat16, jnp.float32
    chips = ("x", "yl")
    grp = ("yh", "z")
    width = HEADS * HEAD
    core = lax.axis_index("core")
    info = jnp.stack([lengths[0], core.astype(jnp.int32)])
    send = call(pack_kernel, [VM] * 4, [((HEADS, 4, ROWS, HEAD), bf16)], name="pack")(
        jnp.swapaxes(th[0], 0, 1), jnp.swapaxes(ih[0], 0, 1), tc[0], ic[0]
    )
    own = lax.all_to_all(send, chips, split_axis=0, concat_axis=0, tiled=True)
    swap = [(0, 1), (1, 0)]
    oth = lax.ppermute(own, "core", swap)
    outgoing = (gain[None, :] * ic[0].astype(f32)).astype(bf16).reshape(residual.shape)
    control = lax.all_to_all(
        jnp.stack([residual, outgoing], axis=1), grp, split_axis=0, concat_axis=0, tiled=True
    )
    part = ((CHIPS, 2, ROWS, HEAD), f32)
    aq, mine, give = call(
        attention_kernel,
        [SM, VM, VM],
        [((2, NQ, HEAD), bf16), part, part],
        [
            pltpu.VMEM((NQ, HEAD), bf16),
            pltpu.VMEM((NQ, HEAD), bf16),
            pltpu.VMEM((NK, HEAD), bf16),
            pltpu.VMEM((NK, HEAD), bf16),
            pltpu.VMEM((BQ, NK), f32),
            pltpu.VMEM((BQ, NK), bf16),
            pltpu.VMEM((HEAD, NK), f32),
            pltpu.VMEM((HEAD, NK), f32),
            pltpu.VMEM((8, TXT_KEYS), f32),
        ],
        name="attention",
        cost_estimate=pl.CostEstimate(
            flops=14 * NQ * NK * HEAD, bytes_accessed=8 << 20, transcendentals=NQ * NK
        ),
    )(info, own, oth)
    theirs = lax.ppermute(give, "core", swap)
    ready = call(combine_kernel, [VM] * 3, [((CHIPS, 4, ROWS, HEAD), bf16)], name="combine")(
        aq, mine, theirs
    )
    back = lax.all_to_all(ready, chips, split_axis=0, concat_axis=0, tiled=True)
    arrived = control[:, 0].reshape(IMG, width)
    ta, io, tg, ig = call(
        unpack_kernel,
        [VM] * 3,
        [((TXT, width), bf16), ((IMG, width), bf16), ((3, TXT, width), bf16), ((3, IMG, width), bf16)],
        name="unpack",
    )(back, arrived, gain[None, :])
    return (
        ta[None],
        io[None],
        jnp.swapaxes(tg, 0, 1)[None],
        jnp.swapaxes(ig, 0, 1)[None],
        control[:, 1],
    )


def solution(mesh):
    fine = Mesh(mesh.devices.reshape(2, 8, 4, 4, 2), ("yh", "z", "x", "yl", "core"))
    grp = ("yh", "z")
    seq = ("x", "yl", "core")
    in_specs = (
        P(grp, seq, None, None),
        P(grp, seq, None, None),
        P(grp, seq, None),
        P(grp, seq, None),
        P(None, seq, grp, None),
        P(),
        P(grp),
    )
    out_specs = (
        P(grp, seq, None),
        P(grp, seq, None),
        P(grp, seq, None, None),
        P(grp, seq, None, None),
        P(None, seq, grp, None),
    )
    return jax.shard_map(body, mesh=fine, in_specs=in_specs, out_specs=out_specs, check_vma=False)
```

time: 268 us -> 143 us (0.53)
  waiting for transfers between devices: 88.3 us -> 47.1 us
  matrix products: 34.6 us -> 0 us
  starting transfers between devices: 48.1 us -> 24.2 us
  Pallas kernels: 0 us -> 18.2 us
  blocking collectives: 57.5 us -> 40.7 us
  local copies, waits for them, and re-layouts: 23.2 us -> 9.25 us
  other arithmetic: 12.4 us -> 1.33 us
    all_to_all x8 -> x2, waiting for transfers between devices: 88.3 us -> 46.1 us  [the longest x1 30.6 us: body(): back = lax.all_to_all(ready, chips, split_axis=0, concat_axis=0, tiled=True)]
    dot_general x28 -> x0, matrix products: 34.6 us -> none  [the longest x4 12.4 us: forward_step(): jnp.dot(weights, value_block, preferred_element_type=jnp.float32)]
    all_to_all x8 -> x2, starting transfers between devices: 48.1 us -> 18.5 us  [the longest x1 12.8 us: body(): lax.all_to_all(jnp.stack([residual, outgoing], axis=1), grp, split_axis=0...]
    pallas_call x0 -> x4, Pallas kernels: none -> 18.2 us  [the longest x1 15.4 us: body(): call(attention_kernel, [SM, VM, VM], [((2, NQ, HEAD), bf16), part, part],...]
    all_to_all x2 -> x1, blocking collectives: 57.5 us -> 40.7 us  [body(): own = lax.all_to_all(send, chips, split_axis=0, concat_axis=0, tiled=True)]
    ppermute x0 -> x2, starting transfers between devices: none -> 5.67 us  [the longest x1 3.4 us: body(): oth = lax.ppermute(own, 'core', swap)]
    broadcast_in_dim x5 -> x0, local copies, waits for them, and re-layouts: 4.96 us -> none  [the longest x1 1.47 us: body(): text_attention = attention_rows[:text_rows][None]]
    reduce_sum x7 -> x0, other arithmetic: 3.38 us -> none  [the longest x4 1.92 us: stats_step(): jnp.sum(jnp.exp(scores - new_max[:, None]), axis=1)]
  transfers between devices with their start and end apart: 8 -> 4, of which waited for: 6 -> 3; matrix products, arithmetic and copies ran while one was open for 24% -> 3% of each run, Pallas kernels for 0% -> 1%
where the time goes in v1:
time: 143 us; the launch traced here: 142 us
  waiting for transfers between devices  47.1 us (33%)
  blocking collectives  40.7 us (28%)
  starting transfers between devices  24.2 us (17%)
  Pallas kernels  18.2 us (13%)
  local copies, waits for them, and re-layouts  9.25 us (6%)
    all_to_all x1, blocking collectives, body(): own = lax.all_to_all(send, chips, split_axis=0, concat_axis=0, tiled=True)  40.7 us
    all_to_all x1, waiting for transfers between devices, body(): back = lax.all_to_all(ready, chips, split_axis=0, concat_axis=0, tiled=True)  30.6 us
    all_to_all x1, waiting for transfers between devices, body(): lax.all_to_all(jnp.stack([residual, outgoing], axis=1), grp, split_axis=0...  15.6 us
    pallas_call x1, Pallas kernels, body(): call(attention_kernel, [SM, VM, VM], [((2, NQ, HEAD), bf16), part, part],...  15.4 us
    all_to_all x1, starting transfers between devices, body(): lax.all_to_all(jnp.stack([residual, outgoing], axis=1), grp, split_axis=0...  12.8 us
    unnamed x21, local copies, waits for them, and re-layouts  8.23 us
    all_to_all x1, starting transfers between devices, body(): back = lax.all_to_all(ready, chips, split_axis=0, concat_axis=0, tiled=True)  5.75 us
    ppermute x1, starting transfers between devices, body(): oth = lax.ppermute(own, 'core', swap)  3.4 us
  transfers between devices with their start and end apart: 4, of which 3 were waited for; matrix products, arithmetic and copies ran while one was open for 3% of the time, Pallas kernels for 1%

profile of v1, /device:TPU:1, one launch (start us, length us, event | category | flops | bytes accessed | tf_op | source)
XLA Modules:
  0.0 142.2 jit_solution(2753392471554856209)
XLA Ops:
  0.6 0.0 copy-start
  0.6 0.9 copy-done
  1.6 0.0 copy-start.2
  1.6 1.1 copy-done.2
  2.7 0.0 copy-start.3
  2.7 0.9 copy-done.3
  3.6 0.0 copy-start.4
  3.6 0.8 copy-done.4
  4.5 0.2 pack.1
  4.7 0.0 copy-start.1
  4.7 40.7 %all_to_all.15.own = bf16[16,4,80,128]{3,2,1,0:T(8,128)(2,1)S(1)} all-to-all(bf16[16,4,80,128]{3,2,1,0:T(8,128)(2,1)S(1)} %pack.1), channel_id=1, replica_groups=mesh['yh'=2,'z'=8,'x'=4,'yl'=4,'core'=2] {'x','yl'}, dimensions={0} | all-to-all | bytes 2621440 | tf_op jit(solution)/shard_map/all_to_all | solution.py:169
  45.5 3.4 %collective-permute-start = (bf16[16,4,80,128]{3,2,1,0:T(8,128)(2,1)S(1)}, bf16[16,4,80,128]{3,2,1,0:T(8,128)(2,1)S(1)}, u32[]{:S(2)}, u32[]{:S(2)}) collective-permute-start(bf16[16,4,80,128]{3,2,1,0:T(8,128)(2,1)S(1)} %all_to_all.15.own), channel_id=1, source_target_pairs={{0,1},{1,0},{2,3},{3,2},{4,5},{5,4},{6,7},{7,6},{8,9},{9,8},{10,11... | collective-permute-start | bytes 3932168 | tf_op jit(solution)/shard_map/ppermute | solution.py:171
  48.9 0.0 copy-done.1
  48.9 1.0 reshape.34
  50.5 0.1 pad_add_fusion.info
  50.6 0.0 copy-start.5
  50.6 0.9 collective-permute-done.oth
  51.5 0.0 copy-start.6
  51.5 1.1 copy-done.6
  52.6 0.0 copy-start.7
  52.6 1.3 copy-done.7
  53.9 0.0 copy-start.8
  53.9 0.0 copy-start.9
  53.9 15.4 %attention.1 = (bf16[2,1280,128]{2,1,0:T(8,128)(2,1)S(1)}, f32[16,2,80,128]{3,2,1,0:T(8,128)S(1)}, f32[16,2,80,128]{3,2,1,0:T(8,128)}) custom-call(s32[2]{0:T(128)S(1)} %pad_add_fusion.info, bf16[16,4,80,128]{3,2,1,0:T(8,128)(2,1)S(1)} %all_to_all.15.own, bf16[16,4,80,128]{3,2,1,0:T(8,128)(2,1)S(1)} %copy-done.7), custom_call_target="tpu_custom_call" | custom-call | flops 5872025600 | bytes 8388608 | tf_op jit(solution)/shard_map/attention/pallas_call | solution.py:177
  69.3 2.3 %collective-permute-start.1 = (f32[16,2,80,128]{3,2,1,0:T(8,128)}, f32[16,2,80,128]{3,2,1,0:T(8,128)S(1)}, u32[]{:S(2)}, u32[]{:S(2)}) collective-permute-start(f32[16,2,80,128]{3,2,1,0:T(8,128)} %get-tuple-element.14), channel_id=1, source_target_pairs={{0,1},{1,0},{2,3},{3,2},{4,5},{5,4},{6,7},{7,6},{8,9},{9,8},{10,11... | collective-permute-start | bytes 3932168 | tf_op jit(solution)/shard_map/ppermute | solution.py:197
  71.6 0.0 copy-done.5
  71.6 0.0 copy-done.8
  71.6 0.1 multiply_convert_fusion
  71.7 0.0 copy-done.9
  71.7 1.1 pad_maximum_fusion
  72.9 12.8 %all-to-all-start.2 = ((bf16[16,2,1,4,2048]{4,3,2,1,0:T(4,128)(2,1)}), bf16[16,2,1,4,2048]{4,3,2,1,0:T(4,128)(2,1)}, u32[]{:S(2)}, u32[]{:S(2)}) async-start(bf16[16,2,1,4,2048]{4,3,2,1,0:T(4,128)(2,1)} %pad_maximum_fusion), calls=%async_computation.2 | async-start | bytes 1048576 | tf_op jit(solution)/shard_map/all_to_all | solution.py:173
  85.6 0.0 collective-permute-done.1.theirs
  85.7 1.3 combine.1
  86.9 15.6 %all-to-all-done.2 = bf16[16,2,1,4,2048]{4,3,2,1,0:T(4,128)(2,1)} async-done(((bf16[16,2,1,4,2048]{4,3,2,1,0:T(4,128)(2,1)}), bf16[16,2,1,4,2048]{4,3,2,1,0:T(4,128)(2,1)}, u32[]{:S(2)}, u32[]{:S(2)}) %all-to-all-start.2) | async-done | bytes 524320 | tf_op jit(solution)/shard_map/all_to_all | solution.py:173
  102.5 5.8 %all-to-all-start.1 = ((bf16[16,4,80,128]{3,2,1,0:T(8,128)(2,1)}), bf16[16,4,80,128]{3,2,1,0:T(8,128)(2,1)S(1)}, u32[]{:S(2)}, u32[]{:S(2)}) async-start(bf16[16,4,80,128]{3,2,1,0:T(8,128)(2,1)} %combine.1), calls=%async_computation.1 | async-start | bytes 2621440 | tf_op jit(solution)/shard_map/all_to_all | solution.py:201
  108.2 2.0 %slice_bitcast_fusion = (bf16[16,1,4,2048]{3,2,1,0:T(4,128)(2,1)}, bf16[16,1,1,4,2048]{4,3,2,1,0:T(4,128)(2,1)S(1)}) fusion(bf16[16,2,1,4,2048]{4,3,2,1,0:T(4,128)(2,1)} %all-to-all-done.2), kind=kLoop, calls=%fused_computation.2 | loop fusion | bytes 1048576
  110.2 0.1 reshape_squeeze.3.residual
  110.3 30.6 %all-to-all-done.1.back = bf16[16,4,80,128]{3,2,1,0:T(8,128)(2,1)S(1)} async-done(((bf16[16,4,80,128]{3,2,1,0:T(8,128)(2,1)}), bf16[16,4,80,128]{3,2,1,0:T(8,128)(2,1)S(1)}, u32[]{:S(2)}, u32[]{:S(2)}) %all-to-all-start.1) | async-done | bytes 1310752 | tf_op jit(solution)/shard_map/all_to_all | solution.py:201
  140.8 1.4 unpack.1
Async XLA Ops:
  0.6 1.0 copy-start
  1.6 1.1 copy-start.2
  2.7 0.9 copy-start.3
  3.6 0.8 copy-start.4
  4.7 44.2 %copy-start.1 = (bf16[1,64,2048]{2,1,0:T(8,128)(2,1)S(1)}, bf16[1,64,2048]{2,1,0:T(8,128)(2,1)}, u32[]{:S(2)}) copy-start(bf16[1,64,2048]{2,1,0:T(8,128)(2,1)} %param.10) | copy-start | bytes 786436
  45.5 6.0 %collective-permute-start = (bf16[16,4,80,128]{3,2,1,0:T(8,128)(2,1)S(1)}, bf16[16,4,80,128]{3,2,1,0:T(8,128)(2,1)S(1)}, u32[]{:S(2)}, u32[]{:S(2)}) collective-permute-start(bf16[16,4,80,128]{3,2,1,0:T(8,128)(2,1)S(1)} %all_to_all.15.own), channel_id=1, source_target_pairs={{0,1},{1,0},{2,3},{3,2},{4,5},{5,4},{6,7},{7,6},{8,9},{9,8},{10,11... | collective-permute-start | bytes 3932168 | tf_op jit(solution)/shard_map/ppermute | solution.py:171
  50.6 21.0 %copy-start.5 = (f32[2048]{0:T(1024)S(1)}, f32[2048]{0:T(1024)}, u32[]{:S(2)}) copy-start(f32[2048]{0:T(1024)} %param.12) | copy-start | bytes 24580
  51.5 1.1 copy-start.6
  52.6 1.3 copy-start.7
  53.9 17.7 %copy-start.8 = (f32[16,1,1,4,2048]{4,3,2,1,0:T(4,128)S(1)}, f32[16,1,1,4,2048]{4,3,2,1,0:T(4,128)}, u32[]{:S(2)}) copy-start(f32[16,1,1,4,2048]{4,3,2,1,0:T(4,128)} %reshape.34) | copy-start | bytes 1572868
  53.9 17.8 %copy-start.9 = (bf16[16,1,4,2048]{3,2,1,0:T(4,128)(2,1)S(1)}, bf16[16,1,4,2048]{3,2,1,0:T(4,128)(2,1)}, u32[]{:S(2)}) copy-start(bf16[16,1,4,2048]{3,2,1,0:T(4,128)(2,1)} %param.11) | copy-start | bytes 786436
  69.3 16.3 %collective-permute-start.1 = (f32[16,2,80,128]{3,2,1,0:T(8,128)}, f32[16,2,80,128]{3,2,1,0:T(8,128)S(1)}, u32[]{:S(2)}, u32[]{:S(2)}) collective-permute-start(f32[16,2,80,128]{3,2,1,0:T(8,128)} %get-tuple-element.14), channel_id=1, source_target_pairs={{0,1},{1,0},{2,3},{3,2},{4,5},{5,4},{6,7},{7,6},{8,9},{9,8},{10,11... | collective-permute-start | bytes 3932168 | tf_op jit(solution)/shard_map/ppermute | solution.py:197
  72.9 29.6 %all-to-all-start.2 = ((bf16[16,2,1,4,2048]{4,3,2,1,0:T(4,128)(2,1)}), bf16[16,2,1,4,2048]{4,3,2,1,0:T(4,128)(2,1)}, u32[]{:S(2)}, u32[]{:S(2)}) async-start(bf16[16,2,1,4,2048]{4,3,2,1,0:T(4,128)(2,1)} %pad_maximum_fusion), calls=%async_computation.2 | async-start | bytes 1048576 | tf_op jit(solution)/shard_map/all_to_all | solution.py:173
  102.5 38.4 %all-to-all-start.1 = ((bf16[16,4,80,128]{3,2,1,0:T(8,128)(2,1)}), bf16[16,4,80,128]{3,2,1,0:T(8,128)(2,1)S(1)}, u32[]{:S(2)}, u32[]{:S(2)}) async-start(bf16[16,4,80,128]{3,2,1,0:T(8,128)(2,1)} %combine.1), calls=%async_computation.1 | async-start | bytes 2621440 | tf_op jit(solution)/shard_map/all_to_all | solution.py:201

commit v2 on v1

--- a/solution.py
+++ b/solution.py
@@ -13,6 +13,8 @@
 TXT = 16
 IMG = 64
 ROWS = TXT + IMG
+ZS = 8
+EARLY = 5
 CHIPS = 16
 SCALE = 1.0 / math.sqrt(HEAD)
 SCALE2 = SCALE * math.log2(math.e)
@@ -24,6 +26,7 @@
 
 VM = pl.BlockSpec(memory_space=pltpu.VMEM)
 SM = pl.BlockSpec(memory_space=pltpu.SMEM)
+HBM = pl.BlockSpec(memory_space=pltpu.HBM)
 
 
 def dot(a, b):
@@ -34,14 +37,56 @@
     return lax.dot_general(a, b, (((1,), (1,)), ((), ())), preferred_element_type=jnp.float32)
 
 
-def pack_kernel(th, ih, tc, ic, out):
+def pack_kernel(th, ih, tc, ic, out, th_s, ih_s, tc_s, ic_s, sems):
+    copies = []
+    for t in range(3):
+        copies.append((ih.at[t], ih_s.at[t]))
+        copies.append((th.at[t], th_s.at[t]))
+    copies += [(ic, ic_s), (tc, tc_s)]
+    copies = [pltpu.make_async_copy(a, b, sems.at[n]) for n, (a, b) in enumerate(copies)]
+    for c in copies:
+        c.start()
+    for c in copies:
+        c.wait()
     for h in range(HEADS):
         cols = slice(h * HEAD, (h + 1) * HEAD)
         for t in range(3):
-            out[h, t, :TXT, :] = th[t, :, cols]
-            out[h, t, TXT:, :] = ih[t, :, cols]
-        out[h, 3, :TXT, :] = tc[:, cols]
-        out[h, 3, TXT:, :] = ic[:, cols]
+            out[h, t, :TXT, :] = th_s[t, :, cols]
+            out[h, t, TXT:, :] = ih_s[t, :, cols]
+        out[h, 3, :TXT, :] = tc_s[:, cols]
+        out[h, 3, TXT:, :] = ic_s[:, cols]
+
+
+def control_pack_kernel(info, residual, ic, gain, *refs):
+    outs, scaled = refs[:ZS], refs[ZS]
+    yh, z = info[2], info[3]
+    for r in range(IMG // 16):
+        x = ic[r * 16 : (r + 1) * 16, :].astype(jnp.float32) * gain[0:1, :]
+        for i in range(4):
+            scaled[r * 4 + i] = x[i * 4 : (i + 1) * 4].astype(jnp.bfloat16)
+    for k in range(ZS):
+        for rel in range(2):
+            g = (yh if rel == 0 else 1 - yh) * ZS + lax.rem(z + k, ZS)
+            outs[k][rel, 0] = residual[g]
+            outs[k][rel, 1] = scaled[g]
+
+
+def control_unpack_kernel(info, *refs):
+    near, far, late = refs[:EARLY], refs[EARLY], refs[EARLY + 1 : ZS + 1]
+    grads, arrived, rows = refs[ZS + 1 :]
+    yh, z = info[2], info[3]
+    for k in range(ZS):
+        for rel in range(2):
+            g = (yh if rel == 0 else 1 - yh) * ZS + lax.rem(z + ZS - k, ZS)
+            if k >= EARLY:
+                src = late[k - EARLY].at[rel]
+            else:
+                src = near[k].at[0] if rel == 0 else far.at[k]
+            rows[g] = src[0]
+            grads[g] = src[1]
+    for r in range(IMG // 16):
+        part = [rows[r * 4 + i].astype(jnp.float32) for i in range(4)]
+        arrived[r * 16 : (r + 1) * 16, :] = jnp.concatenate(part, axis=0).astype(jnp.bfloat16)
 
 
 def attention_kernel(
@@ -142,7 +187,7 @@
             ig[t, :, cols] = back[h, 1 + t, TXT:, :]
 
 
-def call(kernel, ins, outs, scratch=(), **kw):
+def call(kernel, ins, outs, scratch=(), vmem=8, **kw):
     return pl.pallas_call(
         kernel,
         in_specs=ins,
@@ -151,7 +196,7 @@
         if len(outs) > 1
         else jax.ShapeDtypeStruct(*outs[0]),
         scratch_shapes=scratch,
-        compiler_params=pltpu.CompilerParams(vmem_limit_bytes=48 << 20),
+        compiler_params=pltpu.CompilerParams(vmem_limit_bytes=vmem << 20),
         **kw,
     )
 
@@ -162,17 +207,42 @@
     grp = ("yh", "z")
     width = HEADS * HEAD
     core = lax.axis_index("core")
-    info = jnp.stack([lengths[0], core.astype(jnp.int32)])
-    send = call(pack_kernel, [VM] * 4, [((HEADS, 4, ROWS, HEAD), bf16)], name="pack")(
-        jnp.swapaxes(th[0], 0, 1), jnp.swapaxes(ih[0], 0, 1), tc[0], ic[0]
-    )
+    index = [core, lax.axis_index("yh"), lax.axis_index("z")]
+    info = jnp.stack([lengths[0]] + [i.astype(jnp.int32) for i in index])
+    send = call(
+        pack_kernel,
+        [HBM] * 4,
+        [((HEADS, 4, ROWS, HEAD), bf16)],
+        [
+            pltpu.VMEM((3, TXT, width), bf16),
+            pltpu.VMEM((3, IMG, width), bf16),
+            pltpu.VMEM((TXT, width), bf16),
+            pltpu.VMEM((IMG, width), bf16),
+            pltpu.SemaphoreType.DMA((8,)),
+        ],
+        vmem=63,
+        name="pack",
+    )(jnp.swapaxes(th[0], 0, 1), jnp.swapaxes(ih[0], 0, 1), tc[0], ic[0])
+    send, late_ic = lax.optimization_barrier((send, ic[0]))
     own = lax.all_to_all(send, chips, split_axis=0, concat_axis=0, tiled=True)
     swap = [(0, 1), (1, 0)]
+    piece = (2, 2, 4, width)
+    pieces = call(
+        control_pack_kernel,
+        [SM] + [VM] * 3,
+        [(piece, bf16)] * ZS,
+        [pltpu.VMEM((16, 4, width), bf16)],
+        name="control_pack",
+    )(info, residual[:, 0], late_ic, gain[None, :])
+
+    def shift(x, k):
+        return lax.ppermute(x, "z", [(i, (i + k) % ZS) for i in range(ZS)])
+
+    pieces = list(pieces)
+    near = pieces[:1] + [shift(pieces[k], k) for k in range(1, EARLY)]
+    own, *near = lax.optimization_barrier([own] + near)
     oth = lax.ppermute(own, "core", swap)
-    outgoing = (gain[None, :] * ic[0].astype(f32)).astype(bf16).reshape(residual.shape)
-    control = lax.all_to_all(
-        jnp.stack([residual, outgoing], axis=1), grp, split_axis=0, concat_axis=0, tiled=True
-    )
+    far = lax.ppermute(jnp.stack([p[1] for p in near + pieces[EARLY:]]), "yh", swap)
     part = ((CHIPS, 2, ROWS, HEAD), f32)
     aq, mine, give = call(
         attention_kernel,
@@ -189,17 +259,28 @@
             pltpu.VMEM((HEAD, NK), f32),
             pltpu.VMEM((8, TXT_KEYS), f32),
         ],
+        vmem=20,
         name="attention",
         cost_estimate=pl.CostEstimate(
             flops=14 * NQ * NK * HEAD, bytes_accessed=8 << 20, transcendentals=NQ * NK
         ),
     )(info, own, oth)
+    give, far = lax.optimization_barrier((give, far))
     theirs = lax.ppermute(give, "core", swap)
     ready = call(combine_kernel, [VM] * 3, [((CHIPS, 4, ROWS, HEAD), bf16)], name="combine")(
         aq, mine, theirs
     )
+    late = [jnp.stack([pieces[k][0], far[k]]) for k in range(EARLY, ZS)]
+    ready, *late = lax.optimization_barrier([ready] + late)
+    late = [shift(x, EARLY + n) for n, x in enumerate(late)]
     back = lax.all_to_all(ready, chips, split_axis=0, concat_axis=0, tiled=True)
-    arrived = control[:, 0].reshape(IMG, width)
+    grads, arrived = call(
+        control_unpack_kernel,
+        [SM] + [VM] * (ZS + 1),
+        [((16, 4, width), bf16), ((IMG, width), bf16)],
+        [pltpu.VMEM((16, 4, width), bf16)],
+        name="control_unpack",
+    )(info, *near, far, *late)
     ta, io, tg, ig = call(
         unpack_kernel,
         [VM] * 3,
@@ -211,7 +292,7 @@
         io[None],
         jnp.swapaxes(tg, 0, 1)[None],
         jnp.swapaxes(ig, 0, 1)[None],
-        control[:, 1],
+        grads[:, None],
     )
 
 

time: 143 us -> 112 us (0.78)
  blocking collectives: 40.7 us -> 0 us
  starting transfers between devices: 24.2 us -> 57.3 us
  waiting for transfers between devices: 47.1 us -> 30.2 us
  local copies, waits for them, and re-layouts: 9.25 us -> 0.27 us
  Pallas kernels: 18.2 us -> 21.4 us
    all_to_all x1 -> x0, blocking collectives: 40.7 us -> none  [body(): own = lax.all_to_all(send, chips, split_axis=0, concat_axis=0, tiled=True)]
    ppermute x0 -> x8, starting transfers between devices: none -> 39.6 us  [the longest x7 34.8 us: shift(): return lax.ppermute(x, 'z', [(i, (i + k) % ZS) for i in range(ZS)])]
    all_to_all x1, waiting for transfers between devices: 30.6 us -> 10.8 us  [body(): back = lax.all_to_all(ready, chips, split_axis=0, concat_axis=0, tiled=True)]
    ppermute x0 -> x8, waiting for transfers between devices: none -> 11.5 us  [the longest x7 11.5 us: shift(): return lax.ppermute(x, 'z', [(i, (i + k) % ZS) for i in range(ZS)])]
    all_to_all x1, waiting for transfers between devices: 15.6 us -> 5.27 us  [body(): own = lax.all_to_all(send, chips, split_axis=0, concat_axis=0, tiled=True)]
    unnamed x21 -> x11, local copies, waits for them, and re-layouts: 8.23 us -> 0.12 us
    all_to_all x1, starting transfers between devices: 12.8 us -> 8.14 us  [body(): own = lax.all_to_all(send, chips, split_axis=0, concat_axis=0, tiled=True)]
    pallas_call x1 -> x3, Pallas kernels: 0.23 us -> 4.54 us  [the longest x1 2.63 us: body(): call(pack_kernel, [HBM] * 4, [((HEADS, 4, ROWS, HEAD), bf16)], [pltpu.VME...]
  transfers between devices with their start and end apart: 4 -> 12, of which waited for: 3 -> 6; matrix products, arithmetic and copies ran while one was open for 3% -> 0% of each run, Pallas kernels for 1% -> 15%
where the time goes in v2:
time: 112 us; the launch traced here: 111 us
  starting transfers between devices  57.3 us (51%)
  waiting for transfers between devices  30.2 us (27%)
  Pallas kernels  21.4 us (19%)
  between operations  1.53 us (1%)
    ppermute x7, starting transfers between devices, shift(): return lax.ppermute(x, 'z', [(i, (i + k) % ZS) for i in range(ZS)])  34.8 us
    pallas_call x1, Pallas kernels, body(): call(attention_kernel, [SM, VM, VM], [((2, NQ, HEAD), bf16), part, part],...  14.3 us
    ppermute x7, waiting for transfers between devices, shift(): return lax.ppermute(x, 'z', [(i, (i + k) % ZS) for i in range(ZS)])  11.5 us
    all_to_all x1, waiting for transfers between devices, body(): back = lax.all_to_all(ready, chips, split_axis=0, concat_axis=0, tiled=True)  10.8 us
    all_to_all x1, starting transfers between devices, body(): own = lax.all_to_all(send, chips, split_axis=0, concat_axis=0, tiled=True)  8.14 us
    all_to_all x1, waiting for transfers between devices, body(): own = lax.all_to_all(send, chips, split_axis=0, concat_axis=0, tiled=True)  5.27 us
    ppermute x1, starting transfers between devices, body(): lax.ppermute(jnp.stack([p[1] for p in near + pieces[EARLY:]]), 'yh', swap)  4.8 us
    all_to_all x1, starting transfers between devices, body(): back = lax.all_to_all(ready, chips, split_axis=0, concat_axis=0, tiled=True)  3.72 us
  transfers between devices with their start and end apart: 12, of which 6 were waited for; matrix products, arithmetic and copies ran while one was open for 0% of the time, Pallas kernels for 15%

profile of v2, /device:TPU:1, one launch (start us, length us, event | category | flops | bytes accessed | tf_op | source)
XLA Modules:
  0.0 110.9 jit_solution(13785507860932033344)
XLA Ops:
  0.6 2.6 %pack.1 = bf16[16,4,80,128]{3,2,1,0:T(8,128)(2,1)} custom-call(bf16[3,16,2048]{2,1,0:T(8,128)(2,1)} %bitcast.30, bf16[3,64,2048]{2,1,0:T(8,128)(2,1)} %bitcast.29, bf16[16,2048]{1,0:T(8,128)(2,1)} %bitcast.31, bf16[64,2048]{1,0:T(8,128)(2,1)} %bitcast.24), custom_call_target="tpu_custom_call" | custom-call | tf_op jit(solution)/shard_map/pack/pallas_call | solution.py:212
  3.3 0.0 copy-start
  3.3 0.0 copy-start.1
  3.3 0.0 copy-start.2
  3.3 8.1 %all-to-all-start = ((bf16[16,4,80,128]{3,2,1,0:T(8,128)(2,1)}), bf16[16,4,80,128]{3,2,1,0:T(8,128)(2,1)S(1)}, u32[]{:S(2)}, u32[]{:S(2)}) async-start(bf16[16,4,80,128]{3,2,1,0:T(8,128)(2,1)} %pack.1), calls=%async_computation | async-start | bytes 2621440 | tf_op jit(solution)/shard_map/all_to_all | solution.py:227
  12.1 0.1 pad_add_fusion.info
  12.2 0.0 copy-done
  12.2 0.0 copy-done.1
  12.2 0.0 copy-done.2
  12.2 0.6 control_pack.1
  12.8 4.0 %collective-permute-start = (bf16[2,2,4,2048]{3,2,1,0:T(4,128)(2,1)S(1)}, bf16[2,2,4,2048]{3,2,1,0:T(4,128)(2,1)S(1)}, u32[]{:S(2)}, u32[]{:S(2)}) collective-permute-start(bf16[2,2,4,2048]{3,2,1,0:T(4,128)(2,1)S(1)} %get-tuple-element.39), channel_id=1, source_target_pairs={{0,32},{32,64},{64,96},{96,128},{128,160},{160,192},{192,224},{224... | collective-permute-start | bytes 196616 | tf_op jit(solution)/shard_map/ppermute | solution.py:239
  16.8 5.8 %collective-permute-start.1 = (bf16[2,2,4,2048]{3,2,1,0:T(4,128)(2,1)S(1)}, bf16[2,2,4,2048]{3,2,1,0:T(4,128)(2,1)S(1)}, u32[]{:S(2)}, u32[]{:S(2)}) collective-permute-start(bf16[2,2,4,2048]{3,2,1,0:T(4,128)(2,1)S(1)} %get-tuple-element.40), channel_id=1, source_target_pairs={{0,64},{32,96},{64,128},{96,160},{128,192},{160,224},{192,0},{224,... | collective-permute-start | bytes 196616 | tf_op jit(solution)/shard_map/ppermute | solution.py:239
  22.6 7.0 %collective-permute-start.2 = (bf16[2,2,4,2048]{3,2,1,0:T(4,128)(2,1)S(1)}, bf16[2,2,4,2048]{3,2,1,0:T(4,128)(2,1)S(1)}, u32[]{:S(2)}, u32[]{:S(2)}) collective-permute-start(bf16[2,2,4,2048]{3,2,1,0:T(4,128)(2,1)S(1)} %get-tuple-element.41), channel_id=1, source_target_pairs={{0,96},{32,128},{64,160},{96,192},{128,224},{160,0},{192,32},{224,... | collective-permute-start | bytes 196616 | tf_op jit(solution)/shard_map/ppermute | solution.py:239
  29.7 2.8 %collective-permute-start.3 = (bf16[2,2,4,2048]{3,2,1,0:T(4,128)(2,1)S(1)}, bf16[2,2,4,2048]{3,2,1,0:T(4,128)(2,1)S(1)}, u32[]{:S(2)}, u32[]{:S(2)}) collective-permute-start(bf16[2,2,4,2048]{3,2,1,0:T(4,128)(2,1)S(1)} %get-tuple-element.42), channel_id=1, source_target_pairs={{0,128},{32,160},{64,192},{96,224},{128,0},{160,32},{192,64},{224,... | collective-permute-start | bytes 196616 | tf_op jit(solution)/shard_map/ppermute | solution.py:239
  32.5 0.0 collective-permute-done.refs_1_
  32.5 0.0 collective-permute-done.1.refs_2_
  32.5 0.0 collective-permute-done.2.refs_3_
  32.6 6.2 %collective-permute-done.3.refs_4_ = bf16[2,2,4,2048]{3,2,1,0:T(4,128)(2,1)S(1)} collective-permute-done((bf16[2,2,4,2048]{3,2,1,0:T(4,128)(2,1)S(1)}, bf16[2,2,4,2048]{3,2,1,0:T(4,128)(2,1)S(1)}, u32[]{:S(2)}, u32[]{:S(2)}) %collective-permute-start.3) | collective-permute-done | bytes 65568 | tf_op jit(solution)/shard_map/ppermute | solution.py:239
  38.7 5.3 %all-to-all-done.own = bf16[16,4,80,128]{3,2,1,0:T(8,128)(2,1)S(1)} async-done(((bf16[16,4,80,128]{3,2,1,0:T(8,128)(2,1)}), bf16[16,4,80,128]{3,2,1,0:T(8,128)(2,1)S(1)}, u32[]{:S(2)}, u32[]{:S(2)}) %all-to-all-start) | async-done | bytes 1310752 | tf_op jit(solution)/shard_map/all_to_all | solution.py:227
  44.0 3.7 %collective-permute-start.4 = (bf16[16,4,80,128]{3,2,1,0:T(8,128)(2,1)S(1)}, bf16[16,4,80,128]{3,2,1,0:T(8,128)(2,1)S(1)}, u32[]{:S(2)}, u32[]{:S(2)}) collective-permute-start(bf16[16,4,80,128]{3,2,1,0:T(8,128)(2,1)S(1)} %all-to-all-done.own), channel_id=1, source_target_pairs={{0,1},{1,0},{2,3},{3,2},{4,5},{5,4},{6,7},{7,6},{8,9},{9,8},{10,11... | collective-permute-start | bytes 3932168 | tf_op jit(solution)/shard_map/ppermute | solution.py:244
  47.9 4.8 %collective-permute-start.5 = (bf16[8,2,4,2048]{3,2,1,0:T(4,128)(2,1)S(1)}, bf16[8,2,4,2048]{3,2,1,0:T(4,128)(2,1)S(1)}, u32[]{:S(2)}, u32[]{:S(2)}) collective-permute-start(bf16[8,2,4,2048]{3,2,1,0:T(4,128)(2,1)S(1)} %get-tuple-element.76), channel_id=1, source_target_pairs={{0,256},{256,0},{1,257},{257,1},{2,258},{258,2},{3,259},{259,3},{4... | collective-permute-start | bytes 786440 | tf_op jit(solution)/shard_map/ppermute | solution.py:245
  52.7 0.0 collective-permute-done.4.oth
  52.7 14.3 %attention.1 = (bf16[2,1280,128]{2,1,0:T(8,128)(2,1)S(1)}, f32[16,2,80,128]{3,2,1,0:T(8,128)S(1)}, f32[16,2,80,128]{3,2,1,0:T(8,128)S(1)}) custom-call(s32[4]{0:T(128)S(1)} %pad_add_fusion.info, bf16[16,4,80,128]{3,2,1,0:T(8,128)(2,1)S(1)} %all-to-all-done.own, bf16[16,4,80,128]{3,2,1,0:T(8,128)(2,1)S(1)} %collective-permute-done.4.oth), custom_call_target="tpu_custom_call" | custom-call | flops 5872025600 | bytes 8388608 | tf_op jit(solution)/shard_map/attention/pallas_call | solution.py:247
  67.0 0.0 collective-permute-done.5.refs_5_
  67.0 2.2 %collective-permute-start.6 = (f32[16,2,80,128]{3,2,1,0:T(8,128)S(1)}, f32[16,2,80,128]{3,2,1,0:T(8,128)S(1)}, u32[]{:S(2)}, u32[]{:S(2)}) collective-permute-start(f32[16,2,80,128]{3,2,1,0:T(8,128)S(1)} %get-tuple-element.55), channel_id=1, source_target_pairs={{0,1},{1,0},{2,3},{3,2},{4,5},{5,4},{6,7},{7,6},{8,9},{9,8},{10,11... | collective-permute-start | bytes 3932168 | tf_op jit(solution)/shard_map/ppermute | solution.py:269
  69.3 0.1 pad_maximum_fusion
  69.4 2.5 %collective-permute-done.6.theirs = f32[16,2,80,128]{3,2,1,0:T(8,128)S(1)} collective-permute-done((f32[16,2,80,128]{3,2,1,0:T(8,128)S(1)}, f32[16,2,80,128]{3,2,1,0:T(8,128)S(1)}, u32[]{:S(2)}, u32[]{:S(2)}) %collective-permute-start.6) | collective-permute-done | bytes 1310752 | tf_op jit(solution)/shard_map/ppermute | solution.py:269
  71.9 1.3 %combine.1 = bf16[16,4,80,128]{3,2,1,0:T(8,128)(2,1)} custom-call(bf16[2,1280,128]{2,1,0:T(8,128)(2,1)S(1)} %get-tuple-element.44.aq, f32[16,2,80,128]{3,2,1,0:T(8,128)S(1)} %get-tuple-element.45.mine, f32[16,2,80,128]{3,2,1,0:T(8,128)S(1)} %collective-permute-done.6.theirs), custom_call_target="tpu_custom_call" | custom-call | tf_op jit(solution)/shard_map/combine/pallas_call | solution.py:270
  73.2 3.7 %all-to-all-start.1 = ((bf16[16,4,80,128]{3,2,1,0:T(8,128)(2,1)}), bf16[16,4,80,128]{3,2,1,0:T(8,128)(2,1)S(1)}, u32[]{:S(2)}, u32[]{:S(2)}) async-start(bf16[16,4,80,128]{3,2,1,0:T(8,128)(2,1)} %combine.1), calls=%async_computation.1 | async-start | bytes 2621440 | tf_op jit(solution)/shard_map/all_to_all | solution.py:276
  76.9 11.0 %collective-permute-start.7 = (bf16[2,2,4,2048]{3,2,1,0:T(4,128)(2,1)S(1)}, bf16[2,2,4,2048]{3,2,1,0:T(4,128)(2,1)S(1)}, u32[]{:S(2)}, u32[]{:S(2)}) collective-permute-start(bf16[2,2,4,2048]{3,2,1,0:T(4,128)(2,1)S(1)} %get-tuple-element.58), channel_id=1, source_target_pairs={{0,160},{32,192},{64,224},{96,0},{128,32},{160,64},{192,96},{224,1... | collective-permute-start | bytes 196616 | tf_op jit(solution)/shard_map/ppermute | solution.py:239
  88.0 1.9 %collective-permute-start.8 = (bf16[2,2,4,2048]{3,2,1,0:T(4,128)(2,1)S(1)}, bf16[2,2,4,2048]{3,2,1,0:T(4,128)(2,1)S(1)}, u32[]{:S(2)}, u32[]{:S(2)}) collective-permute-start(bf16[2,2,4,2048]{3,2,1,0:T(4,128)(2,1)S(1)} %get-tuple-element.59), channel_id=1, source_target_pairs={{0,192},{32,224},{64,0},{96,32},{128,64},{160,96},{192,128},{224,1... | collective-permute-start | bytes 196616 | tf_op jit(solution)/shard_map/ppermute | solution.py:239
  89.9 2.2 %collective-permute-start.9 = (bf16[2,2,4,2048]{3,2,1,0:T(4,128)(2,1)S(1)}, bf16[2,2,4,2048]{3,2,1,0:T(4,128)(2,1)S(1)}, u32[]{:S(2)}, u32[]{:S(2)}) collective-permute-start(bf16[2,2,4,2048]{3,2,1,0:T(4,128)(2,1)S(1)} %pad_maximum_fusion.2), channel_id=1, source_target_pairs={{0,224},{32,0},{64,32},{96,64},{128,96},{160,128},{192,160},{224,1... | collective-permute-start | bytes 196616 | tf_op jit(solution)/shard_map/ppermute | solution.py:239
  92.1 0.0 collective-permute-done.7.refs_6_
  92.1 2.8 %collective-permute-done.8.refs_7_ = bf16[2,2,4,2048]{3,2,1,0:T(4,128)(2,1)S(1)} collective-permute-done((bf16[2,2,4,2048]{3,2,1,0:T(4,128)(2,1)S(1)}, bf16[2,2,4,2048]{3,2,1,0:T(4,128)(2,1)S(1)}, u32[]{:S(2)}, u32[]{:S(2)}) %collective-permute-start.8) | collective-permute-done | bytes 65568 | tf_op jit(solution)/shard_map/ppermute | solution.py:239
  94.9 2.6 %collective-permute-done.9.refs_8_ = bf16[2,2,4,2048]{3,2,1,0:T(4,128)(2,1)S(1)} collective-permute-done((bf16[2,2,4,2048]{3,2,1,0:T(4,128)(2,1)S(1)}, bf16[2,2,4,2048]{3,2,1,0:T(4,128)(2,1)S(1)}, u32[]{:S(2)}, u32[]{:S(2)}) %collective-permute-start.9) | collective-permute-done | bytes 65568 | tf_op jit(solution)/shard_map/ppermute | solution.py:239
  97.5 1.3 %control_unpack.1 = (bf16[16,4,2048]{2,1,0:T(4,128)(2,1)}, bf16[64,2048]{1,0:T(8,128)(2,1)S(1)}) custom-call(s32[4]{0:T(128)S(1)} %pad_add_fusion.info, bf16[2,2,4,2048]{3,2,1,0:T(4,128)(2,1)S(1)} %get-tuple-element.47.refs_0_, bf16[2,2,4,2048]{3,2,1,0:T(4,128)(2,1)S(1)} %collective-permute-done.refs_1_, ...), custom_call_target="tpu_custom_call" | custom-call | tf_op jit(solution)/shard_map/control_unpack/pallas_call | solution.py:277
  98.7 10.8 %all-to-all-done.1.back = bf16[16,4,80,128]{3,2,1,0:T(8,128)(2,1)S(1)} async-done(((bf16[16,4,80,128]{3,2,1,0:T(8,128)(2,1)}), bf16[16,4,80,128]{3,2,1,0:T(8,128)(2,1)S(1)}, u32[]{:S(2)}, u32[]{:S(2)}) %all-to-all-start.1) | async-done | bytes 1310752 | tf_op jit(solution)/shard_map/all_to_all | solution.py:276
  109.6 1.4 %unpack.1 = (bf16[16,2048]{1,0:T(8,128)(2,1)}, bf16[64,2048]{1,0:T(8,128)(2,1)}, bf16[3,16,2048]{2,1,0:T(8,128)(2,1)}, bf16[3,64,2048]{2,1,0:T(8,128)(2,1)}) custom-call(bf16[16,4,80,128]{3,2,1,0:T(8,128)(2,1)S(1)} %all-to-all-done.1.back, bf16[64,2048]{1,0:T(8,128)(2,1)S(1)} %get-tuple-element.61.residual, f32[1,2048]{1,0:T(1,128)S(1)} %bitcast.28), custom_call_target="tpu_custom_call" | custom-call | tf_op jit(solution)/shard_map/unpack/pallas_call | solution.py:284
  (10 shorter events, 0.3 us)
Async XLA Ops:
  3.3 8.9 %copy-start = (bf16[1,64,2048]{2,1,0:T(8,128)(2,1)S(1)}, bf16[1,64,2048]{2,1,0:T(8,128)(2,1)}, u32[]{:S(2)}) copy-start(bf16[1,64,2048]{2,1,0:T(8,128)(2,1)} %param.10) | copy-start | bytes 786436
  3.3 8.9 %copy-start.1 = (bf16[16,1,4,2048]{3,2,1,0:T(4,128)(2,1)S(1)}, bf16[16,1,4,2048]{3,2,1,0:T(4,128)(2,1)}, u32[]{:S(2)}) copy-start(bf16[16,1,4,2048]{3,2,1,0:T(4,128)(2,1)} %param.11) | copy-start | bytes 786436
  3.3 8.9 %copy-start.2 = (f32[2048]{0:T(1024)S(1)}, f32[2048]{0:T(1024)}, u32[]{:S(2)}) copy-start(f32[2048]{0:T(1024)} %param.12) | copy-start | bytes 24580
  3.3 40.7 %all-to-all-start = ((bf16[16,4,80,128]{3,2,1,0:T(8,128)(2,1)}), bf16[16,4,80,128]{3,2,1,0:T(8,128)(2,1)S(1)}, u32[]{:S(2)}, u32[]{:S(2)}) async-start(bf16[16,4,80,128]{3,2,1,0:T(8,128)(2,1)} %pack.1), calls=%async_computation | async-start | bytes 2621440 | tf_op jit(solution)/shard_map/all_to_all | solution.py:227
  12.8 19.7 %collective-permute-start = (bf16[2,2,4,2048]{3,2,1,0:T(4,128)(2,1)S(1)}, bf16[2,2,4,2048]{3,2,1,0:T(4,128)(2,1)S(1)}, u32[]{:S(2)}, u32[]{:S(2)}) collective-permute-start(bf16[2,2,4,2048]{3,2,1,0:T(4,128)(2,1)S(1)} %get-tuple-element.39), channel_id=1, source_target_pairs={{0,32},{32,64},{64,96},{96,128},{128,160},{160,192},{192,224},{224... | collective-permute-start | bytes 196616 | tf_op jit(solution)/shard_map/ppermute | solution.py:239
  16.8 15.7 %collective-permute-start.1 = (bf16[2,2,4,2048]{3,2,1,0:T(4,128)(2,1)S(1)}, bf16[2,2,4,2048]{3,2,1,0:T(4,128)(2,1)S(1)}, u32[]{:S(2)}, u32[]{:S(2)}) collective-permute-start(bf16[2,2,4,2048]{3,2,1,0:T(4,128)(2,1)S(1)} %get-tuple-element.40), channel_id=1, source_target_pairs={{0,64},{32,96},{64,128},{96,160},{128,192},{160,224},{192,0},{224,... | collective-permute-start | bytes 196616 | tf_op jit(solution)/shard_map/ppermute | solution.py:239
  22.6 9.9 %collective-permute-start.2 = (bf16[2,2,4,2048]{3,2,1,0:T(4,128)(2,1)S(1)}, bf16[2,2,4,2048]{3,2,1,0:T(4,128)(2,1)S(1)}, u32[]{:S(2)}, u32[]{:S(2)}) collective-permute-start(bf16[2,2,4,2048]{3,2,1,0:T(4,128)(2,1)S(1)} %get-tuple-element.41), channel_id=1, source_target_pairs={{0,96},{32,128},{64,160},{96,192},{128,224},{160,0},{192,32},{224,... | collective-permute-start | bytes 196616 | tf_op jit(solution)/shard_map/ppermute | solution.py:239
  29.7 9.0 %collective-permute-start.3 = (bf16[2,2,4,2048]{3,2,1,0:T(4,128)(2,1)S(1)}, bf16[2,2,4,2048]{3,2,1,0:T(4,128)(2,1)S(1)}, u32[]{:S(2)}, u32[]{:S(2)}) collective-permute-start(bf16[2,2,4,2048]{3,2,1,0:T(4,128)(2,1)S(1)} %get-tuple-element.42), channel_id=1, source_target_pairs={{0,128},{32,160},{64,192},{96,224},{128,0},{160,32},{192,64},{224,... | collective-permute-start | bytes 196616 | tf_op jit(solution)/shard_map/ppermute | solution.py:239
  44.0 8.7 %collective-permute-start.4 = (bf16[16,4,80,128]{3,2,1,0:T(8,128)(2,1)S(1)}, bf16[16,4,80,128]{3,2,1,0:T(8,128)(2,1)S(1)}, u32[]{:S(2)}, u32[]{:S(2)}) collective-permute-start(bf16[16,4,80,128]{3,2,1,0:T(8,128)(2,1)S(1)} %all-to-all-done.own), channel_id=1, source_target_pairs={{0,1},{1,0},{2,3},{3,2},{4,5},{5,4},{6,7},{7,6},{8,9},{9,8},{10,11... | collective-permute-start | bytes 3932168 | tf_op jit(solution)/shard_map/ppermute | solution.py:244
  47.9 19.1 %collective-permute-start.5 = (bf16[8,2,4,2048]{3,2,1,0:T(4,128)(2,1)S(1)}, bf16[8,2,4,2048]{3,2,1,0:T(4,128)(2,1)S(1)}, u32[]{:S(2)}, u32[]{:S(2)}) collective-permute-start(bf16[8,2,4,2048]{3,2,1,0:T(4,128)(2,1)S(1)} %get-tuple-element.76), channel_id=1, source_target_pairs={{0,256},{256,0},{1,257},{257,1},{2,258},{258,2},{3,259},{259,3},{4... | collective-permute-start | bytes 786440 | tf_op jit(solution)/shard_map/ppermute | solution.py:245
  67.0 4.9 %collective-permute-start.6 = (f32[16,2,80,128]{3,2,1,0:T(8,128)S(1)}, f32[16,2,80,128]{3,2,1,0:T(8,128)S(1)}, u32[]{:S(2)}, u32[]{:S(2)}) collective-permute-start(f32[16,2,80,128]{3,2,1,0:T(8,128)S(1)} %get-tuple-element.55), channel_id=1, source_target_pairs={{0,1},{1,0},{2,3},{3,2},{4,5},{5,4},{6,7},{7,6},{8,9},{9,8},{10,11... | collective-permute-start | bytes 3932168 | tf_op jit(solution)/shard_map/ppermute | solution.py:269
  73.2 36.4 %all-to-all-start.1 = ((bf16[16,4,80,128]{3,2,1,0:T(8,128)(2,1)}), bf16[16,4,80,128]{3,2,1,0:T(8,128)(2,1)S(1)}, u32[]{:S(2)}, u32[]{:S(2)}) async-start(bf16[16,4,80,128]{3,2,1,0:T(8,128)(2,1)} %combine.1), calls=%async_computation.1 | async-start | bytes 2621440 | tf_op jit(solution)/shard_map/all_to_all | solution.py:276
  76.9 15.2 %collective-permute-start.7 = (bf16[2,2,4,2048]{3,2,1,0:T(4,128)(2,1)S(1)}, bf16[2,2,4,2048]{3,2,1,0:T(4,128)(2,1)S(1)}, u32[]{:S(2)}, u32[]{:S(2)}) collective-permute-start(bf16[2,2,4,2048]{3,2,1,0:T(4,128)(2,1)S(1)} %get-tuple-element.58), channel_id=1, source_target_pairs={{0,160},{32,192},{64,224},{96,0},{128,32},{160,64},{192,96},{224,1... | collective-permute-start | bytes 196616 | tf_op jit(solution)/shard_map/ppermute | solution.py:239
  88.0 6.9 %collective-permute-start.8 = (bf16[2,2,4,2048]{3,2,1,0:T(4,128)(2,1)S(1)}, bf16[2,2,4,2048]{3,2,1,0:T(4,128)(2,1)S(1)}, u32[]{:S(2)}, u32[]{:S(2)}) collective-permute-start(bf16[2,2,4,2048]{3,2,1,0:T(4,128)(2,1)S(1)} %get-tuple-element.59), channel_id=1, source_target_pairs={{0,192},{32,224},{64,0},{96,32},{128,64},{160,96},{192,128},{224,1... | collective-permute-start | bytes 196616 | tf_op jit(solution)/shard_map/ppermute | solution.py:239
  89.9 7.6 %collective-permute-start.9 = (bf16[2,2,4,2048]{3,2,1,0:T(4,128)(2,1)S(1)}, bf16[2,2,4,2048]{3,2,1,0:T(4,128)(2,1)S(1)}, u32[]{:S(2)}, u32[]{:S(2)}) collective-permute-start(bf16[2,2,4,2048]{3,2,1,0:T(4,128)(2,1)S(1)} %pad_maximum_fusion.2), channel_id=1, source_target_pairs={{0,224},{32,0},{64,32},{96,64},{128,96},{160,128},{192,160},{224,1... | collective-permute-start | bytes 196616 | tf_op jit(solution)/shard_map/ppermute | solution.py:239

commit v3 on v2

v3 whole, which is shorter than its diff:
```python
import functools
import math

import jax
import jax.numpy as jnp
from jax import lax
from jax.experimental import pallas as pl
from jax.experimental.pallas import tpu as pltpu
from jax.sharding import Mesh, PartitionSpec as P

HEAD = 128
HEADS = 16
TXT = 16
IMG = 64
ROWS = TXT + IMG
ZS = 8
EARLY = 5
CHIPS = 16
SCALE = 1.0 / math.sqrt(HEAD)
SCALE2 = SCALE * math.log2(math.e)
BQ = 256
NQ = CHIPS * ROWS
NK = 2 * NQ
HALF_TXT = CHIPS * TXT

VM = pl.BlockSpec(memory_space=pltpu.VMEM)
SM = pl.BlockSpec(memory_space=pltpu.SMEM)
ANY = pl.BlockSpec(memory_space=pl.ANY)
HBM = pl.BlockSpec(memory_space=pltpu.HBM)


def dot(a, b):
    return lax.dot_general(a, b, (((1,), (0,)), ((), ())), preferred_element_type=jnp.float32)


def dot_t(a, b):
    return lax.dot_general(a, b, (((1,), (1,)), ((), ())), preferred_element_type=jnp.float32)


def pack_kernel(th, ih, tc, ic, out, th_s, ih_s, tc_s, ic_s, out_s, in_sems, out_sems):
    pairs = [(ih.at[t], ih_s.at[t], th.at[t], th_s.at[t]) for t in range(3)]
    pairs.append((ic, ic_s, tc, tc_s))
    copies = []
    for n, (a, b, c, d) in enumerate(pairs):
        copies.append(
            (
                pltpu.make_async_copy(a, b, in_sems.at[n, 0]),
                pltpu.make_async_copy(c, d, in_sems.at[n, 1]),
            )
        )
    for image, text in copies:
        image.start()
        text.start()
    leaving = []
    for t, (image, text) in enumerate(copies):
        image.wait()
        text.wait()
        for h in range(HEADS):
            cols = slice(h * HEAD, (h + 1) * HEAD)
            out_s[t, h, :TXT, :] = th_s[t, :, cols] if t < 3 else tc_s[:, cols]
            out_s[t, h, TXT:, :] = ih_s[t, :, cols] if t < 3 else ic_s[:, cols]
        leaving.append(pltpu.make_async_copy(out_s.at[t], out.at[:, t], out_sems.at[t]))
        leaving[-1].start()
    for copy in leaving:
        copy.wait()


def control_pack_kernel(info, residual, ic, gain, *refs):
    outs, scaled = refs[:ZS], refs[ZS]
    yh, z = info[2], info[3]
    for r in range(IMG // 16):
        x = ic[r * 16 : (r + 1) * 16, :].astype(jnp.float32) * gain[0:1, :]
        for i in range(4):
            scaled[r * 4 + i] = x[i * 4 : (i + 1) * 4].astype(jnp.bfloat16)
    for k in range(ZS):
        for rel in range(2):
            g = (yh if rel == 0 else 1 - yh) * ZS + lax.rem(z + k, ZS)
            outs[k][rel, 0] = residual[g]
            outs[k][rel, 1] = scaled[g]


def control_unpack_kernel(info, *refs):
    near, far, late = refs[:EARLY], refs[EARLY], refs[EARLY + 1 : ZS + 1]
    grads, arrived, rows = refs[ZS + 1 :]
    yh, z = info[2], info[3]
    for k in range(ZS):
        for rel in range(2):
            g = (yh if rel == 0 else 1 - yh) * ZS + lax.rem(z + ZS - k, ZS)
            if k >= EARLY:
                src = late[k - EARLY].at[rel]
            else:
                src = near[k].at[0] if rel == 0 else far.at[k]
            rows[g] = src[0]
            grads[g] = src[1]
    for r in range(IMG // 16):
        part = [rows[r * 4 + i].astype(jnp.float32) for i in range(4)]
        arrived[r * 16 : (r + 1) * 16, :] = jnp.concatenate(part, axis=0).astype(jnp.bfloat16)


def attention_kernel(
    info, own, oth, part, give, e_own, ds_own, qgt, q_s, g_s, k_s, v_s, s_s, e_oth, ds_oth, mask_s
):
    length = info[0]
    core = info[1]
    for s in range(CHIPS):
        q_s[s * ROWS : (s + 1) * ROWS, :] = own[s, 0]
        g_s[s * ROWS : (s + 1) * ROWS, :] = own[s, 3]
        for h, src in ((0, own), (1, oth)):
            for t, dst in ((1, k_s), (2, v_s)):
                at = h * NQ + s * TXT
                dst[at : at + TXT, :] = src[s, t, :TXT, :]
                at = h * NQ + HALF_TXT + s * IMG
                dst[at : at + IMG, :] = src[s, t, TXT:, :]
    pos = lax.broadcasted_iota(jnp.int32, (8, HALF_TXT), 1)
    for h in range(2):
        first = (core if h == 0 else 1 - core) * TXT
        token = (pos // TXT) * (2 * TXT) + first + pos % TXT
        mask_s[h] = jnp.where(token < length, 0.0, -jnp.inf)

    def place(i, t, x):
        at, end = i * BQ, (i + 1) * BQ
        while at < end:
            s, r = divmod(at, ROWS)
            n = min(ROWS - r, end - at)
            part[s, t, r : r + n, :] = x[at - i * BQ : at - i * BQ + n]
            at += n

    def block(i):
        rows = slice(i * BQ, (i + 1) * BQ)
        q = q_s[rows, :]
        g = g_s[rows, :]
        top = None
        for h in range(2):
            s = dot_t(q, k_s[h * NQ : (h + 1) * NQ, :])
            text = s[:, :HALF_TXT] + mask_s[h, 0:1, :]
            s_s[:, h * NQ : h * NQ + HALF_TXT] = text
            s_s[:, h * NQ + HALF_TXT : (h + 1) * NQ] = s[:, HALF_TXT:]
            for t in range(NQ // 128):
                x = (text if t < HALF_TXT // 128 else s)[:, t * 128 : (t + 1) * 128]
                top = x if top is None else jnp.maximum(top, x)
        row_max = jnp.max(top, axis=1, keepdims=True)
        a = total = None
        for h, dst in ((0, e_own), (1, e_oth)):
            cols = slice(h * NQ, (h + 1) * NQ)
            e = jnp.exp2((s_s[:, cols] - row_max) * SCALE2)
            for t in range(NQ // 128):
                x = e[:, t * 128 : (t + 1) * 128]
                total = x if total is None else total + x
            e = e.astype(jnp.bfloat16)
            dst[rows, :] = e
            x = dot(e, v_s[cols, :])
            a = x if a is None else a + x
        inv = 1.0 / jnp.sum(total, axis=1, keepdims=True)
        ab = (a * inv).astype(jnp.bfloat16)
        gs = (g.astype(jnp.float32) * inv).astype(jnp.bfloat16)
        delta = jnp.sum(gs.astype(jnp.float32) * ab.astype(jnp.float32), axis=1, keepdims=True)
        place(i, 0, ab)
        qgt[0, :, rows] = q.T
        qgt[1, :, rows] = gs.T
        dq = None
        for h, src, dst in ((0, e_own, ds_own), (1, e_oth, ds_oth)):
            cols = slice(h * NQ, (h + 1) * NQ)
            dp = dot_t(gs, v_s[cols, :]) - delta
            ds = src[rows, :] * dp.astype(jnp.bfloat16)
            dst[rows, :] = ds
            x = dot(ds, k_s[cols, :])
            dq = x if dq is None else dq + x
        place(i, 1, (dq * SCALE).astype(jnp.bfloat16))

    for i in range(NQ // BQ):
        block(i)
    give[0] = (dot(qgt[0], ds_oth[...]) * SCALE).astype(jnp.bfloat16)
    give[1] = dot(qgt[1], e_oth[...]).astype(jnp.bfloat16)


def key_grad_kernel(qgt, e_own, ds_own, mine):
    mine[0] = dot(qgt[0], ds_own[...]) * SCALE
    mine[1] = dot(qgt[1], e_own[...])


def combine_kernel(part, mine, theirs, out, x_s, sems):
    del part
    copies = []
    for t in range(2):
        x = (mine[t] + theirs[t].astype(jnp.float32)).astype(jnp.bfloat16).T
        for s in range(CHIPS):
            x_s[t, s, :TXT, :] = x[s * TXT : (s + 1) * TXT]
            x_s[t, s, TXT:, :] = x[HALF_TXT + s * IMG : HALF_TXT + (s + 1) * IMG]
        copies.append(pltpu.make_async_copy(x_s.at[t], out.at[:, 2 + t], sems.at[t]))
        copies[-1].start()
    for copy in copies:
        copy.wait()


def unpack_kernel(back, residual, gain, ta, io, tg, ig, ta_s, io_s, tg_s, ig_s, sems):
    copies = []

    def send(a, b):
        copies.append(pltpu.make_async_copy(a, b, sems.at[len(copies)]))
        copies[-1].start()

    for t in range(3):
        for h in range(HEADS):
            cols = slice(h * HEAD, (h + 1) * HEAD)
            tg_s[t, :, cols] = back[h, 1 + t, :TXT, :]
            ig_s[t, :, cols] = back[h, 1 + t, TXT:, :]
        send(ig_s.at[t], ig.at[t])
        send(tg_s.at[t], tg.at[t])
    for h in range(HEADS):
        cols = slice(h * HEAD, (h + 1) * HEAD)
        ta_s[:, cols] = back[h, 0, :TXT, :]
        io_s[:, cols] = (
            back[h, 0, TXT:, :].astype(jnp.float32)
            + gain[0:1, cols] * residual[:, cols].astype(jnp.float32)
        ).astype(jnp.bfloat16)
    send(io_s, io)
    send(ta_s, ta)
    for copy in copies:
        copy.wait()


def call(kernel, ins, outs, scratch=(), vmem=8, out_place=VM, **kw):
    return pl.pallas_call(
        kernel,
        in_specs=ins,
        out_specs=[out_place] * len(outs) if len(outs) > 1 else out_place,
        out_shape=[jax.ShapeDtypeStruct(s, d) for s, d in outs]
        if len(outs) > 1
        else jax.ShapeDtypeStruct(*outs[0]),
        scratch_shapes=scratch,
        compiler_params=pltpu.CompilerParams(vmem_limit_bytes=vmem << 20),
        **kw,
    )


def body(th, ih, tc, ic, residual, gain, lengths):
    bf16, f32 = jnp.bfloat16, jnp.float32
    chips = ("x", "yl")
    grp = ("yh", "z")
    width = HEADS * HEAD
    core = lax.axis_index("core")
    index = [core, lax.axis_index("yh"), lax.axis_index("z")]
    info = jnp.stack([lengths[0]] + [i.astype(jnp.int32) for i in index])
    send = call(
        pack_kernel,
        [HBM] * 4,
        [((HEADS, 4, ROWS, HEAD), bf16)],
        out_place=HBM,
        scratch=[
            pltpu.VMEM((3, TXT, width), bf16),
            pltpu.VMEM((3, IMG, width), bf16),
            pltpu.VMEM((TXT, width), bf16),
            pltpu.VMEM((IMG, width), bf16),
            pltpu.VMEM((4, HEADS, ROWS, HEAD), bf16),
            pltpu.SemaphoreType.DMA((4, 2)),
            pltpu.SemaphoreType.DMA((4,)),
        ],
        vmem=63,
        name="pack",
    )(jnp.swapaxes(th[0], 0, 1), jnp.swapaxes(ih[0], 0, 1), tc[0], ic[0])
    send, late_ic = lax.optimization_barrier((send, ic[0]))
    own = lax.all_to_all(send, chips, split_axis=0, concat_axis=0, tiled=True)
    swap = [(0, 1), (1, 0)]
    piece = (2, 2, 4, width)
    pieces = call(
        control_pack_kernel,
        [SM] + [VM] * 3,
        [(piece, bf16)] * ZS,
        [pltpu.VMEM((16, 4, width), bf16)],
        name="control_pack",
    )(info, residual[:, 0], late_ic, gain[None, :])

    def shift(x, k):
        return lax.ppermute(x, "z", [(i, (i + k) % ZS) for i in range(ZS)])

    pieces = list(pieces)
    near = pieces[:1] + [shift(pieces[k], k) for k in range(1, EARLY)]
    own, *near = lax.optimization_barrier([own] + near)
    oth = lax.ppermute(own, "core", swap)
    far = lax.ppermute(jnp.stack([p[1] for p in near + pieces[EARLY:]]), "yh", swap)
    square = ((NQ, NQ), bf16)
    turned = ((2, HEAD, NQ), bf16)
    part, give, e_own, ds_own, qgt = call(
        attention_kernel,
        [SM, VM, VM],
        [((CHIPS, 4, ROWS, HEAD), bf16), turned, square, square, turned],
        [
            pltpu.VMEM((NQ, HEAD), bf16),
            pltpu.VMEM((NQ, HEAD), bf16),
            pltpu.VMEM((NK, HEAD), bf16),
            pltpu.VMEM((NK, HEAD), bf16),
            pltpu.VMEM((BQ, NK), f32),
            pltpu.VMEM((NQ, NQ), bf16),
            pltpu.VMEM((NQ, NQ), bf16),
            pltpu.VMEM((2, 8, HALF_TXT), f32),
        ],
        vmem=32,
        name="attention",
        cost_estimate=pl.CostEstimate(
            flops=12 * NQ * NK * HEAD, bytes_accessed=8 << 20, transcendentals=NQ * NK
        ),
    )(info, own, oth)
    theirs = lax.ppermute(give, "core", swap)
    qgt, far = lax.optimization_barrier((qgt, far))
    mine = call(key_grad_kernel, [VM] * 3, [((2, HEAD, NQ), f32)], vmem=16, name="key_grad")(
        qgt, e_own, ds_own
    )
    ready = call(
        combine_kernel,
        [ANY, VM, VM],
        [((CHIPS, 4, ROWS, HEAD), bf16)],
        out_place=ANY,
        scratch=[pltpu.VMEM((2, CHIPS, ROWS, HEAD), bf16), pltpu.SemaphoreType.DMA((2,))],
        input_output_aliases={0: 0},
        name="combine",
    )(part, mine, theirs)
    late = [jnp.stack([pieces[k][0], far[k]]) for k in range(EARLY, ZS)]
    ready, *late = lax.optimization_barrier([ready] + late)
    late = [shift(x, EARLY + n) for n, x in enumerate(late)]
    back = lax.all_to_all(ready, chips, split_axis=0, concat_axis=0, tiled=True)
    grads, arrived = call(
        control_unpack_kernel,
        [SM] + [VM] * (ZS + 1),
        [((16, 4, width), bf16), ((IMG, width), bf16)],
        [pltpu.VMEM((16, 4, width), bf16)],
        name="control_unpack",
    )(info, *near, far, *late)
    results = [((TXT, width), bf16), ((IMG, width), bf16)]
    results += [((3, TXT, width), bf16), ((3, IMG, width), bf16)]
    ta, io, tg, ig = call(
        unpack_kernel,
        [VM] * 3,
        results,
        out_place=HBM,
        scratch=[pltpu.VMEM(*r) for r in results] + [pltpu.SemaphoreType.DMA((8,))],
        name="unpack",
    )(back, arrived, gain[None, :])
    return (
        ta[None],
        io[None],
        jnp.swapaxes(tg, 0, 1)[None],
        jnp.swapaxes(ig, 0, 1)[None],
        grads[:, None],
    )


def solution(mesh):
    fine = Mesh(mesh.devices.reshape(2, 8, 4, 4, 2), ("yh", "z", "x", "yl", "core"))
    grp = ("yh", "z")
    seq = ("x", "yl", "core")
    in_specs = (
        P(grp, seq, None, None),
        P(grp, seq, None, None),
        P(grp, seq, None),
        P(grp, seq, None),
        P(None, seq, grp, None),
        P(),
        P(grp),
    )
    out_specs = (
        P(grp, seq, None),
        P(grp, seq, None),
        P(grp, seq, None, None),
        P(grp, seq, None, None),
        P(None, seq, grp, None),
    )
    return jax.shard_map(body, mesh=fine, in_specs=in_specs, out_specs=out_specs, check_vma=False)
```

time: 112 us -> 110 us (0.982)
  Pallas kernels: 21.4 us -> 18.6 us
    pallas_call x4 -> x5, Pallas kernels: 19.5 us -> 16.7 us  [the longest x1 11.3 us: body(): call(attention_kernel, [SM, VM, VM], [((CHIPS, 4, ROWS, HEAD), bf16), tur...]
    ppermute x1, waiting for transfers between devices: 0.01 us -> 2.44 us  [body(): lax.ppermute(jnp.stack([p[1] for p in near + pieces[EARLY:]]), 'yh', swap)]
    ppermute x1, waiting for transfers between devices: 2.52 us -> 0.47 us  [body(): theirs = lax.ppermute(give, 'core', swap)]
  transfers between devices with their start and end apart: 12 -> 12, of which waited for: 6 -> 7; matrix products, arithmetic and copies ran while one was open for 0% -> 0% of each run, Pallas kernels for 15% -> 13%
where the time goes in v3:
time: 110 us; the launch traced here: 109 us
  starting transfers between devices  58 us (53%)
  waiting for transfers between devices  30.6 us (28%)
  Pallas kernels  18.6 us (17%)
  between operations  1.53 us (1%)
    ppermute x7, starting transfers between devices, shift(): return lax.ppermute(x, 'z', [(i, (i + k) % ZS) for i in range(ZS)])  34.8 us
    ppermute x7, waiting for transfers between devices, shift(): return lax.ppermute(x, 'z', [(i, (i + k) % ZS) for i in range(ZS)])  11.5 us
    pallas_call x1, Pallas kernels, body(): call(attention_kernel, [SM, VM, VM], [((CHIPS, 4, ROWS, HEAD), bf16), tur...  11.3 us
    all_to_all x1, waiting for transfers between devices, body(): back = lax.all_to_all(ready, chips, split_axis=0, concat_axis=0, tiled=True)  10.8 us
    all_to_all x1, starting transfers between devices, body(): own = lax.all_to_all(send, chips, split_axis=0, concat_axis=0, tiled=True)  8.14 us
    all_to_all x1, waiting for transfers between devices, body(): own = lax.all_to_all(send, chips, split_axis=0, concat_axis=0, tiled=True)  5.27 us
    ppermute x1, starting transfers between devices, body(): lax.ppermute(jnp.stack([p[1] for p in near + pieces[EARLY:]]), 'yh', swap)  4.8 us
    all_to_all x1, starting transfers between devices, body(): back = lax.all_to_all(ready, chips, split_axis=0, concat_axis=0, tiled=True)  4.25 us
  transfers between devices with their start and end apart: 12, of which 7 were waited for; matrix products, arithmetic and copies ran while one was open for 0% of the time, Pallas kernels for 13%

profile of v3, /device:TPU:1, one launch (start us, length us, event | category | flops | bytes accessed | tf_op | source)
XLA Modules:
  0.0 109.2 jit_solution(10441886680908039860)
XLA Ops:
  0.6 2.2 %pack.1 = bf16[16,4,80,128]{3,2,1,0:T(8,128)(2,1)} custom-call(bf16[3,16,2048]{2,1,0:T(8,128)(2,1)} %bitcast.30, bf16[3,64,2048]{2,1,0:T(8,128)(2,1)} %bitcast.29, bf16[16,2048]{1,0:T(8,128)(2,1)} %bitcast.31, bf16[64,2048]{1,0:T(8,128)(2,1)} %bitcast.24), custom_call_target="tpu_custom_call" | custom-call | tf_op jit(solution)/shard_map/pack/pallas_call | solution.py:244
  2.8 0.0 copy-start
  2.9 0.0 copy-start.1
  2.9 0.0 copy-start.2
  2.9 8.1 %all-to-all-start = ((bf16[16,4,80,128]{3,2,1,0:T(8,128)(2,1)}), bf16[16,4,80,128]{3,2,1,0:T(8,128)(2,1)S(1)}, u32[]{:S(2)}, u32[]{:S(2)}) async-start(bf16[16,4,80,128]{3,2,1,0:T(8,128)(2,1)} %pack.1), calls=%async_computation | async-start | bytes 2621440 | tf_op jit(solution)/shard_map/all_to_all | solution.py:262
  11.7 0.1 pad_add_fusion.info
  11.8 0.0 copy-done
  11.8 0.0 copy-done.1
  11.8 0.0 copy-done.2
  11.8 0.6 control_pack.1
  12.4 4.0 %collective-permute-start = (bf16[2,2,4,2048]{3,2,1,0:T(4,128)(2,1)S(1)}, bf16[2,2,4,2048]{3,2,1,0:T(4,128)(2,1)S(1)}, u32[]{:S(2)}, u32[]{:S(2)}) collective-permute-start(bf16[2,2,4,2048]{3,2,1,0:T(4,128)(2,1)S(1)} %get-tuple-element.41), channel_id=1, source_target_pairs={{0,32},{32,64},{64,96},{96,128},{128,160},{160,192},{192,224},{224... | collective-permute-start | bytes 196616 | tf_op jit(solution)/shard_map/ppermute | solution.py:274
  16.4 5.8 %collective-permute-start.1 = (bf16[2,2,4,2048]{3,2,1,0:T(4,128)(2,1)S(1)}, bf16[2,2,4,2048]{3,2,1,0:T(4,128)(2,1)S(1)}, u32[]{:S(2)}, u32[]{:S(2)}) collective-permute-start(bf16[2,2,4,2048]{3,2,1,0:T(4,128)(2,1)S(1)} %get-tuple-element.42), channel_id=1, source_target_pairs={{0,64},{32,96},{64,128},{96,160},{128,192},{160,224},{192,0},{224,... | collective-permute-start | bytes 196616 | tf_op jit(solution)/shard_map/ppermute | solution.py:274
  22.2 7.0 %collective-permute-start.2 = (bf16[2,2,4,2048]{3,2,1,0:T(4,128)(2,1)S(1)}, bf16[2,2,4,2048]{3,2,1,0:T(4,128)(2,1)S(1)}, u32[]{:S(2)}, u32[]{:S(2)}) collective-permute-start(bf16[2,2,4,2048]{3,2,1,0:T(4,128)(2,1)S(1)} %get-tuple-element.43), channel_id=1, source_target_pairs={{0,96},{32,128},{64,160},{96,192},{128,224},{160,0},{192,32},{224,... | collective-permute-start | bytes 196616 | tf_op jit(solution)/shard_map/ppermute | solution.py:274
  29.3 2.8 %collective-permute-start.3 = (bf16[2,2,4,2048]{3,2,1,0:T(4,128)(2,1)S(1)}, bf16[2,2,4,2048]{3,2,1,0:T(4,128)(2,1)S(1)}, u32[]{:S(2)}, u32[]{:S(2)}) collective-permute-start(bf16[2,2,4,2048]{3,2,1,0:T(4,128)(2,1)S(1)} %get-tuple-element.44), channel_id=1, source_target_pairs={{0,128},{32,160},{64,192},{96,224},{128,0},{160,32},{192,64},{224,... | collective-permute-start | bytes 196616 | tf_op jit(solution)/shard_map/ppermute | solution.py:274
  32.1 0.0 collective-permute-done.refs_1_
  32.1 0.0 collective-permute-done.1.refs_2_
  32.1 0.0 collective-permute-done.2.refs_3_
  32.1 6.2 %collective-permute-done.3.refs_4_ = bf16[2,2,4,2048]{3,2,1,0:T(4,128)(2,1)S(1)} collective-permute-done((bf16[2,2,4,2048]{3,2,1,0:T(4,128)(2,1)S(1)}, bf16[2,2,4,2048]{3,2,1,0:T(4,128)(2,1)S(1)}, u32[]{:S(2)}, u32[]{:S(2)}) %collective-permute-start.3) | collective-permute-done | bytes 65568 | tf_op jit(solution)/shard_map/ppermute | solution.py:274
  38.3 5.3 %all-to-all-done.own = bf16[16,4,80,128]{3,2,1,0:T(8,128)(2,1)S(1)} async-done(((bf16[16,4,80,128]{3,2,1,0:T(8,128)(2,1)}), bf16[16,4,80,128]{3,2,1,0:T(8,128)(2,1)S(1)}, u32[]{:S(2)}, u32[]{:S(2)}) %all-to-all-start) | async-done | bytes 1310752 | tf_op jit(solution)/shard_map/all_to_all | solution.py:262
  43.6 3.7 %collective-permute-start.4 = (bf16[16,4,80,128]{3,2,1,0:T(8,128)(2,1)S(1)}, bf16[16,4,80,128]{3,2,1,0:T(8,128)(2,1)S(1)}, u32[]{:S(2)}, u32[]{:S(2)}) collective-permute-start(bf16[16,4,80,128]{3,2,1,0:T(8,128)(2,1)S(1)} %all-to-all-done.own), channel_id=1, source_target_pairs={{0,1},{1,0},{2,3},{3,2},{4,5},{5,4},{6,7},{7,6},{8,9},{9,8},{10,11... | collective-permute-start | bytes 3932168 | tf_op jit(solution)/shard_map/ppermute | solution.py:279
  47.5 4.8 %collective-permute-start.5 = (bf16[8,2,4,2048]{3,2,1,0:T(4,128)(2,1)S(1)}, bf16[8,2,4,2048]{3,2,1,0:T(4,128)(2,1)S(1)}, u32[]{:S(2)}, u32[]{:S(2)}) collective-permute-start(bf16[8,2,4,2048]{3,2,1,0:T(4,128)(2,1)S(1)} %get-tuple-element.80), channel_id=1, source_target_pairs={{0,256},{256,0},{1,257},{257,1},{2,258},{258,2},{3,259},{259,3},{4... | collective-permute-start | bytes 786440 | tf_op jit(solution)/shard_map/ppermute | solution.py:280
  52.3 0.0 collective-permute-done.4.oth
  52.3 11.3 %attention.1 = (bf16[16,4,80,128]{3,2,1,0:T(8,128)(2,1)}, bf16[2,128,1280]{2,1,0:T(8,128)(2,1)S(1)}, bf16[1280,1280]{1,0:T(8,128)(2,1)S(1)}, bf16[1280,1280]{1,0:T(8,128)(2,1)S(1)}, bf16[2,128,1280]{2,1,0:T(8,128)(2,1)S(1)}) custom-call(s32[4]{0:T(128)S(1)} %pad_add_fusion.info, bf16[16,4,80,128]{3,2,1,0:T(8,128)(2,1)S(1)} %all-to-all-done.own, ...), custom_call_target="tpu_custom_call" | custom-call | flops 5033164800 | bytes 8388608 | tf_op jit(solution)/shard_map/attention/pallas_call | solution.py:283
  63.6 2.4 %collective-permute-done.5.refs_5_ = bf16[8,2,4,2048]{3,2,1,0:T(4,128)(2,1)S(1)} collective-permute-done((bf16[8,2,4,2048]{3,2,1,0:T(4,128)(2,1)S(1)}, bf16[8,2,4,2048]{3,2,1,0:T(4,128)(2,1)S(1)}, u32[]{:S(2)}, u32[]{:S(2)}) %collective-permute-start.5) | collective-permute-done | bytes 262176 | tf_op jit(solution)/shard_map/ppermute | solution.py:280
  66.0 2.3 %collective-permute-start.6 = (bf16[2,128,1280]{2,1,0:T(8,128)(2,1)S(1)}, bf16[2,128,1280]{2,1,0:T(8,128)(2,1)S(1)}, u32[]{:S(2)}, u32[]{:S(2)}) collective-permute-start(bf16[2,128,1280]{2,1,0:T(8,128)(2,1)S(1)} %get-tuple-element.59), channel_id=1, source_target_pairs={{0,1},{1,0},{2,3},{3,2},{4,5},{5,4},{6,7},{7,6},{8,9},{9,8},{10,11... | collective-permute-start | bytes 1966088 | tf_op jit(solution)/shard_map/ppermute | solution.py:303
  68.4 1.0 key_grad.1.mine
  69.5 0.1 pad_maximum_fusion
  69.6 0.5 collective-permute-done.6.theirs
  70.1 1.1 combine.1
  71.1 4.3 %all-to-all-start.1 = ((bf16[16,4,80,128]{3,2,1,0:T(8,128)(2,1)}), bf16[16,4,80,128]{3,2,1,0:T(8,128)(2,1)S(1)}, u32[]{:S(2)}, u32[]{:S(2)}) async-start(bf16[16,4,80,128]{3,2,1,0:T(8,128)(2,1)} %combine.1), calls=%async_computation.1 | async-start | bytes 2621440 | tf_op jit(solution)/shard_map/all_to_all | solution.py:320
  75.4 11.0 %collective-permute-start.7 = (bf16[2,2,4,2048]{3,2,1,0:T(4,128)(2,1)S(1)}, bf16[2,2,4,2048]{3,2,1,0:T(4,128)(2,1)S(1)}, u32[]{:S(2)}, u32[]{:S(2)}) collective-permute-start(bf16[2,2,4,2048]{3,2,1,0:T(4,128)(2,1)S(1)} %get-tuple-element.62), channel_id=1, source_target_pairs={{0,160},{32,192},{64,224},{96,0},{128,32},{160,64},{192,96},{224,1... | collective-permute-start | bytes 196616 | tf_op jit(solution)/shard_map/ppermute | solution.py:274
  86.4 1.9 %collective-permute-start.8 = (bf16[2,2,4,2048]{3,2,1,0:T(4,128)(2,1)S(1)}, bf16[2,2,4,2048]{3,2,1,0:T(4,128)(2,1)S(1)}, u32[]{:S(2)}, u32[]{:S(2)}) collective-permute-start(bf16[2,2,4,2048]{3,2,1,0:T(4,128)(2,1)S(1)} %get-tuple-element.63), channel_id=1, source_target_pairs={{0,192},{32,224},{64,0},{96,32},{128,64},{160,96},{192,128},{224,1... | collective-permute-start | bytes 196616 | tf_op jit(solution)/shard_map/ppermute | solution.py:274
  88.4 2.2 %collective-permute-start.9 = (bf16[2,2,4,2048]{3,2,1,0:T(4,128)(2,1)S(1)}, bf16[2,2,4,2048]{3,2,1,0:T(4,128)(2,1)S(1)}, u32[]{:S(2)}, u32[]{:S(2)}) collective-permute-start(bf16[2,2,4,2048]{3,2,1,0:T(4,128)(2,1)S(1)} %pad_maximum_fusion.2), channel_id=1, source_target_pairs={{0,224},{32,0},{64,32},{96,64},{128,96},{160,128},{192,160},{224,1... | collective-permute-start | bytes 196616 | tf_op jit(solution)/shard_map/ppermute | solution.py:274
  90.6 0.0 collective-permute-done.7.refs_6_
  90.6 2.8 %collective-permute-done.8.refs_7_ = bf16[2,2,4,2048]{3,2,1,0:T(4,128)(2,1)S(1)} collective-permute-done((bf16[2,2,4,2048]{3,2,1,0:T(4,128)(2,1)S(1)}, bf16[2,2,4,2048]{3,2,1,0:T(4,128)(2,1)S(1)}, u32[]{:S(2)}, u32[]{:S(2)}) %collective-permute-start.8) | collective-permute-done | bytes 65568 | tf_op jit(solution)/shard_map/ppermute | solution.py:274
  93.3 2.6 %collective-permute-done.9.refs_8_ = bf16[2,2,4,2048]{3,2,1,0:T(4,128)(2,1)S(1)} collective-permute-done((bf16[2,2,4,2048]{3,2,1,0:T(4,128)(2,1)S(1)}, bf16[2,2,4,2048]{3,2,1,0:T(4,128)(2,1)S(1)}, u32[]{:S(2)}, u32[]{:S(2)}) %collective-permute-start.9) | collective-permute-done | bytes 65568 | tf_op jit(solution)/shard_map/ppermute | solution.py:274
  95.9 1.3 %control_unpack.1 = (bf16[16,4,2048]{2,1,0:T(4,128)(2,1)}, bf16[64,2048]{1,0:T(8,128)(2,1)S(1)}) custom-call(s32[4]{0:T(128)S(1)} %pad_add_fusion.info, bf16[2,2,4,2048]{3,2,1,0:T(4,128)(2,1)S(1)} %get-tuple-element.48.refs_0_, bf16[2,2,4,2048]{3,2,1,0:T(4,128)(2,1)S(1)} %collective-permute-done.refs_1_, ...), custom_call_target="tpu_custom_call" | custom-call | tf_op jit(solution)/shard_map/control_unpack/pallas_call | solution.py:321
  97.2 10.8 %all-to-all-done.1.back = bf16[16,4,80,128]{3,2,1,0:T(8,128)(2,1)S(1)} async-done(((bf16[16,4,80,128]{3,2,1,0:T(8,128)(2,1)}), bf16[16,4,80,128]{3,2,1,0:T(8,128)(2,1)S(1)}, u32[]{:S(2)}, u32[]{:S(2)}) %all-to-all-start.1) | async-done | bytes 1310752 | tf_op jit(solution)/shard_map/all_to_all | solution.py:320
  108.0 1.2 %unpack.1 = (bf16[16,2048]{1,0:T(8,128)(2,1)}, bf16[64,2048]{1,0:T(8,128)(2,1)}, bf16[3,16,2048]{2,1,0:T(8,128)(2,1)}, bf16[3,64,2048]{2,1,0:T(8,128)(2,1)}) custom-call(bf16[16,4,80,128]{3,2,1,0:T(8,128)(2,1)S(1)} %all-to-all-done.1.back, bf16[64,2048]{1,0:T(8,128)(2,1)S(1)} %get-tuple-element.65.residual, f32[1,2048]{1,0:T(1,128)S(1)} %bitcast.28), custom_call_target="tpu_custom_call" | custom-call | tf_op jit(solution)/shard_map/unpack/pallas_call | solution.py:330
  (10 shorter events, 0.3 us)
Async XLA Ops:
  2.8 8.9 %copy-start = (bf16[1,64,2048]{2,1,0:T(8,128)(2,1)S(1)}, bf16[1,64,2048]{2,1,0:T(8,128)(2,1)}, u32[]{:S(2)}) copy-start(bf16[1,64,2048]{2,1,0:T(8,128)(2,1)} %param.10) | copy-start | bytes 786436
  2.9 8.9 %copy-start.1 = (bf16[16,1,4,2048]{3,2,1,0:T(4,128)(2,1)S(1)}, bf16[16,1,4,2048]{3,2,1,0:T(4,128)(2,1)}, u32[]{:S(2)}) copy-start(bf16[16,1,4,2048]{3,2,1,0:T(4,128)(2,1)} %param.11) | copy-start | bytes 786436
  2.9 8.9 %copy-start.2 = (f32[2048]{0:T(1024)S(1)}, f32[2048]{0:T(1024)}, u32[]{:S(2)}) copy-start(f32[2048]{0:T(1024)} %param.12) | copy-start | bytes 24580
  2.9 40.7 %all-to-all-start = ((bf16[16,4,80,128]{3,2,1,0:T(8,128)(2,1)}), bf16[16,4,80,128]{3,2,1,0:T(8,128)(2,1)S(1)}, u32[]{:S(2)}, u32[]{:S(2)}) async-start(bf16[16,4,80,128]{3,2,1,0:T(8,128)(2,1)} %pack.1), calls=%async_computation | async-start | bytes 2621440 | tf_op jit(solution)/shard_map/all_to_all | solution.py:262
  12.4 19.7 %collective-permute-start = (bf16[2,2,4,2048]{3,2,1,0:T(4,128)(2,1)S(1)}, bf16[2,2,4,2048]{3,2,1,0:T(4,128)(2,1)S(1)}, u32[]{:S(2)}, u32[]{:S(2)}) collective-permute-start(bf16[2,2,4,2048]{3,2,1,0:T(4,128)(2,1)S(1)} %get-tuple-element.41), channel_id=1, source_target_pairs={{0,32},{32,64},{64,96},{96,128},{128,160},{160,192},{192,224},{224... | collective-permute-start | bytes 196616 | tf_op jit(solution)/shard_map/ppermute | solution.py:274
  16.4 15.7 %collective-permute-start.1 = (bf16[2,2,4,2048]{3,2,1,0:T(4,128)(2,1)S(1)}, bf16[2,2,4,2048]{3,2,1,0:T(4,128)(2,1)S(1)}, u32[]{:S(2)}, u32[]{:S(2)}) collective-permute-start(bf16[2,2,4,2048]{3,2,1,0:T(4,128)(2,1)S(1)} %get-tuple-element.42), channel_id=1, source_target_pairs={{0,64},{32,96},{64,128},{96,160},{128,192},{160,224},{192,0},{224,... | collective-permute-start | bytes 196616 | tf_op jit(solution)/shard_map/ppermute | solution.py:274
  22.2 9.9 %collective-permute-start.2 = (bf16[2,2,4,2048]{3,2,1,0:T(4,128)(2,1)S(1)}, bf16[2,2,4,2048]{3,2,1,0:T(4,128)(2,1)S(1)}, u32[]{:S(2)}, u32[]{:S(2)}) collective-permute-start(bf16[2,2,4,2048]{3,2,1,0:T(4,128)(2,1)S(1)} %get-tuple-element.43), channel_id=1, source_target_pairs={{0,96},{32,128},{64,160},{96,192},{128,224},{160,0},{192,32},{224,... | collective-permute-start | bytes 196616 | tf_op jit(solution)/shard_map/ppermute | solution.py:274
  29.3 9.0 %collective-permute-start.3 = (bf16[2,2,4,2048]{3,2,1,0:T(4,128)(2,1)S(1)}, bf16[2,2,4,2048]{3,2,1,0:T(4,128)(2,1)S(1)}, u32[]{:S(2)}, u32[]{:S(2)}) collective-permute-start(bf16[2,2,4,2048]{3,2,1,0:T(4,128)(2,1)S(1)} %get-tuple-element.44), channel_id=1, source_target_pairs={{0,128},{32,160},{64,192},{96,224},{128,0},{160,32},{192,64},{224,... | collective-permute-start | bytes 196616 | tf_op jit(solution)/shard_map/ppermute | solution.py:274
  43.6 8.7 %collective-permute-start.4 = (bf16[16,4,80,128]{3,2,1,0:T(8,128)(2,1)S(1)}, bf16[16,4,80,128]{3,2,1,0:T(8,128)(2,1)S(1)}, u32[]{:S(2)}, u32[]{:S(2)}) collective-permute-start(bf16[16,4,80,128]{3,2,1,0:T(8,128)(2,1)S(1)} %all-to-all-done.own), channel_id=1, source_target_pairs={{0,1},{1,0},{2,3},{3,2},{4,5},{5,4},{6,7},{7,6},{8,9},{9,8},{10,11... | collective-permute-start | bytes 3932168 | tf_op jit(solution)/shard_map/ppermute | solution.py:279
  47.5 18.5 %collective-permute-start.5 = (bf16[8,2,4,2048]{3,2,1,0:T(4,128)(2,1)S(1)}, bf16[8,2,4,2048]{3,2,1,0:T(4,128)(2,1)S(1)}, u32[]{:S(2)}, u32[]{:S(2)}) collective-permute-start(bf16[8,2,4,2048]{3,2,1,0:T(4,128)(2,1)S(1)} %get-tuple-element.80), channel_id=1, source_target_pairs={{0,256},{256,0},{1,257},{257,1},{2,258},{258,2},{3,259},{259,3},{4... | collective-permute-start | bytes 786440 | tf_op jit(solution)/shard_map/ppermute | solution.py:280
  66.0 4.0 %collective-permute-start.6 = (bf16[2,128,1280]{2,1,0:T(8,128)(2,1)S(1)}, bf16[2,128,1280]{2,1,0:T(8,128)(2,1)S(1)}, u32[]{:S(2)}, u32[]{:S(2)}) collective-permute-start(bf16[2,128,1280]{2,1,0:T(8,128)(2,1)S(1)} %get-tuple-element.59), channel_id=1, source_target_pairs={{0,1},{1,0},{2,3},{3,2},{4,5},{5,4},{6,7},{7,6},{8,9},{9,8},{10,11... | collective-permute-start | bytes 1966088 | tf_op jit(solution)/shard_map/ppermute | solution.py:303
  71.1 36.9 %all-to-all-start.1 = ((bf16[16,4,80,128]{3,2,1,0:T(8,128)(2,1)}), bf16[16,4,80,128]{3,2,1,0:T(8,128)(2,1)S(1)}, u32[]{:S(2)}, u32[]{:S(2)}) async-start(bf16[16,4,80,128]{3,2,1,0:T(8,128)(2,1)} %combine.1), calls=%async_computation.1 | async-start | bytes 2621440 | tf_op jit(solution)/shard_map/all_to_all | solution.py:320
  75.4 15.2 %collective-permute-start.7 = (bf16[2,2,4,2048]{3,2,1,0:T(4,128)(2,1)S(1)}, bf16[2,2,4,2048]{3,2,1,0:T(4,128)(2,1)S(1)}, u32[]{:S(2)}, u32[]{:S(2)}) collective-permute-start(bf16[2,2,4,2048]{3,2,1,0:T(4,128)(2,1)S(1)} %get-tuple-element.62), channel_id=1, source_target_pairs={{0,160},{32,192},{64,224},{96,0},{128,32},{160,64},{192,96},{224,1... | collective-permute-start | bytes 196616 | tf_op jit(solution)/shard_map/ppermute | solution.py:274
  86.4 6.9 %collective-permute-start.8 = (bf16[2,2,4,2048]{3,2,1,0:T(4,128)(2,1)S(1)}, bf16[2,2,4,2048]{3,2,1,0:T(4,128)(2,1)S(1)}, u32[]{:S(2)}, u32[]{:S(2)}) collective-permute-start(bf16[2,2,4,2048]{3,2,1,0:T(4,128)(2,1)S(1)} %get-tuple-element.63), channel_id=1, source_target_pairs={{0,192},{32,224},{64,0},{96,32},{128,64},{160,96},{192,128},{224,1... | collective-permute-start | bytes 196616 | tf_op jit(solution)/shard_map/ppermute | solution.py:274
  88.4 7.6 %collective-permute-start.9 = (bf16[2,2,4,2048]{3,2,1,0:T(4,128)(2,1)S(1)}, bf16[2,2,4,2048]{3,2,1,0:T(4,128)(2,1)S(1)}, u32[]{:S(2)}, u32[]{:S(2)}) collective-permute-start(bf16[2,2,4,2048]{3,2,1,0:T(4,128)(2,1)S(1)} %pad_maximum_fusion.2), channel_id=1, source_target_pairs={{0,224},{32,0},{64,32},{96,64},{128,96},{160,128},{192,160},{224,1... | collective-permute-start | bytes 196616 | tf_op jit(solution)/shard_map/ppermute | solution.py:274

commit v4 on v3

--- a/solution.py
+++ b/solution.py
@@ -278,42 +278,52 @@
     own, *near = lax.optimization_barrier([own] + near)
     oth = lax.ppermute(own, "core", swap)
     far = lax.ppermute(jnp.stack([p[1] for p in near + pieces[EARLY:]]), "yh", swap)
-    square = ((NQ, NQ), bf16)
-    turned = ((2, HEAD, NQ), bf16)
-    part, give, e_own, ds_own, qgt = call(
-        attention_kernel,
-        [SM, VM, VM],
-        [((CHIPS, 4, ROWS, HEAD), bf16), turned, square, square, turned],
-        [
-            pltpu.VMEM((NQ, HEAD), bf16),
-            pltpu.VMEM((NQ, HEAD), bf16),
-            pltpu.VMEM((NK, HEAD), bf16),
-            pltpu.VMEM((NK, HEAD), bf16),
-            pltpu.VMEM((BQ, NK), f32),
-            pltpu.VMEM((NQ, NQ), bf16),
-            pltpu.VMEM((NQ, NQ), bf16),
-            pltpu.VMEM((2, 8, HALF_TXT), f32),
-        ],
-        vmem=32,
-        name="attention",
-        cost_estimate=pl.CostEstimate(
-            flops=12 * NQ * NK * HEAD, bytes_accessed=8 << 20, transcendentals=NQ * NK
-        ),
-    )(info, own, oth)
-    theirs = lax.ppermute(give, "core", swap)
-    qgt, far = lax.optimization_barrier((qgt, far))
-    mine = call(key_grad_kernel, [VM] * 3, [((2, HEAD, NQ), f32)], vmem=16, name="key_grad")(
-        qgt, e_own, ds_own
-    )
-    ready = call(
-        combine_kernel,
-        [ANY, VM, VM],
-        [((CHIPS, 4, ROWS, HEAD), bf16)],
-        out_place=ANY,
-        scratch=[pltpu.VMEM((2, CHIPS, ROWS, HEAD), bf16), pltpu.SemaphoreType.DMA((2,))],
-        input_output_aliases={0: 0},
-        name="combine",
-    )(part, mine, theirs)
+    def attend(info, own, oth):
+        square = ((NQ, NQ), bf16)
+        turned = ((2, HEAD, NQ), bf16)
+        part, give, e_own, ds_own, qgt = call(
+            attention_kernel,
+            [SM, VM, VM],
+            [((CHIPS, 4, ROWS, HEAD), bf16), turned, square, square, turned],
+            [
+                pltpu.VMEM((NQ, HEAD), bf16),
+                pltpu.VMEM((NQ, HEAD), bf16),
+                pltpu.VMEM((NK, HEAD), bf16),
+                pltpu.VMEM((NK, HEAD), bf16),
+                pltpu.VMEM((BQ, NK), f32),
+                pltpu.VMEM((NQ, NQ), bf16),
+                pltpu.VMEM((NQ, NQ), bf16),
+                pltpu.VMEM((2, 8, HALF_TXT), f32),
+            ],
+            vmem=32,
+            name="attention",
+            cost_estimate=pl.CostEstimate(
+                flops=12 * NQ * NK * HEAD, bytes_accessed=8 << 20, transcendentals=NQ * NK
+            ),
+        )(info, own, oth)
+        theirs = lax.ppermute(give, "core", swap)
+        mine = call(key_grad_kernel, [VM] * 3, [((2, HEAD, NQ), f32)], vmem=16, name="key_grad")(
+            qgt, e_own, ds_own
+        )
+        return call(
+            combine_kernel,
+            [ANY, VM, VM],
+            [((CHIPS, 4, ROWS, HEAD), bf16)],
+            out_place=ANY,
+            scratch=[pltpu.VMEM((2, CHIPS, ROWS, HEAD), bf16), pltpu.SemaphoreType.DMA((2,))],
+            input_output_aliases={0: 0},
+            name="combine",
+        )(part, mine, theirs)
+
+    ready = lax.cond(
+        lengths[0] >= 0,
+        attend,
+        lambda info, own, oth: jnp.zeros((CHIPS, 4, ROWS, HEAD), bf16),
+        info,
+        own,
+        oth,
+    )
+    ready, far = lax.optimization_barrier((ready, far))
     late = [jnp.stack([pieces[k][0], far[k]]) for k in range(EARLY, ZS)]
     ready, *late = lax.optimization_barrier([ready] + late)
     late = [shift(x, EARLY + n) for n, x in enumerate(late)]

time: 110 us -> 108 us (0.982)
  waiting for transfers between devices: 30.6 us -> 29.3 us
  starting transfers between devices: 58 us -> 56.9 us
    ppermute x1, waiting for transfers between devices: 2.44 us -> 0.01 us  [body(): lax.ppermute(jnp.stack([p[1] for p in near + pieces[EARLY:]]), 'yh', swap)]
    all_to_all x1, waiting for transfers between devices: 10.8 us -> 12.2 us  [body(): back = lax.all_to_all(ready, chips, split_axis=0, concat_axis=0, tiled=True)]
  transfers between devices with their start and end apart: 12 -> 12, of which waited for: 7 -> 6; matrix products, arithmetic and copies ran while one was open for 0% -> 0% of each run, Pallas kernels for 13% -> 15%
where the time goes in v4:
time: 108 us
  starting transfers between devices  56.9 us (53%)
  waiting for transfers between devices  29.3 us (27%)
  Pallas kernels  19.4 us (18%)
  between operations  1.53 us (1%)
    ppermute x7, starting transfers between devices, shift(): return lax.ppermute(x, 'z', [(i, (i + k) % ZS) for i in range(ZS)])  34.4 us
    all_to_all x1, waiting for transfers between devices, body(): back = lax.all_to_all(ready, chips, split_axis=0, concat_axis=0, tiled=True)  12.2 us
    pallas_call x1, Pallas kernels, attend(): call(attention_kernel, [SM, VM, VM], [((CHIPS, 4, ROWS, HEAD), bf16), tur...  12.1 us
    ppermute x7, waiting for transfers between devices, shift(): return lax.ppermute(x, 'z', [(i, (i + k) % ZS) for i in range(ZS)])  11.1 us
    all_to_all x1, starting transfers between devices, body(): own = lax.all_to_all(send, chips, split_axis=0, concat_axis=0, tiled=True)  8.14 us
    all_to_all x1, waiting for transfers between devices, body(): own = lax.all_to_all(send, chips, split_axis=0, concat_axis=0, tiled=True)  5.27 us
    ppermute x1, starting transfers between devices, body(): lax.ppermute(jnp.stack([p[1] for p in near + pieces[EARLY:]]), 'yh', swap)  4.8 us
    all_to_all x1, starting transfers between devices, body(): back = lax.all_to_all(ready, chips, split_axis=0, concat_axis=0, tiled=True)  3.71 us
  transfers between devices with their start and end apart: 12, of which 6 were waited for; matrix products, arithmetic and copies ran while one was open for 0% of the time, Pallas kernels for 15%

profile of v4, /device:TPU:1, one launch (start us, length us, event | category | flops | bytes accessed | tf_op | source)
XLA Modules:
  0.0 107.7 jit_solution(16594236857175021247)
XLA Ops:
  0.6 2.2 %pack.1 = bf16[16,4,80,128]{3,2,1,0:T(8,128)(2,1)} custom-call(bf16[3,16,2048]{2,1,0:T(8,128)(2,1)} %bitcast.31, bf16[3,64,2048]{2,1,0:T(8,128)(2,1)} %bitcast.30, bf16[16,2048]{1,0:T(8,128)(2,1)} %bitcast.32, bf16[64,2048]{1,0:T(8,128)(2,1)} %bitcast.25), custom_call_target="tpu_custom_call" | custom-call | tf_op jit(solution)/shard_map/pack/pallas_call | solution.py:244
  2.8 0.0 copy-start
  2.9 0.0 copy-start.1
  2.9 0.0 copy-start.2
  2.9 8.1 %all-to-all-start = ((bf16[16,4,80,128]{3,2,1,0:T(8,128)(2,1)}), bf16[16,4,80,128]{3,2,1,0:T(8,128)(2,1)S(1)}, u32[]{:S(2)}, u32[]{:S(2)}) async-start(bf16[16,4,80,128]{3,2,1,0:T(8,128)(2,1)} %pack.1), calls=%async_computation | async-start | bytes 2621440 | tf_op jit(solution)/shard_map/all_to_all | solution.py:262
  11.7 0.1 pad_add_fusion.info
  11.7 0.0 copy-done
  11.8 0.0 copy-done.1
  11.8 0.0 copy-done.2
  11.8 0.6 control_pack.1
  12.4 4.0 %collective-permute-start.1 = (bf16[2,2,4,2048]{3,2,1,0:T(4,128)(2,1)S(1)}, bf16[2,2,4,2048]{3,2,1,0:T(4,128)(2,1)S(1)}, u32[]{:S(2)}, u32[]{:S(2)}) collective-permute-start(bf16[2,2,4,2048]{3,2,1,0:T(4,128)(2,1)S(1)} %get-tuple-element.53), channel_id=1, source_target_pairs={{0,32},{32,64},{64,96},{96,128},{128,160},{160,192},{192,224},{224... | collective-permute-start | bytes 196616 | tf_op jit(solution)/shard_map/ppermute | solution.py:274
  16.4 5.8 %collective-permute-start.2 = (bf16[2,2,4,2048]{3,2,1,0:T(4,128)(2,1)S(1)}, bf16[2,2,4,2048]{3,2,1,0:T(4,128)(2,1)S(1)}, u32[]{:S(2)}, u32[]{:S(2)}) collective-permute-start(bf16[2,2,4,2048]{3,2,1,0:T(4,128)(2,1)S(1)} %get-tuple-element.54), channel_id=1, source_target_pairs={{0,64},{32,96},{64,128},{96,160},{128,192},{160,224},{192,0},{224,... | collective-permute-start | bytes 196616 | tf_op jit(solution)/shard_map/ppermute | solution.py:274
  22.2 7.0 %collective-permute-start.3 = (bf16[2,2,4,2048]{3,2,1,0:T(4,128)(2,1)S(1)}, bf16[2,2,4,2048]{3,2,1,0:T(4,128)(2,1)S(1)}, u32[]{:S(2)}, u32[]{:S(2)}) collective-permute-start(bf16[2,2,4,2048]{3,2,1,0:T(4,128)(2,1)S(1)} %get-tuple-element.55), channel_id=1, source_target_pairs={{0,96},{32,128},{64,160},{96,192},{128,224},{160,0},{192,32},{224,... | collective-permute-start | bytes 196616 | tf_op jit(solution)/shard_map/ppermute | solution.py:274
  29.3 2.8 %collective-permute-start.4 = (bf16[2,2,4,2048]{3,2,1,0:T(4,128)(2,1)S(1)}, bf16[2,2,4,2048]{3,2,1,0:T(4,128)(2,1)S(1)}, u32[]{:S(2)}, u32[]{:S(2)}) collective-permute-start(bf16[2,2,4,2048]{3,2,1,0:T(4,128)(2,1)S(1)} %get-tuple-element.56), channel_id=1, source_target_pairs={{0,128},{32,160},{64,192},{96,224},{128,0},{160,32},{192,64},{224,... | collective-permute-start | bytes 196616 | tf_op jit(solution)/shard_map/ppermute | solution.py:274
  32.1 0.0 collective-permute-done.1.refs_1_
  32.1 0.0 collective-permute-done.2.refs_2_
  32.1 0.0 collective-permute-done.3.refs_3_
  32.1 6.2 %collective-permute-done.4.refs_4_ = bf16[2,2,4,2048]{3,2,1,0:T(4,128)(2,1)S(1)} collective-permute-done((bf16[2,2,4,2048]{3,2,1,0:T(4,128)(2,1)S(1)}, bf16[2,2,4,2048]{3,2,1,0:T(4,128)(2,1)S(1)}, u32[]{:S(2)}, u32[]{:S(2)}) %collective-permute-start.4) | collective-permute-done | bytes 65568 | tf_op jit(solution)/shard_map/ppermute | solution.py:274
  38.3 5.3 %all-to-all-done = bf16[16,4,80,128]{3,2,1,0:T(8,128)(2,1)S(1)} async-done(((bf16[16,4,80,128]{3,2,1,0:T(8,128)(2,1)}), bf16[16,4,80,128]{3,2,1,0:T(8,128)(2,1)S(1)}, u32[]{:S(2)}, u32[]{:S(2)}) %all-to-all-start) | async-done | bytes 1310752 | tf_op jit(solution)/shard_map/all_to_all | solution.py:262
  43.6 3.7 %collective-permute-start.5 = (bf16[16,4,80,128]{3,2,1,0:T(8,128)(2,1)S(1)}, bf16[16,4,80,128]{3,2,1,0:T(8,128)(2,1)}, u32[]{:S(2)}, u32[]{:S(2)}) collective-permute-start(bf16[16,4,80,128]{3,2,1,0:T(8,128)(2,1)S(1)} %all-to-all-done), channel_id=1, source_target_pairs={{0,1},{1,0},{2,3},{3,2},{4,5},{5,4},{6,7},{7,6},{8,9},{9,8},{10,11... | collective-permute-start | bytes 3932168 | tf_op jit(solution)/shard_map/ppermute | solution.py:279
  47.5 4.8 %collective-permute-start.6 = (bf16[8,2,4,2048]{3,2,1,0:T(4,128)(2,1)S(1)}, bf16[8,2,4,2048]{3,2,1,0:T(4,128)(2,1)S(1)}, u32[]{:S(2)}, u32[]{:S(2)}) collective-permute-start(bf16[8,2,4,2048]{3,2,1,0:T(4,128)(2,1)S(1)} %get-tuple-element.87), channel_id=1, source_target_pairs={{0,256},{256,0},{1,257},{257,1},{2,258},{258,2},{3,259},{259,3},{4... | collective-permute-start | bytes 786440 | tf_op jit(solution)/shard_map/ppermute | solution.py:280
  52.3 0.0 collective-permute-done.5
  52.3 17.1 %conditional.1 = (bf16[16,4,80,128]{3,2,1,0:T(8,128)(2,1)}) conditional(s32[]{:T(128)} %bitcast, () %tuple.18, (s32[4]{0:T(128)S(1)}, bf16[16,4,80,128]{3,2,1,0:T(8,128)(2,1)S(1)}, bf16[16,4,80,128]{3,2,1,0:T(8,128)(2,1)}) %tuple.21), branch_computations={%region_0.0_spmd, %region_1.0_spmd} | conditional | flops 5033164800 | bytes 11010096 | solution.py:318
  52.3 12.1 %attention.1 = (bf16[16,4,80,128]{3,2,1,0:T(8,128)(2,1)}, bf16[2,128,1280]{2,1,0:T(8,128)(2,1)S(1)}, bf16[1280,1280]{1,0:T(8,128)(2,1)S(1)}, bf16[1280,1280]{1,0:T(8,128)(2,1)S(1)}, bf16[2,128,1280]{2,1,0:T(8,128)(2,1)S(1)}) custom-call(s32[4]{0:T(128)S(1)} %get-tuple-element.2.info, bf16[16,4,80,128]{3,2,1,0:T(8,128)(2,1)S(1)} %get-tuple-element.10.own, ...), custom_call_target="tpu_custom_call" | custom-call | flops 5033164800 | bytes 8388608 | tf_op jit(solution)/shard_map/cond/branch_1_fun/attention/pallas_call | solution.py:284
  64.4 2.2 %collective-permute-start = (bf16[2,128,1280]{2,1,0:T(8,128)(2,1)S(1)}, bf16[2,128,1280]{2,1,0:T(8,128)(2,1)S(1)}, u32[]{:S(2)}, u32[]{:S(2)}) collective-permute-start(bf16[2,128,1280]{2,1,0:T(8,128)(2,1)S(1)} %get-tuple-element.16), channel_id=1, source_target_pairs={{0,1},{1,0},{2,3},{3,2},{4,5},{5,4},{6,7},{7,6},{8,9},{9,8},{10,11... | collective-permute-start | bytes 1966088 | tf_op jit(solution)/shard_map/cond/branch_1_fun/ppermute | solution.py:304
  66.6 1.0 key_grad.1.mine
  67.6 0.8 collective-permute-done.theirs
  68.4 1.0 combine.1
  69.4 0.0 collective-permute-done.6.refs_5_
  69.5 0.1 pad_maximum_fusion
  69.6 3.7 %all-to-all-start.1 = ((bf16[16,4,80,128]{3,2,1,0:T(8,128)(2,1)}), bf16[16,4,80,128]{3,2,1,0:T(8,128)(2,1)S(1)}, u32[]{:S(2)}, u32[]{:S(2)}) async-start(bf16[16,4,80,128]{3,2,1,0:T(8,128)(2,1)} %get-tuple-element.94), calls=%async_computation.1 | async-start | bytes 2621440 | tf_op jit(solution)/shard_map/all_to_all | solution.py:330
  73.3 10.6 %collective-permute-start.7 = (bf16[2,2,4,2048]{3,2,1,0:T(4,128)(2,1)S(1)}, bf16[2,2,4,2048]{3,2,1,0:T(4,128)(2,1)S(1)}, u32[]{:S(2)}, u32[]{:S(2)}) collective-permute-start(bf16[2,2,4,2048]{3,2,1,0:T(4,128)(2,1)S(1)} %get-tuple-element.69), channel_id=1, source_target_pairs={{0,160},{32,192},{64,224},{96,0},{128,32},{160,64},{192,96},{224,1... | collective-permute-start | bytes 196616 | tf_op jit(solution)/shard_map/ppermute | solution.py:274
  84.0 1.9 %collective-permute-start.8 = (bf16[2,2,4,2048]{3,2,1,0:T(4,128)(2,1)S(1)}, bf16[2,2,4,2048]{3,2,1,0:T(4,128)(2,1)S(1)}, u32[]{:S(2)}, u32[]{:S(2)}) collective-permute-start(bf16[2,2,4,2048]{3,2,1,0:T(4,128)(2,1)S(1)} %get-tuple-element.70), channel_id=1, source_target_pairs={{0,192},{32,224},{64,0},{96,32},{128,64},{160,96},{192,128},{224,1... | collective-permute-start | bytes 196616 | tf_op jit(solution)/shard_map/ppermute | solution.py:274
  85.9 2.2 %collective-permute-start.9 = (bf16[2,2,4,2048]{3,2,1,0:T(4,128)(2,1)S(1)}, bf16[2,2,4,2048]{3,2,1,0:T(4,128)(2,1)S(1)}, u32[]{:S(2)}, u32[]{:S(2)}) collective-permute-start(bf16[2,2,4,2048]{3,2,1,0:T(4,128)(2,1)S(1)} %pad_maximum_fusion.2), channel_id=1, source_target_pairs={{0,224},{32,0},{64,32},{96,64},{128,96},{160,128},{192,160},{224,1... | collective-permute-start | bytes 196616 | tf_op jit(solution)/shard_map/ppermute | solution.py:274
  88.1 0.0 collective-permute-done.7.refs_6_
  88.1 2.4 %collective-permute-done.8.refs_7_ = bf16[2,2,4,2048]{3,2,1,0:T(4,128)(2,1)S(1)} collective-permute-done((bf16[2,2,4,2048]{3,2,1,0:T(4,128)(2,1)S(1)}, bf16[2,2,4,2048]{3,2,1,0:T(4,128)(2,1)S(1)}, u32[]{:S(2)}, u32[]{:S(2)}) %collective-permute-start.8) | collective-permute-done | bytes 65568 | tf_op jit(solution)/shard_map/ppermute | solution.py:274
  90.6 2.4 %collective-permute-done.9.refs_8_ = bf16[2,2,4,2048]{3,2,1,0:T(4,128)(2,1)S(1)} collective-permute-done((bf16[2,2,4,2048]{3,2,1,0:T(4,128)(2,1)S(1)}, bf16[2,2,4,2048]{3,2,1,0:T(4,128)(2,1)S(1)}, u32[]{:S(2)}, u32[]{:S(2)}) %collective-permute-start.9) | collective-permute-done | bytes 65568 | tf_op jit(solution)/shard_map/ppermute | solution.py:274
  93.0 1.3 %control_unpack.1 = (bf16[16,4,2048]{2,1,0:T(4,128)(2,1)}, bf16[64,2048]{1,0:T(8,128)(2,1)S(1)}) custom-call(s32[4]{0:T(128)S(1)} %pad_add_fusion.info, bf16[2,2,4,2048]{3,2,1,0:T(4,128)(2,1)S(1)} %get-tuple-element.58.refs_0_, bf16[2,2,4,2048]{3,2,1,0:T(4,128)(2,1)S(1)} %collective-permute-done.1.refs_1_, ...), custom_call_target="tpu_custom_call" | custom-call | tf_op jit(solution)/shard_map/control_unpack/pallas_call | solution.py:331
  94.3 12.2 %all-to-all-done.1.back = bf16[16,4,80,128]{3,2,1,0:T(8,128)(2,1)S(1)} async-done(((bf16[16,4,80,128]{3,2,1,0:T(8,128)(2,1)}), bf16[16,4,80,128]{3,2,1,0:T(8,128)(2,1)S(1)}, u32[]{:S(2)}, u32[]{:S(2)}) %all-to-all-start.1) | async-done | bytes 1310752 | tf_op jit(solution)/shard_map/all_to_all | solution.py:330
  106.5 1.2 %unpack.1 = (bf16[16,2048]{1,0:T(8,128)(2,1)}, bf16[64,2048]{1,0:T(8,128)(2,1)}, bf16[3,16,2048]{2,1,0:T(8,128)(2,1)}, bf16[3,64,2048]{2,1,0:T(8,128)(2,1)}) custom-call(bf16[16,4,80,128]{3,2,1,0:T(8,128)(2,1)S(1)} %all-to-all-done.1.back, bf16[64,2048]{1,0:T(8,128)(2,1)S(1)} %get-tuple-element.72.residual, f32[1,2048]{1,0:T(1,128)S(1)} %bitcast.29), custom_call_target="tpu_custom_call" | custom-call | tf_op jit(solution)/shard_map/unpack/pallas_call | solution.py:340
  (10 shorter events, 0.3 us)
Async XLA Ops:
  2.8 8.9 %copy-start = (bf16[1,64,2048]{2,1,0:T(8,128)(2,1)S(1)}, bf16[1,64,2048]{2,1,0:T(8,128)(2,1)}, u32[]{:S(2)}) copy-start(bf16[1,64,2048]{2,1,0:T(8,128)(2,1)} %param.12) | copy-start | bytes 786436
  2.9 8.9 %copy-start.1 = (bf16[16,1,4,2048]{3,2,1,0:T(4,128)(2,1)S(1)}, bf16[16,1,4,2048]{3,2,1,0:T(4,128)(2,1)}, u32[]{:S(2)}) copy-start(bf16[16,1,4,2048]{3,2,1,0:T(4,128)(2,1)} %param.13) | copy-start | bytes 786436
  2.9 8.9 %copy-start.2 = (f32[2048]{0:T(1024)S(1)}, f32[2048]{0:T(1024)}, u32[]{:S(2)}) copy-start(f32[2048]{0:T(1024)} %param.14) | copy-start | bytes 24580
  2.9 40.7 %all-to-all-start = ((bf16[16,4,80,128]{3,2,1,0:T(8,128)(2,1)}), bf16[16,4,80,128]{3,2,1,0:T(8,128)(2,1)S(1)}, u32[]{:S(2)}, u32[]{:S(2)}) async-start(bf16[16,4,80,128]{3,2,1,0:T(8,128)(2,1)} %pack.1), calls=%async_computation | async-start | bytes 2621440 | tf_op jit(solution)/shard_map/all_to_all | solution.py:262
  12.4 19.7 %collective-permute-start.1 = (bf16[2,2,4,2048]{3,2,1,0:T(4,128)(2,1)S(1)}, bf16[2,2,4,2048]{3,2,1,0:T(4,128)(2,1)S(1)}, u32[]{:S(2)}, u32[]{:S(2)}) collective-permute-start(bf16[2,2,4,2048]{3,2,1,0:T(4,128)(2,1)S(1)} %get-tuple-element.53), channel_id=1, source_target_pairs={{0,32},{32,64},{64,96},{96,128},{128,160},{160,192},{192,224},{224... | collective-permute-start | bytes 196616 | tf_op jit(solution)/shard_map/ppermute | solution.py:274
  16.4 15.7 %collective-permute-start.2 = (bf16[2,2,4,2048]{3,2,1,0:T(4,128)(2,1)S(1)}, bf16[2,2,4,2048]{3,2,1,0:T(4,128)(2,1)S(1)}, u32[]{:S(2)}, u32[]{:S(2)}) collective-permute-start(bf16[2,2,4,2048]{3,2,1,0:T(4,128)(2,1)S(1)} %get-tuple-element.54), channel_id=1, source_target_pairs={{0,64},{32,96},{64,128},{96,160},{128,192},{160,224},{192,0},{224,... | collective-permute-start | bytes 196616 | tf_op jit(solution)/shard_map/ppermute | solution.py:274
  22.2 9.9 %collective-permute-start.3 = (bf16[2,2,4,2048]{3,2,1,0:T(4,128)(2,1)S(1)}, bf16[2,2,4,2048]{3,2,1,0:T(4,128)(2,1)S(1)}, u32[]{:S(2)}, u32[]{:S(2)}) collective-permute-start(bf16[2,2,4,2048]{3,2,1,0:T(4,128)(2,1)S(1)} %get-tuple-element.55), channel_id=1, source_target_pairs={{0,96},{32,128},{64,160},{96,192},{128,224},{160,0},{192,32},{224,... | collective-permute-start | bytes 196616 | tf_op jit(solution)/shard_map/ppermute | solution.py:274
  29.3 9.0 %collective-permute-start.4 = (bf16[2,2,4,2048]{3,2,1,0:T(4,128)(2,1)S(1)}, bf16[2,2,4,2048]{3,2,1,0:T(4,128)(2,1)S(1)}, u32[]{:S(2)}, u32[]{:S(2)}) collective-permute-start(bf16[2,2,4,2048]{3,2,1,0:T(4,128)(2,1)S(1)} %get-tuple-element.56), channel_id=1, source_target_pairs={{0,128},{32,160},{64,192},{96,224},{128,0},{160,32},{192,64},{224,... | collective-permute-start | bytes 196616 | tf_op jit(solution)/shard_map/ppermute | solution.py:274
  43.6 8.7 %collective-permute-start.5 = (bf16[16,4,80,128]{3,2,1,0:T(8,128)(2,1)S(1)}, bf16[16,4,80,128]{3,2,1,0:T(8,128)(2,1)}, u32[]{:S(2)}, u32[]{:S(2)}) collective-permute-start(bf16[16,4,80,128]{3,2,1,0:T(8,128)(2,1)S(1)} %all-to-all-done), channel_id=1, source_target_pairs={{0,1},{1,0},{2,3},{3,2},{4,5},{5,4},{6,7},{7,6},{8,9},{9,8},{10,11... | collective-permute-start | bytes 3932168 | tf_op jit(solution)/shard_map/ppermute | solution.py:279
  47.5 21.9 %collective-permute-start.6 = (bf16[8,2,4,2048]{3,2,1,0:T(4,128)(2,1)S(1)}, bf16[8,2,4,2048]{3,2,1,0:T(4,128)(2,1)S(1)}, u32[]{:S(2)}, u32[]{:S(2)}) collective-permute-start(bf16[8,2,4,2048]{3,2,1,0:T(4,128)(2,1)S(1)} %get-tuple-element.87), channel_id=1, source_target_pairs={{0,256},{256,0},{1,257},{257,1},{2,258},{258,2},{3,259},{259,3},{4... | collective-permute-start | bytes 786440 | tf_op jit(solution)/shard_map/ppermute | solution.py:280
  64.4 4.0 %collective-permute-start = (bf16[2,128,1280]{2,1,0:T(8,128)(2,1)S(1)}, bf16[2,128,1280]{2,1,0:T(8,128)(2,1)S(1)}, u32[]{:S(2)}, u32[]{:S(2)}) collective-permute-start(bf16[2,128,1280]{2,1,0:T(8,128)(2,1)S(1)} %get-tuple-element.16), channel_id=1, source_target_pairs={{0,1},{1,0},{2,3},{3,2},{4,5},{5,4},{6,7},{7,6},{8,9},{9,8},{10,11... | collective-permute-start | bytes 1966088 | tf_op jit(solution)/shard_map/cond/branch_1_fun/ppermute | solution.py:304
  69.6 36.9 %all-to-all-start.1 = ((bf16[16,4,80,128]{3,2,1,0:T(8,128)(2,1)}), bf16[16,4,80,128]{3,2,1,0:T(8,128)(2,1)S(1)}, u32[]{:S(2)}, u32[]{:S(2)}) async-start(bf16[16,4,80,128]{3,2,1,0:T(8,128)(2,1)} %get-tuple-element.94), calls=%async_computation.1 | async-start | bytes 2621440 | tf_op jit(solution)/shard_map/all_to_all | solution.py:330
  73.3 14.8 %collective-permute-start.7 = (bf16[2,2,4,2048]{3,2,1,0:T(4,128)(2,1)S(1)}, bf16[2,2,4,2048]{3,2,1,0:T(4,128)(2,1)S(1)}, u32[]{:S(2)}, u32[]{:S(2)}) collective-permute-start(bf16[2,2,4,2048]{3,2,1,0:T(4,128)(2,1)S(1)} %get-tuple-element.69), channel_id=1, source_target_pairs={{0,160},{32,192},{64,224},{96,0},{128,32},{160,64},{192,96},{224,1... | collective-permute-start | bytes 196616 | tf_op jit(solution)/shard_map/ppermute | solution.py:274
  84.0 6.6 %collective-permute-start.8 = (bf16[2,2,4,2048]{3,2,1,0:T(4,128)(2,1)S(1)}, bf16[2,2,4,2048]{3,2,1,0:T(4,128)(2,1)S(1)}, u32[]{:S(2)}, u32[]{:S(2)}) collective-permute-start(bf16[2,2,4,2048]{3,2,1,0:T(4,128)(2,1)S(1)} %get-tuple-element.70), channel_id=1, source_target_pairs={{0,192},{32,224},{64,0},{96,32},{128,64},{160,96},{192,128},{224,1... | collective-permute-start | bytes 196616 | tf_op jit(solution)/shard_map/ppermute | solution.py:274
  85.9 7.1 %collective-permute-start.9 = (bf16[2,2,4,2048]{3,2,1,0:T(4,128)(2,1)S(1)}, bf16[2,2,4,2048]{3,2,1,0:T(4,128)(2,1)S(1)}, u32[]{:S(2)}, u32[]{:S(2)}) collective-permute-start(bf16[2,2,4,2048]{3,2,1,0:T(4,128)(2,1)S(1)} %pad_maximum_fusion.2), channel_id=1, source_target_pairs={{0,224},{32,0},{64,32},{96,64},{128,96},{160,128},{192,160},{224,1... | collective-permute-start | bytes 196616 | tf_op jit(solution)/shard_map/ppermute | solution.py:274

commit v5 on v4

--- a/solution.py
+++ b/solution.py
@@ -98,7 +98,7 @@
 
 
 def attention_kernel(
-    info, own, oth, part, give, e_own, ds_own, qgt, q_s, g_s, k_s, v_s, s_s, e_oth, ds_oth, mask_s
+    info, own, oth, aq, give, e_own, ds_own, qgt, q_s, g_s, k_s, v_s, s_s, e_oth, ds_oth, mask_s
 ):
     length = info[0]
     core = info[1]
@@ -122,7 +122,7 @@
         while at < end:
             s, r = divmod(at, ROWS)
             n = min(ROWS - r, end - at)
-            part[s, t, r : r + n, :] = x[at - i * BQ : at - i * BQ + n]
+            aq[t, s, r : r + n, :] = x[at - i * BQ : at - i * BQ + n]
             at += n
 
     def block(i):
@@ -173,9 +173,14 @@
     give[1] = dot(qgt[1], e_oth[...]).astype(jnp.bfloat16)
 
 
-def key_grad_kernel(qgt, e_own, ds_own, mine):
+def key_grad_kernel(qgt, e_own, ds_own, aq, mine, out, sems):
+    copies = [pltpu.make_async_copy(aq.at[t], out.at[:, t], sems.at[t]) for t in range(2)]
+    for copy in copies:
+        copy.start()
     mine[0] = dot(qgt[0], ds_own[...]) * SCALE
     mine[1] = dot(qgt[1], e_own[...])
+    for copy in copies:
+        copy.wait()
 
 
 def combine_kernel(part, mine, theirs, out, x_s, sems):
@@ -223,7 +228,9 @@
     return pl.pallas_call(
         kernel,
         in_specs=ins,
-        out_specs=[out_place] * len(outs) if len(outs) > 1 else out_place,
+        out_specs=out_place
+        if isinstance(out_place, list) or len(outs) == 1
+        else [out_place] * len(outs),
         out_shape=[jax.ShapeDtypeStruct(s, d) for s, d in outs]
         if len(outs) > 1
         else jax.ShapeDtypeStruct(*outs[0]),
@@ -281,10 +288,10 @@
     def attend(info, own, oth):
         square = ((NQ, NQ), bf16)
         turned = ((2, HEAD, NQ), bf16)
-        part, give, e_own, ds_own, qgt = call(
+        aq, give, e_own, ds_own, qgt = call(
             attention_kernel,
             [SM, VM, VM],
-            [((CHIPS, 4, ROWS, HEAD), bf16), turned, square, square, turned],
+            [((2, CHIPS, ROWS, HEAD), bf16), turned, square, square, turned],
             [
                 pltpu.VMEM((NQ, HEAD), bf16),
                 pltpu.VMEM((NQ, HEAD), bf16),
@@ -302,9 +309,15 @@
             ),
         )(info, own, oth)
         theirs = lax.ppermute(give, "core", swap)
-        mine = call(key_grad_kernel, [VM] * 3, [((2, HEAD, NQ), f32)], vmem=16, name="key_grad")(
-            qgt, e_own, ds_own
-        )
+        mine, part = call(
+            key_grad_kernel,
+            [VM] * 4,
+            [((2, HEAD, NQ), f32), ((CHIPS, 4, ROWS, HEAD), bf16)],
+            [pltpu.SemaphoreType.DMA((2,))],
+            vmem=16,
+            out_place=[VM, ANY],
+            name="key_grad",
+        )(qgt, e_own, ds_own, aq)
         return call(
             combine_kernel,
             [ANY, VM, VM],

time: 108 us -> 108 us (level)
  no operation moved by 1% of the time
where the time goes in v5:
time: 108 us; the launch traced here: 107 us
  starting transfers between devices  56.9 us (53%)
  waiting for transfers between devices  29.3 us (27%)
  Pallas kernels  19.2 us (18%)
  between operations  1.53 us (1%)
    ppermute x7, starting transfers between devices, shift(): return lax.ppermute(x, 'z', [(i, (i + k) % ZS) for i in range(ZS)])  34.4 us
    all_to_all x1, waiting for transfers between devices, body(): back = lax.all_to_all(ready, chips, split_axis=0, concat_axis=0, tiled=True)  12.2 us
    pallas_call x1, Pallas kernels, attend(): call(attention_kernel, [SM, VM, VM], [((2, CHIPS, ROWS, HEAD), bf16), tur...  11.8 us
    ppermute x7, waiting for transfers between devices, shift(): return lax.ppermute(x, 'z', [(i, (i + k) % ZS) for i in range(ZS)])  11.1 us
    all_to_all x1, starting transfers between devices, body(): own = lax.all_to_all(send, chips, split_axis=0, concat_axis=0, tiled=True)  8.14 us
    all_to_all x1, waiting for transfers between devices, body(): own = lax.all_to_all(send, chips, split_axis=0, concat_axis=0, tiled=True)  5.27 us
    ppermute x1, starting transfers between devices, body(): lax.ppermute(jnp.stack([p[1] for p in near + pieces[EARLY:]]), 'yh', swap)  4.8 us
    all_to_all x1, starting transfers between devices, body(): back = lax.all_to_all(ready, chips, split_axis=0, concat_axis=0, tiled=True)  3.71 us
  transfers between devices with their start and end apart: 12, of which 6 were waited for; matrix products, arithmetic and copies ran while one was open for 0% of the time, Pallas kernels for 15%

profile of v5, /device:TPU:1, one launch (start us, length us, event | category | flops | bytes accessed | tf_op | source)
XLA Modules:
  0.0 107.4 jit_solution(17951319147654227505)
XLA Ops:
  0.6 2.2 %pack.1 = bf16[16,4,80,128]{3,2,1,0:T(8,128)(2,1)} custom-call(bf16[3,16,2048]{2,1,0:T(8,128)(2,1)} %bitcast.31, bf16[3,64,2048]{2,1,0:T(8,128)(2,1)} %bitcast.30, bf16[16,2048]{1,0:T(8,128)(2,1)} %bitcast.32, bf16[64,2048]{1,0:T(8,128)(2,1)} %bitcast.25), custom_call_target="tpu_custom_call" | custom-call | tf_op jit(solution)/shard_map/pack/pallas_call | solution.py:251
  2.8 0.0 copy-start
  2.9 0.0 copy-start.1
  2.9 0.0 copy-start.2
  2.9 8.1 %all-to-all-start = ((bf16[16,4,80,128]{3,2,1,0:T(8,128)(2,1)}), bf16[16,4,80,128]{3,2,1,0:T(8,128)(2,1)S(1)}, u32[]{:S(2)}, u32[]{:S(2)}) async-start(bf16[16,4,80,128]{3,2,1,0:T(8,128)(2,1)} %pack.1), calls=%async_computation | async-start | bytes 2621440 | tf_op jit(solution)/shard_map/all_to_all | solution.py:269
  11.7 0.1 pad_add_fusion.info
  11.8 0.0 copy-done
  11.8 0.0 copy-done.1
  11.8 0.0 copy-done.2
  11.8 0.6 control_pack.1
  12.4 4.0 %collective-permute-start.1 = (bf16[2,2,4,2048]{3,2,1,0:T(4,128)(2,1)S(1)}, bf16[2,2,4,2048]{3,2,1,0:T(4,128)(2,1)S(1)}, u32[]{:S(2)}, u32[]{:S(2)}) collective-permute-start(bf16[2,2,4,2048]{3,2,1,0:T(4,128)(2,1)S(1)} %get-tuple-element.55), channel_id=1, source_target_pairs={{0,32},{32,64},{64,96},{96,128},{128,160},{160,192},{192,224},{224... | collective-permute-start | bytes 196616 | tf_op jit(solution)/shard_map/ppermute | solution.py:281
  16.4 5.8 %collective-permute-start.2 = (bf16[2,2,4,2048]{3,2,1,0:T(4,128)(2,1)S(1)}, bf16[2,2,4,2048]{3,2,1,0:T(4,128)(2,1)S(1)}, u32[]{:S(2)}, u32[]{:S(2)}) collective-permute-start(bf16[2,2,4,2048]{3,2,1,0:T(4,128)(2,1)S(1)} %get-tuple-element.56), channel_id=1, source_target_pairs={{0,64},{32,96},{64,128},{96,160},{128,192},{160,224},{192,0},{224,... | collective-permute-start | bytes 196616 | tf_op jit(solution)/shard_map/ppermute | solution.py:281
  22.2 7.0 %collective-permute-start.3 = (bf16[2,2,4,2048]{3,2,1,0:T(4,128)(2,1)S(1)}, bf16[2,2,4,2048]{3,2,1,0:T(4,128)(2,1)S(1)}, u32[]{:S(2)}, u32[]{:S(2)}) collective-permute-start(bf16[2,2,4,2048]{3,2,1,0:T(4,128)(2,1)S(1)} %get-tuple-element.57), channel_id=1, source_target_pairs={{0,96},{32,128},{64,160},{96,192},{128,224},{160,0},{192,32},{224,... | collective-permute-start | bytes 196616 | tf_op jit(solution)/shard_map/ppermute | solution.py:281
  29.3 2.8 %collective-permute-start.4 = (bf16[2,2,4,2048]{3,2,1,0:T(4,128)(2,1)S(1)}, bf16[2,2,4,2048]{3,2,1,0:T(4,128)(2,1)S(1)}, u32[]{:S(2)}, u32[]{:S(2)}) collective-permute-start(bf16[2,2,4,2048]{3,2,1,0:T(4,128)(2,1)S(1)} %get-tuple-element.58), channel_id=1, source_target_pairs={{0,128},{32,160},{64,192},{96,224},{128,0},{160,32},{192,64},{224,... | collective-permute-start | bytes 196616 | tf_op jit(solution)/shard_map/ppermute | solution.py:281
  32.1 0.0 collective-permute-done.1.refs_1_
  32.1 0.0 collective-permute-done.2.refs_2_
  32.1 0.0 collective-permute-done.3.refs_3_
  32.1 6.2 %collective-permute-done.4.refs_4_ = bf16[2,2,4,2048]{3,2,1,0:T(4,128)(2,1)S(1)} collective-permute-done((bf16[2,2,4,2048]{3,2,1,0:T(4,128)(2,1)S(1)}, bf16[2,2,4,2048]{3,2,1,0:T(4,128)(2,1)S(1)}, u32[]{:S(2)}, u32[]{:S(2)}) %collective-permute-start.4) | collective-permute-done | bytes 65568 | tf_op jit(solution)/shard_map/ppermute | solution.py:281
  38.3 5.3 %all-to-all-done = bf16[16,4,80,128]{3,2,1,0:T(8,128)(2,1)S(1)} async-done(((bf16[16,4,80,128]{3,2,1,0:T(8,128)(2,1)}), bf16[16,4,80,128]{3,2,1,0:T(8,128)(2,1)S(1)}, u32[]{:S(2)}, u32[]{:S(2)}) %all-to-all-start) | async-done | bytes 1310752 | tf_op jit(solution)/shard_map/all_to_all | solution.py:269
  43.6 3.7 %collective-permute-start.5 = (bf16[16,4,80,128]{3,2,1,0:T(8,128)(2,1)S(1)}, bf16[16,4,80,128]{3,2,1,0:T(8,128)(2,1)}, u32[]{:S(2)}, u32[]{:S(2)}) collective-permute-start(bf16[16,4,80,128]{3,2,1,0:T(8,128)(2,1)S(1)} %all-to-all-done), channel_id=1, source_target_pairs={{0,1},{1,0},{2,3},{3,2},{4,5},{5,4},{6,7},{7,6},{8,9},{9,8},{10,11... | collective-permute-start | bytes 3932168 | tf_op jit(solution)/shard_map/ppermute | solution.py:286
  47.5 4.8 %collective-permute-start.6 = (bf16[8,2,4,2048]{3,2,1,0:T(4,128)(2,1)S(1)}, bf16[8,2,4,2048]{3,2,1,0:T(4,128)(2,1)S(1)}, u32[]{:S(2)}, u32[]{:S(2)}) collective-permute-start(bf16[8,2,4,2048]{3,2,1,0:T(4,128)(2,1)S(1)} %get-tuple-element.89), channel_id=1, source_target_pairs={{0,256},{256,0},{1,257},{257,1},{2,258},{258,2},{3,259},{259,3},{4... | collective-permute-start | bytes 786440 | tf_op jit(solution)/shard_map/ppermute | solution.py:287
  52.3 0.0 collective-permute-done.5
  52.3 16.9 %conditional.1 = (bf16[16,4,80,128]{3,2,1,0:T(8,128)(2,1)}) conditional(s32[]{:T(128)} %bitcast, () %tuple.18, (s32[4]{0:T(128)S(1)}, bf16[16,4,80,128]{3,2,1,0:T(8,128)(2,1)S(1)}, bf16[16,4,80,128]{3,2,1,0:T(8,128)(2,1)}) %tuple.21), branch_computations={%region_0.0_spmd, %region_1.0_spmd} | conditional | flops 5033164800 | bytes 11010096 | solution.py:331
  52.3 11.8 %attention.1 = (bf16[2,16,80,128]{3,2,1,0:T(8,128)(2,1)S(1)}, bf16[2,128,1280]{2,1,0:T(8,128)(2,1)S(1)}, bf16[1280,1280]{1,0:T(8,128)(2,1)S(1)}, bf16[1280,1280]{1,0:T(8,128)(2,1)S(1)}, bf16[2,128,1280]{2,1,0:T(8,128)(2,1)S(1)}) custom-call(s32[4]{0:T(128)S(1)} %get-tuple-element.2.info, bf16[16,4,80,128]{3,2,1,0:T(8,128)(2,1)S(1)} %get-tuple-element.10.own, ...), custom_call_target="tpu_custom_call" | custom-call | flops 5033164800 | bytes 8388608 | tf_op jit(solution)/shard_map/cond/branch_1_fun/attention/pallas_call | solution.py:291
  64.1 2.2 %collective-permute-start = (bf16[2,128,1280]{2,1,0:T(8,128)(2,1)S(1)}, bf16[2,128,1280]{2,1,0:T(8,128)(2,1)S(1)}, u32[]{:S(2)}, u32[]{:S(2)}) collective-permute-start(bf16[2,128,1280]{2,1,0:T(8,128)(2,1)S(1)} %get-tuple-element.18), channel_id=1, source_target_pairs={{0,1},{1,0},{2,3},{3,2},{4,5},{5,4},{6,7},{7,6},{8,9},{9,8},{10,11... | collective-permute-start | bytes 1966088 | tf_op jit(solution)/shard_map/cond/branch_1_fun/ppermute | solution.py:311
  66.4 1.1 key_grad.1
  67.4 0.7 collective-permute-done.theirs
  68.1 1.0 combine.1
  69.2 0.0 collective-permute-done.6.refs_5_
  69.3 0.1 pad_maximum_fusion
  69.4 3.7 %all-to-all-start.1 = ((bf16[16,4,80,128]{3,2,1,0:T(8,128)(2,1)}), bf16[16,4,80,128]{3,2,1,0:T(8,128)(2,1)S(1)}, u32[]{:S(2)}, u32[]{:S(2)}) async-start(bf16[16,4,80,128]{3,2,1,0:T(8,128)(2,1)} %get-tuple-element.96), calls=%async_computation.1 | async-start | bytes 2621440 | tf_op jit(solution)/shard_map/all_to_all | solution.py:343
  73.1 10.6 %collective-permute-start.7 = (bf16[2,2,4,2048]{3,2,1,0:T(4,128)(2,1)S(1)}, bf16[2,2,4,2048]{3,2,1,0:T(4,128)(2,1)S(1)}, u32[]{:S(2)}, u32[]{:S(2)}) collective-permute-start(bf16[2,2,4,2048]{3,2,1,0:T(4,128)(2,1)S(1)} %get-tuple-element.71), channel_id=1, source_target_pairs={{0,160},{32,192},{64,224},{96,0},{128,32},{160,64},{192,96},{224,1... | collective-permute-start | bytes 196616 | tf_op jit(solution)/shard_map/ppermute | solution.py:281
  83.8 1.9 %collective-permute-start.8 = (bf16[2,2,4,2048]{3,2,1,0:T(4,128)(2,1)S(1)}, bf16[2,2,4,2048]{3,2,1,0:T(4,128)(2,1)S(1)}, u32[]{:S(2)}, u32[]{:S(2)}) collective-permute-start(bf16[2,2,4,2048]{3,2,1,0:T(4,128)(2,1)S(1)} %get-tuple-element.72), channel_id=1, source_target_pairs={{0,192},{32,224},{64,0},{96,32},{128,64},{160,96},{192,128},{224,1... | collective-permute-start | bytes 196616 | tf_op jit(solution)/shard_map/ppermute | solution.py:281
  85.7 2.2 %collective-permute-start.9 = (bf16[2,2,4,2048]{3,2,1,0:T(4,128)(2,1)S(1)}, bf16[2,2,4,2048]{3,2,1,0:T(4,128)(2,1)S(1)}, u32[]{:S(2)}, u32[]{:S(2)}) collective-permute-start(bf16[2,2,4,2048]{3,2,1,0:T(4,128)(2,1)S(1)} %pad_maximum_fusion.2), channel_id=1, source_target_pairs={{0,224},{32,0},{64,32},{96,64},{128,96},{160,128},{192,160},{224,1... | collective-permute-start | bytes 196616 | tf_op jit(solution)/shard_map/ppermute | solution.py:281
  87.9 0.0 collective-permute-done.7.refs_6_
  87.9 2.5 %collective-permute-done.8.refs_7_ = bf16[2,2,4,2048]{3,2,1,0:T(4,128)(2,1)S(1)} collective-permute-done((bf16[2,2,4,2048]{3,2,1,0:T(4,128)(2,1)S(1)}, bf16[2,2,4,2048]{3,2,1,0:T(4,128)(2,1)S(1)}, u32[]{:S(2)}, u32[]{:S(2)}) %collective-permute-start.8) | collective-permute-done | bytes 65568 | tf_op jit(solution)/shard_map/ppermute | solution.py:281
  90.4 2.4 %collective-permute-done.9.refs_8_ = bf16[2,2,4,2048]{3,2,1,0:T(4,128)(2,1)S(1)} collective-permute-done((bf16[2,2,4,2048]{3,2,1,0:T(4,128)(2,1)S(1)}, bf16[2,2,4,2048]{3,2,1,0:T(4,128)(2,1)S(1)}, u32[]{:S(2)}, u32[]{:S(2)}) %collective-permute-start.9) | collective-permute-done | bytes 65568 | tf_op jit(solution)/shard_map/ppermute | solution.py:281
  92.8 1.3 %control_unpack.1 = (bf16[16,4,2048]{2,1,0:T(4,128)(2,1)}, bf16[64,2048]{1,0:T(8,128)(2,1)S(1)}) custom-call(s32[4]{0:T(128)S(1)} %pad_add_fusion.info, bf16[2,2,4,2048]{3,2,1,0:T(4,128)(2,1)S(1)} %get-tuple-element.60.refs_0_, bf16[2,2,4,2048]{3,2,1,0:T(4,128)(2,1)S(1)} %collective-permute-done.1.refs_1_, ...), custom_call_target="tpu_custom_call" | custom-call | tf_op jit(solution)/shard_map/control_unpack/pallas_call | solution.py:344
  94.1 12.2 %all-to-all-done.1.back = bf16[16,4,80,128]{3,2,1,0:T(8,128)(2,1)S(1)} async-done(((bf16[16,4,80,128]{3,2,1,0:T(8,128)(2,1)}), bf16[16,4,80,128]{3,2,1,0:T(8,128)(2,1)S(1)}, u32[]{:S(2)}, u32[]{:S(2)}) %all-to-all-start.1) | async-done | bytes 1310752 | tf_op jit(solution)/shard_map/all_to_all | solution.py:343
  106.3 1.2 %unpack.1 = (bf16[16,2048]{1,0:T(8,128)(2,1)}, bf16[64,2048]{1,0:T(8,128)(2,1)}, bf16[3,16,2048]{2,1,0:T(8,128)(2,1)}, bf16[3,64,2048]{2,1,0:T(8,128)(2,1)}) custom-call(bf16[16,4,80,128]{3,2,1,0:T(8,128)(2,1)S(1)} %all-to-all-done.1.back, bf16[64,2048]{1,0:T(8,128)(2,1)S(1)} %get-tuple-element.74.residual, f32[1,2048]{1,0:T(1,128)S(1)} %bitcast.29), custom_call_target="tpu_custom_call" | custom-call | tf_op jit(solution)/shard_map/unpack/pallas_call | solution.py:353
  (10 shorter events, 0.3 us)
Async XLA Ops:
  2.8 8.9 %copy-start = (bf16[1,64,2048]{2,1,0:T(8,128)(2,1)S(1)}, bf16[1,64,2048]{2,1,0:T(8,128)(2,1)}, u32[]{:S(2)}) copy-start(bf16[1,64,2048]{2,1,0:T(8,128)(2,1)} %param.12) | copy-start | bytes 786436
  2.9 8.9 %copy-start.1 = (bf16[16,1,4,2048]{3,2,1,0:T(4,128)(2,1)S(1)}, bf16[16,1,4,2048]{3,2,1,0:T(4,128)(2,1)}, u32[]{:S(2)}) copy-start(bf16[16,1,4,2048]{3,2,1,0:T(4,128)(2,1)} %param.13) | copy-start | bytes 786436
  2.9 8.9 %copy-start.2 = (f32[2048]{0:T(1024)S(1)}, f32[2048]{0:T(1024)}, u32[]{:S(2)}) copy-start(f32[2048]{0:T(1024)} %param.14) | copy-start | bytes 24580
  2.9 40.7 %all-to-all-start = ((bf16[16,4,80,128]{3,2,1,0:T(8,128)(2,1)}), bf16[16,4,80,128]{3,2,1,0:T(8,128)(2,1)S(1)}, u32[]{:S(2)}, u32[]{:S(2)}) async-start(bf16[16,4,80,128]{3,2,1,0:T(8,128)(2,1)} %pack.1), calls=%async_computation | async-start | bytes 2621440 | tf_op jit(solution)/shard_map/all_to_all | solution.py:269
  12.4 19.7 %collective-permute-start.1 = (bf16[2,2,4,2048]{3,2,1,0:T(4,128)(2,1)S(1)}, bf16[2,2,4,2048]{3,2,1,0:T(4,128)(2,1)S(1)}, u32[]{:S(2)}, u32[]{:S(2)}) collective-permute-start(bf16[2,2,4,2048]{3,2,1,0:T(4,128)(2,1)S(1)} %get-tuple-element.55), channel_id=1, source_target_pairs={{0,32},{32,64},{64,96},{96,128},{128,160},{160,192},{192,224},{224... | collective-permute-start | bytes 196616 | tf_op jit(solution)/shard_map/ppermute | solution.py:281
  16.4 15.7 %collective-permute-start.2 = (bf16[2,2,4,2048]{3,2,1,0:T(4,128)(2,1)S(1)}, bf16[2,2,4,2048]{3,2,1,0:T(4,128)(2,1)S(1)}, u32[]{:S(2)}, u32[]{:S(2)}) collective-permute-start(bf16[2,2,4,2048]{3,2,1,0:T(4,128)(2,1)S(1)} %get-tuple-element.56), channel_id=1, source_target_pairs={{0,64},{32,96},{64,128},{96,160},{128,192},{160,224},{192,0},{224,... | collective-permute-start | bytes 196616 | tf_op jit(solution)/shard_map/ppermute | solution.py:281
  22.2 9.9 %collective-permute-start.3 = (bf16[2,2,4,2048]{3,2,1,0:T(4,128)(2,1)S(1)}, bf16[2,2,4,2048]{3,2,1,0:T(4,128)(2,1)S(1)}, u32[]{:S(2)}, u32[]{:S(2)}) collective-permute-start(bf16[2,2,4,2048]{3,2,1,0:T(4,128)(2,1)S(1)} %get-tuple-element.57), channel_id=1, source_target_pairs={{0,96},{32,128},{64,160},{96,192},{128,224},{160,0},{192,32},{224,... | collective-permute-start | bytes 196616 | tf_op jit(solution)/shard_map/ppermute | solution.py:281
  29.3 9.0 %collective-permute-start.4 = (bf16[2,2,4,2048]{3,2,1,0:T(4,128)(2,1)S(1)}, bf16[2,2,4,2048]{3,2,1,0:T(4,128)(2,1)S(1)}, u32[]{:S(2)}, u32[]{:S(2)}) collective-permute-start(bf16[2,2,4,2048]{3,2,1,0:T(4,128)(2,1)S(1)} %get-tuple-element.58), channel_id=1, source_target_pairs={{0,128},{32,160},{64,192},{96,224},{128,0},{160,32},{192,64},{224,... | collective-permute-start | bytes 196616 | tf_op jit(solution)/shard_map/ppermute | solution.py:281
  43.6 8.7 %collective-permute-start.5 = (bf16[16,4,80,128]{3,2,1,0:T(8,128)(2,1)S(1)}, bf16[16,4,80,128]{3,2,1,0:T(8,128)(2,1)}, u32[]{:S(2)}, u32[]{:S(2)}) collective-permute-start(bf16[16,4,80,128]{3,2,1,0:T(8,128)(2,1)S(1)} %all-to-all-done), channel_id=1, source_target_pairs={{0,1},{1,0},{2,3},{3,2},{4,5},{5,4},{6,7},{7,6},{8,9},{9,8},{10,11... | collective-permute-start | bytes 3932168 | tf_op jit(solution)/shard_map/ppermute | solution.py:286
  47.5 21.7 %collective-permute-start.6 = (bf16[8,2,4,2048]{3,2,1,0:T(4,128)(2,1)S(1)}, bf16[8,2,4,2048]{3,2,1,0:T(4,128)(2,1)S(1)}, u32[]{:S(2)}, u32[]{:S(2)}) collective-permute-start(bf16[8,2,4,2048]{3,2,1,0:T(4,128)(2,1)S(1)} %get-tuple-element.89), channel_id=1, source_target_pairs={{0,256},{256,0},{1,257},{257,1},{2,258},{258,2},{3,259},{259,3},{4... | collective-permute-start | bytes 786440 | tf_op jit(solution)/shard_map/ppermute | solution.py:287
  64.1 4.0 %collective-permute-start = (bf16[2,128,1280]{2,1,0:T(8,128)(2,1)S(1)}, bf16[2,128,1280]{2,1,0:T(8,128)(2,1)S(1)}, u32[]{:S(2)}, u32[]{:S(2)}) collective-permute-start(bf16[2,128,1280]{2,1,0:T(8,128)(2,1)S(1)} %get-tuple-element.18), channel_id=1, source_target_pairs={{0,1},{1,0},{2,3},{3,2},{4,5},{5,4},{6,7},{7,6},{8,9},{9,8},{10,11... | collective-permute-start | bytes 1966088 | tf_op jit(solution)/shard_map/cond/branch_1_fun/ppermute | solution.py:311
  69.4 36.9 %all-to-all-start.1 = ((bf16[16,4,80,128]{3,2,1,0:T(8,128)(2,1)}), bf16[16,4,80,128]{3,2,1,0:T(8,128)(2,1)S(1)}, u32[]{:S(2)}, u32[]{:S(2)}) async-start(bf16[16,4,80,128]{3,2,1,0:T(8,128)(2,1)} %get-tuple-element.96), calls=%async_computation.1 | async-start | bytes 2621440 | tf_op jit(solution)/shard_map/all_to_all | solution.py:343
  73.1 14.8 %collective-permute-start.7 = (bf16[2,2,4,2048]{3,2,1,0:T(4,128)(2,1)S(1)}, bf16[2,2,4,2048]{3,2,1,0:T(4,128)(2,1)S(1)}, u32[]{:S(2)}, u32[]{:S(2)}) collective-permute-start(bf16[2,2,4,2048]{3,2,1,0:T(4,128)(2,1)S(1)} %get-tuple-element.71), channel_id=1, source_target_pairs={{0,160},{32,192},{64,224},{96,0},{128,32},{160,64},{192,96},{224,1... | collective-permute-start | bytes 196616 | tf_op jit(solution)/shard_map/ppermute | solution.py:281
  83.8 6.6 %collective-permute-start.8 = (bf16[2,2,4,2048]{3,2,1,0:T(4,128)(2,1)S(1)}, bf16[2,2,4,2048]{3,2,1,0:T(4,128)(2,1)S(1)}, u32[]{:S(2)}, u32[]{:S(2)}) collective-permute-start(bf16[2,2,4,2048]{3,2,1,0:T(4,128)(2,1)S(1)} %get-tuple-element.72), channel_id=1, source_target_pairs={{0,192},{32,224},{64,0},{96,32},{128,64},{160,96},{192,128},{224,1... | collective-permute-start | bytes 196616 | tf_op jit(solution)/shard_map/ppermute | solution.py:281
  85.7 7.1 %collective-permute-start.9 = (bf16[2,2,4,2048]{3,2,1,0:T(4,128)(2,1)S(1)}, bf16[2,2,4,2048]{3,2,1,0:T(4,128)(2,1)S(1)}, u32[]{:S(2)}, u32[]{:S(2)}) collective-permute-start(bf16[2,2,4,2048]{3,2,1,0:T(4,128)(2,1)S(1)} %pad_maximum_fusion.2), channel_id=1, source_target_pairs={{0,224},{32,0},{64,32},{96,64},{128,96},{160,128},{192,160},{224,1... | collective-permute-start | bytes 196616 | tf_op jit(solution)/shard_map/ppermute | solution.py:281

commit v6 on v5

--- a/solution.py
+++ b/solution.py
@@ -204,13 +204,6 @@
         copies.append(pltpu.make_async_copy(a, b, sems.at[len(copies)]))
         copies[-1].start()
 
-    for t in range(3):
-        for h in range(HEADS):
-            cols = slice(h * HEAD, (h + 1) * HEAD)
-            tg_s[t, :, cols] = back[h, 1 + t, :TXT, :]
-            ig_s[t, :, cols] = back[h, 1 + t, TXT:, :]
-        send(ig_s.at[t], ig.at[t])
-        send(tg_s.at[t], tg.at[t])
     for h in range(HEADS):
         cols = slice(h * HEAD, (h + 1) * HEAD)
         ta_s[:, cols] = back[h, 0, :TXT, :]
@@ -220,6 +213,13 @@
         ).astype(jnp.bfloat16)
     send(io_s, io)
     send(ta_s, ta)
+    for t in range(3):
+        for h in range(HEADS):
+            cols = slice(h * HEAD, (h + 1) * HEAD)
+            tg_s[t, :, cols] = back[h, 1 + t, :TXT, :]
+            ig_s[t, :, cols] = back[h, 1 + t, TXT:, :]
+        send(ig_s.at[t], ig.at[t])
+        send(tg_s.at[t], tg.at[t])
     for copy in copies:
         copy.wait()
 

time: 108 us -> 108 us (level)
  no operation moved by 1% of the time
where the time goes in v6:
time: 108 us
  starting transfers between devices  56.9 us (53%)
  waiting for transfers between devices  29.3 us (27%)
  Pallas kernels  19.3 us (18%)
  between operations  1.53 us (1%)
    ppermute x7, starting transfers between devices, shift(): return lax.ppermute(x, 'z', [(i, (i + k) % ZS) for i in range(ZS)])  34.4 us
    all_to_all x1, waiting for transfers between devices, body(): back = lax.all_to_all(ready, chips, split_axis=0, concat_axis=0, tiled=True)  12.2 us
    pallas_call x1, Pallas kernels, attend(): call(attention_kernel, [SM, VM, VM], [((2, CHIPS, ROWS, HEAD), bf16), tur...  11.8 us
    ppermute x7, waiting for transfers between devices, shift(): return lax.ppermute(x, 'z', [(i, (i + k) % ZS) for i in range(ZS)])  11.1 us
    all_to_all x1, starting transfers between devices, body(): own = lax.all_to_all(send, chips, split_axis=0, concat_axis=0, tiled=True)  8.14 us
    all_to_all x1, waiting for transfers between devices, body(): own = lax.all_to_all(send, chips, split_axis=0, concat_axis=0, tiled=True)  5.27 us
    ppermute x1, starting transfers between devices, body(): lax.ppermute(jnp.stack([p[1] for p in near + pieces[EARLY:]]), 'yh', swap)  4.8 us
    all_to_all x1, starting transfers between devices, body(): back = lax.all_to_all(ready, chips, split_axis=0, concat_axis=0, tiled=True)  3.71 us
  transfers between devices with their start and end apart: 12, of which 6 were waited for; matrix products, arithmetic and copies ran while one was open for 0% of the time, Pallas kernels for 15%

profile of v6, /device:TPU:1, one launch (start us, length us, event | category | flops | bytes accessed | tf_op | source)
XLA Modules:
  0.0 107.5 jit_solution(14658673037067045293)
XLA Ops:
  0.6 2.2 %pack.1 = bf16[16,4,80,128]{3,2,1,0:T(8,128)(2,1)} custom-call(bf16[3,16,2048]{2,1,0:T(8,128)(2,1)} %bitcast.31, bf16[3,64,2048]{2,1,0:T(8,128)(2,1)} %bitcast.30, bf16[16,2048]{1,0:T(8,128)(2,1)} %bitcast.32, bf16[64,2048]{1,0:T(8,128)(2,1)} %bitcast.25), custom_call_target="tpu_custom_call" | custom-call | tf_op jit(solution)/shard_map/pack/pallas_call | solution.py:251
  2.8 0.0 copy-start
  2.9 0.0 copy-start.1
  2.9 0.0 copy-start.2
  2.9 8.1 %all-to-all-start = ((bf16[16,4,80,128]{3,2,1,0:T(8,128)(2,1)}), bf16[16,4,80,128]{3,2,1,0:T(8,128)(2,1)S(1)}, u32[]{:S(2)}, u32[]{:S(2)}) async-start(bf16[16,4,80,128]{3,2,1,0:T(8,128)(2,1)} %pack.1), calls=%async_computation | async-start | bytes 2621440 | tf_op jit(solution)/shard_map/all_to_all | solution.py:269
  11.7 0.1 pad_add_fusion.info
  11.8 0.0 copy-done
  11.8 0.0 copy-done.1
  11.8 0.0 copy-done.2
  11.8 0.6 control_pack.1
  12.4 4.0 %collective-permute-start.1 = (bf16[2,2,4,2048]{3,2,1,0:T(4,128)(2,1)S(1)}, bf16[2,2,4,2048]{3,2,1,0:T(4,128)(2,1)S(1)}, u32[]{:S(2)}, u32[]{:S(2)}) collective-permute-start(bf16[2,2,4,2048]{3,2,1,0:T(4,128)(2,1)S(1)} %get-tuple-element.55), channel_id=1, source_target_pairs={{0,32},{32,64},{64,96},{96,128},{128,160},{160,192},{192,224},{224... | collective-permute-start | bytes 196616 | tf_op jit(solution)/shard_map/ppermute | solution.py:281
  16.4 5.8 %collective-permute-start.2 = (bf16[2,2,4,2048]{3,2,1,0:T(4,128)(2,1)S(1)}, bf16[2,2,4,2048]{3,2,1,0:T(4,128)(2,1)S(1)}, u32[]{:S(2)}, u32[]{:S(2)}) collective-permute-start(bf16[2,2,4,2048]{3,2,1,0:T(4,128)(2,1)S(1)} %get-tuple-element.56), channel_id=1, source_target_pairs={{0,64},{32,96},{64,128},{96,160},{128,192},{160,224},{192,0},{224,... | collective-permute-start | bytes 196616 | tf_op jit(solution)/shard_map/ppermute | solution.py:281
  22.2 7.0 %collective-permute-start.3 = (bf16[2,2,4,2048]{3,2,1,0:T(4,128)(2,1)S(1)}, bf16[2,2,4,2048]{3,2,1,0:T(4,128)(2,1)S(1)}, u32[]{:S(2)}, u32[]{:S(2)}) collective-permute-start(bf16[2,2,4,2048]{3,2,1,0:T(4,128)(2,1)S(1)} %get-tuple-element.57), channel_id=1, source_target_pairs={{0,96},{32,128},{64,160},{96,192},{128,224},{160,0},{192,32},{224,... | collective-permute-start | bytes 196616 | tf_op jit(solution)/shard_map/ppermute | solution.py:281
  29.3 2.8 %collective-permute-start.4 = (bf16[2,2,4,2048]{3,2,1,0:T(4,128)(2,1)S(1)}, bf16[2,2,4,2048]{3,2,1,0:T(4,128)(2,1)S(1)}, u32[]{:S(2)}, u32[]{:S(2)}) collective-permute-start(bf16[2,2,4,2048]{3,2,1,0:T(4,128)(2,1)S(1)} %get-tuple-element.58), channel_id=1, source_target_pairs={{0,128},{32,160},{64,192},{96,224},{128,0},{160,32},{192,64},{224,... | collective-permute-start | bytes 196616 | tf_op jit(solution)/shard_map/ppermute | solution.py:281
  32.1 0.0 collective-permute-done.1.refs_1_
  32.1 0.0 collective-permute-done.2.refs_2_
  32.1 0.0 collective-permute-done.3.refs_3_
  32.1 6.2 %collective-permute-done.4.refs_4_ = bf16[2,2,4,2048]{3,2,1,0:T(4,128)(2,1)S(1)} collective-permute-done((bf16[2,2,4,2048]{3,2,1,0:T(4,128)(2,1)S(1)}, bf16[2,2,4,2048]{3,2,1,0:T(4,128)(2,1)S(1)}, u32[]{:S(2)}, u32[]{:S(2)}) %collective-permute-start.4) | collective-permute-done | bytes 65568 | tf_op jit(solution)/shard_map/ppermute | solution.py:281
  38.3 5.3 %all-to-all-done = bf16[16,4,80,128]{3,2,1,0:T(8,128)(2,1)S(1)} async-done(((bf16[16,4,80,128]{3,2,1,0:T(8,128)(2,1)}), bf16[16,4,80,128]{3,2,1,0:T(8,128)(2,1)S(1)}, u32[]{:S(2)}, u32[]{:S(2)}) %all-to-all-start) | async-done | bytes 1310752 | tf_op jit(solution)/shard_map/all_to_all | solution.py:269
  43.6 3.7 %collective-permute-start.5 = (bf16[16,4,80,128]{3,2,1,0:T(8,128)(2,1)S(1)}, bf16[16,4,80,128]{3,2,1,0:T(8,128)(2,1)}, u32[]{:S(2)}, u32[]{:S(2)}) collective-permute-start(bf16[16,4,80,128]{3,2,1,0:T(8,128)(2,1)S(1)} %all-to-all-done), channel_id=1, source_target_pairs={{0,1},{1,0},{2,3},{3,2},{4,5},{5,4},{6,7},{7,6},{8,9},{9,8},{10,11... | collective-permute-start | bytes 3932168 | tf_op jit(solution)/shard_map/ppermute | solution.py:286
  47.5 4.8 %collective-permute-start.6 = (bf16[8,2,4,2048]{3,2,1,0:T(4,128)(2,1)S(1)}, bf16[8,2,4,2048]{3,2,1,0:T(4,128)(2,1)S(1)}, u32[]{:S(2)}, u32[]{:S(2)}) collective-permute-start(bf16[8,2,4,2048]{3,2,1,0:T(4,128)(2,1)S(1)} %get-tuple-element.89), channel_id=1, source_target_pairs={{0,256},{256,0},{1,257},{257,1},{2,258},{258,2},{3,259},{259,3},{4... | collective-permute-start | bytes 786440 | tf_op jit(solution)/shard_map/ppermute | solution.py:287
  52.3 0.0 collective-permute-done.5
  52.3 16.9 %conditional.1 = (bf16[16,4,80,128]{3,2,1,0:T(8,128)(2,1)}) conditional(s32[]{:T(128)} %bitcast, () %tuple.18, (s32[4]{0:T(128)S(1)}, bf16[16,4,80,128]{3,2,1,0:T(8,128)(2,1)S(1)}, bf16[16,4,80,128]{3,2,1,0:T(8,128)(2,1)}) %tuple.21), branch_computations={%region_0.0_spmd, %region_1.0_spmd} | conditional | flops 5033164800 | bytes 11010096 | solution.py:331
  52.3 11.8 %attention.1 = (bf16[2,16,80,128]{3,2,1,0:T(8,128)(2,1)S(1)}, bf16[2,128,1280]{2,1,0:T(8,128)(2,1)S(1)}, bf16[1280,1280]{1,0:T(8,128)(2,1)S(1)}, bf16[1280,1280]{1,0:T(8,128)(2,1)S(1)}, bf16[2,128,1280]{2,1,0:T(8,128)(2,1)S(1)}) custom-call(s32[4]{0:T(128)S(1)} %get-tuple-element.2.info, bf16[16,4,80,128]{3,2,1,0:T(8,128)(2,1)S(1)} %get-tuple-element.10.own, ...), custom_call_target="tpu_custom_call" | custom-call | flops 5033164800 | bytes 8388608 | tf_op jit(solution)/shard_map/cond/branch_1_fun/attention/pallas_call | solution.py:291
  64.1 2.2 %collective-permute-start = (bf16[2,128,1280]{2,1,0:T(8,128)(2,1)S(1)}, bf16[2,128,1280]{2,1,0:T(8,128)(2,1)S(1)}, u32[]{:S(2)}, u32[]{:S(2)}) collective-permute-start(bf16[2,128,1280]{2,1,0:T(8,128)(2,1)S(1)} %get-tuple-element.18), channel_id=1, source_target_pairs={{0,1},{1,0},{2,3},{3,2},{4,5},{5,4},{6,7},{7,6},{8,9},{9,8},{10,11... | collective-permute-start | bytes 1966088 | tf_op jit(solution)/shard_map/cond/branch_1_fun/ppermute | solution.py:311
  66.4 1.1 key_grad.1
  67.4 0.7 collective-permute-done.theirs
  68.1 1.0 combine.1
  69.2 0.0 collective-permute-done.6.refs_5_
  69.3 0.1 pad_maximum_fusion
  69.4 3.7 %all-to-all-start.1 = ((bf16[16,4,80,128]{3,2,1,0:T(8,128)(2,1)}), bf16[16,4,80,128]{3,2,1,0:T(8,128)(2,1)S(1)}, u32[]{:S(2)}, u32[]{:S(2)}) async-start(bf16[16,4,80,128]{3,2,1,0:T(8,128)(2,1)} %get-tuple-element.96), calls=%async_computation.1 | async-start | bytes 2621440 | tf_op jit(solution)/shard_map/all_to_all | solution.py:343
  73.1 10.6 %collective-permute-start.7 = (bf16[2,2,4,2048]{3,2,1,0:T(4,128)(2,1)S(1)}, bf16[2,2,4,2048]{3,2,1,0:T(4,128)(2,1)S(1)}, u32[]{:S(2)}, u32[]{:S(2)}) collective-permute-start(bf16[2,2,4,2048]{3,2,1,0:T(4,128)(2,1)S(1)} %get-tuple-element.71), channel_id=1, source_target_pairs={{0,160},{32,192},{64,224},{96,0},{128,32},{160,64},{192,96},{224,1... | collective-permute-start | bytes 196616 | tf_op jit(solution)/shard_map/ppermute | solution.py:281
  83.8 1.9 %collective-permute-start.8 = (bf16[2,2,4,2048]{3,2,1,0:T(4,128)(2,1)S(1)}, bf16[2,2,4,2048]{3,2,1,0:T(4,128)(2,1)S(1)}, u32[]{:S(2)}, u32[]{:S(2)}) collective-permute-start(bf16[2,2,4,2048]{3,2,1,0:T(4,128)(2,1)S(1)} %get-tuple-element.72), channel_id=1, source_target_pairs={{0,192},{32,224},{64,0},{96,32},{128,64},{160,96},{192,128},{224,1... | collective-permute-start | bytes 196616 | tf_op jit(solution)/shard_map/ppermute | solution.py:281
  85.7 2.2 %collective-permute-start.9 = (bf16[2,2,4,2048]{3,2,1,0:T(4,128)(2,1)S(1)}, bf16[2,2,4,2048]{3,2,1,0:T(4,128)(2,1)S(1)}, u32[]{:S(2)}, u32[]{:S(2)}) collective-permute-start(bf16[2,2,4,2048]{3,2,1,0:T(4,128)(2,1)S(1)} %pad_maximum_fusion.2), channel_id=1, source_target_pairs={{0,224},{32,0},{64,32},{96,64},{128,96},{160,128},{192,160},{224,1... | collective-permute-start | bytes 196616 | tf_op jit(solution)/shard_map/ppermute | solution.py:281
  87.9 0.0 collective-permute-done.7.refs_6_
  87.9 2.5 %collective-permute-done.8.refs_7_ = bf16[2,2,4,2048]{3,2,1,0:T(4,128)(2,1)S(1)} collective-permute-done((bf16[2,2,4,2048]{3,2,1,0:T(4,128)(2,1)S(1)}, bf16[2,2,4,2048]{3,2,1,0:T(4,128)(2,1)S(1)}, u32[]{:S(2)}, u32[]{:S(2)}) %collective-permute-start.8) | collective-permute-done | bytes 65568 | tf_op jit(solution)/shard_map/ppermute | solution.py:281
  90.4 2.4 %collective-permute-done.9.refs_8_ = bf16[2,2,4,2048]{3,2,1,0:T(4,128)(2,1)S(1)} collective-permute-done((bf16[2,2,4,2048]{3,2,1,0:T(4,128)(2,1)S(1)}, bf16[2,2,4,2048]{3,2,1,0:T(4,128)(2,1)S(1)}, u32[]{:S(2)}, u32[]{:S(2)}) %collective-permute-start.9) | collective-permute-done | bytes 65568 | tf_op jit(solution)/shard_map/ppermute | solution.py:281
  92.8 1.3 %control_unpack.1 = (bf16[16,4,2048]{2,1,0:T(4,128)(2,1)}, bf16[64,2048]{1,0:T(8,128)(2,1)S(1)}) custom-call(s32[4]{0:T(128)S(1)} %pad_add_fusion.info, bf16[2,2,4,2048]{3,2,1,0:T(4,128)(2,1)S(1)} %get-tuple-element.60.refs_0_, bf16[2,2,4,2048]{3,2,1,0:T(4,128)(2,1)S(1)} %collective-permute-done.1.refs_1_, ...), custom_call_target="tpu_custom_call" | custom-call | tf_op jit(solution)/shard_map/control_unpack/pallas_call | solution.py:344
  94.1 12.2 %all-to-all-done.1.back = bf16[16,4,80,128]{3,2,1,0:T(8,128)(2,1)S(1)} async-done(((bf16[16,4,80,128]{3,2,1,0:T(8,128)(2,1)}), bf16[16,4,80,128]{3,2,1,0:T(8,128)(2,1)S(1)}, u32[]{:S(2)}, u32[]{:S(2)}) %all-to-all-start.1) | async-done | bytes 1310752 | tf_op jit(solution)/shard_map/all_to_all | solution.py:343
  106.3 1.3 %unpack.1 = (bf16[16,2048]{1,0:T(8,128)(2,1)}, bf16[64,2048]{1,0:T(8,128)(2,1)}, bf16[3,16,2048]{2,1,0:T(8,128)(2,1)}, bf16[3,64,2048]{2,1,0:T(8,128)(2,1)}) custom-call(bf16[16,4,80,128]{3,2,1,0:T(8,128)(2,1)S(1)} %all-to-all-done.1.back, bf16[64,2048]{1,0:T(8,128)(2,1)S(1)} %get-tuple-element.74.residual, f32[1,2048]{1,0:T(1,128)S(1)} %bitcast.29), custom_call_target="tpu_custom_call" | custom-call | tf_op jit(solution)/shard_map/unpack/pallas_call | solution.py:353
  (10 shorter events, 0.3 us)
Async XLA Ops:
  2.8 8.9 %copy-start = (bf16[1,64,2048]{2,1,0:T(8,128)(2,1)S(1)}, bf16[1,64,2048]{2,1,0:T(8,128)(2,1)}, u32[]{:S(2)}) copy-start(bf16[1,64,2048]{2,1,0:T(8,128)(2,1)} %param.12) | copy-start | bytes 786436
  2.9 8.9 %copy-start.1 = (bf16[16,1,4,2048]{3,2,1,0:T(4,128)(2,1)S(1)}, bf16[16,1,4,2048]{3,2,1,0:T(4,128)(2,1)}, u32[]{:S(2)}) copy-start(bf16[16,1,4,2048]{3,2,1,0:T(4,128)(2,1)} %param.13) | copy-start | bytes 786436
  2.9 8.9 %copy-start.2 = (f32[2048]{0:T(1024)S(1)}, f32[2048]{0:T(1024)}, u32[]{:S(2)}) copy-start(f32[2048]{0:T(1024)} %param.14) | copy-start | bytes 24580
  2.9 40.7 %all-to-all-start = ((bf16[16,4,80,128]{3,2,1,0:T(8,128)(2,1)}), bf16[16,4,80,128]{3,2,1,0:T(8,128)(2,1)S(1)}, u32[]{:S(2)}, u32[]{:S(2)}) async-start(bf16[16,4,80,128]{3,2,1,0:T(8,128)(2,1)} %pack.1), calls=%async_computation | async-start | bytes 2621440 | tf_op jit(solution)/shard_map/all_to_all | solution.py:269
  12.4 19.7 %collective-permute-start.1 = (bf16[2,2,4,2048]{3,2,1,0:T(4,128)(2,1)S(1)}, bf16[2,2,4,2048]{3,2,1,0:T(4,128)(2,1)S(1)}, u32[]{:S(2)}, u32[]{:S(2)}) collective-permute-start(bf16[2,2,4,2048]{3,2,1,0:T(4,128)(2,1)S(1)} %get-tuple-element.55), channel_id=1, source_target_pairs={{0,32},{32,64},{64,96},{96,128},{128,160},{160,192},{192,224},{224... | collective-permute-start | bytes 196616 | tf_op jit(solution)/shard_map/ppermute | solution.py:281
  16.4 15.7 %collective-permute-start.2 = (bf16[2,2,4,2048]{3,2,1,0:T(4,128)(2,1)S(1)}, bf16[2,2,4,2048]{3,2,1,0:T(4,128)(2,1)S(1)}, u32[]{:S(2)}, u32[]{:S(2)}) collective-permute-start(bf16[2,2,4,2048]{3,2,1,0:T(4,128)(2,1)S(1)} %get-tuple-element.56), channel_id=1, source_target_pairs={{0,64},{32,96},{64,128},{96,160},{128,192},{160,224},{192,0},{224,... | collective-permute-start | bytes 196616 | tf_op jit(solution)/shard_map/ppermute | solution.py:281
  22.2 9.9 %collective-permute-start.3 = (bf16[2,2,4,2048]{3,2,1,0:T(4,128)(2,1)S(1)}, bf16[2,2,4,2048]{3,2,1,0:T(4,128)(2,1)S(1)}, u32[]{:S(2)}, u32[]{:S(2)}) collective-permute-start(bf16[2,2,4,2048]{3,2,1,0:T(4,128)(2,1)S(1)} %get-tuple-element.57), channel_id=1, source_target_pairs={{0,96},{32,128},{64,160},{96,192},{128,224},{160,0},{192,32},{224,... | collective-permute-start | bytes 196616 | tf_op jit(solution)/shard_map/ppermute | solution.py:281
  29.3 9.0 %collective-permute-start.4 = (bf16[2,2,4,2048]{3,2,1,0:T(4,128)(2,1)S(1)}, bf16[2,2,4,2048]{3,2,1,0:T(4,128)(2,1)S(1)}, u32[]{:S(2)}, u32[]{:S(2)}) collective-permute-start(bf16[2,2,4,2048]{3,2,1,0:T(4,128)(2,1)S(1)} %get-tuple-element.58), channel_id=1, source_target_pairs={{0,128},{32,160},{64,192},{96,224},{128,0},{160,32},{192,64},{224,... | collective-permute-start | bytes 196616 | tf_op jit(solution)/shard_map/ppermute | solution.py:281
  43.6 8.7 %collective-permute-start.5 = (bf16[16,4,80,128]{3,2,1,0:T(8,128)(2,1)S(1)}, bf16[16,4,80,128]{3,2,1,0:T(8,128)(2,1)}, u32[]{:S(2)}, u32[]{:S(2)}) collective-permute-start(bf16[16,4,80,128]{3,2,1,0:T(8,128)(2,1)S(1)} %all-to-all-done), channel_id=1, source_target_pairs={{0,1},{1,0},{2,3},{3,2},{4,5},{5,4},{6,7},{7,6},{8,9},{9,8},{10,11... | collective-permute-start | bytes 3932168 | tf_op jit(solution)/shard_map/ppermute | solution.py:286
  47.5 21.7 %collective-permute-start.6 = (bf16[8,2,4,2048]{3,2,1,0:T(4,128)(2,1)S(1)}, bf16[8,2,4,2048]{3,2,1,0:T(4,128)(2,1)S(1)}, u32[]{:S(2)}, u32[]{:S(2)}) collective-permute-start(bf16[8,2,4,2048]{3,2,1,0:T(4,128)(2,1)S(1)} %get-tuple-element.89), channel_id=1, source_target_pairs={{0,256},{256,0},{1,257},{257,1},{2,258},{258,2},{3,259},{259,3},{4... | collective-permute-start | bytes 786440 | tf_op jit(solution)/shard_map/ppermute | solution.py:287
  64.1 4.0 %collective-permute-start = (bf16[2,128,1280]{2,1,0:T(8,128)(2,1)S(1)}, bf16[2,128,1280]{2,1,0:T(8,128)(2,1)S(1)}, u32[]{:S(2)}, u32[]{:S(2)}) collective-permute-start(bf16[2,128,1280]{2,1,0:T(8,128)(2,1)S(1)} %get-tuple-element.18), channel_id=1, source_target_pairs={{0,1},{1,0},{2,3},{3,2},{4,5},{5,4},{6,7},{7,6},{8,9},{9,8},{10,11... | collective-permute-start | bytes 1966088 | tf_op jit(solution)/shard_map/cond/branch_1_fun/ppermute | solution.py:311
  69.4 36.9 %all-to-all-start.1 = ((bf16[16,4,80,128]{3,2,1,0:T(8,128)(2,1)}), bf16[16,4,80,128]{3,2,1,0:T(8,128)(2,1)S(1)}, u32[]{:S(2)}, u32[]{:S(2)}) async-start(bf16[16,4,80,128]{3,2,1,0:T(8,128)(2,1)} %get-tuple-element.96), calls=%async_computation.1 | async-start | bytes 2621440 | tf_op jit(solution)/shard_map/all_to_all | solution.py:343
  73.1 14.8 %collective-permute-start.7 = (bf16[2,2,4,2048]{3,2,1,0:T(4,128)(2,1)S(1)}, bf16[2,2,4,2048]{3,2,1,0:T(4,128)(2,1)S(1)}, u32[]{:S(2)}, u32[]{:S(2)}) collective-permute-start(bf16[2,2,4,2048]{3,2,1,0:T(4,128)(2,1)S(1)} %get-tuple-element.71), channel_id=1, source_target_pairs={{0,160},{32,192},{64,224},{96,0},{128,32},{160,64},{192,96},{224,1... | collective-permute-start | bytes 196616 | tf_op jit(solution)/shard_map/ppermute | solution.py:281
  83.8 6.6 %collective-permute-start.8 = (bf16[2,2,4,2048]{3,2,1,0:T(4,128)(2,1)S(1)}, bf16[2,2,4,2048]{3,2,1,0:T(4,128)(2,1)S(1)}, u32[]{:S(2)}, u32[]{:S(2)}) collective-permute-start(bf16[2,2,4,2048]{3,2,1,0:T(4,128)(2,1)S(1)} %get-tuple-element.72), channel_id=1, source_target_pairs={{0,192},{32,224},{64,0},{96,32},{128,64},{160,96},{192,128},{224,1... | collective-permute-start | bytes 196616 | tf_op jit(solution)/shard_map/ppermute | solution.py:281
  85.7 7.1 %collective-permute-start.9 = (bf16[2,2,4,2048]{3,2,1,0:T(4,128)(2,1)S(1)}, bf16[2,2,4,2048]{3,2,1,0:T(4,128)(2,1)S(1)}, u32[]{:S(2)}, u32[]{:S(2)}) collective-permute-start(bf16[2,2,4,2048]{3,2,1,0:T(4,128)(2,1)S(1)} %pad_maximum_fusion.2), channel_id=1, source_target_pairs={{0,224},{32,0},{64,32},{96,64},{128,96},{160,128},{192,160},{224,1... | collective-permute-start | bytes 196616 | tf_op jit(solution)/shard_map/ppermute | solution.py:281
